TPU v7x, 256 devices: a whole 4x4x8 slice. The times are simulated.
256 devices in a mesh: dp: 64 (over y, x, z_lo), feat: 4 (over z_hi, core).
Axes of the slice: x: 4, y: 4, z: 8 (z_hi: 2, z_lo: 4; z = z_hi * 4 + z_lo), core: 2. Of those that a mesh axis runs over, the one named last changes fastest.
Arguments:
- frames: bfloat16 [448, 262144], P('feat', 'dp'), may hold values from -4.5 to 4.5
- residual: float32 [148, 262144], P('feat', 'dp'), may hold values from -6 to 6
- coefficients: float32 [148, 262144], P('feat', 'dp'), may hold values from -6 to 6
- block_index: int32 [2, 512], replicated, may hold values from 0 to 262143, as said below
Outputs:
- residual_out: float32 [148, 262144], P('feat', 'dp')
- coefficients_out: float32 [148, 262144], P('feat', 'dp')
Inputs may be any that keep to these rules, and one draw needn't show every extreme that they name: `block_index`: the 512 indices of one step are distinct.
All inputs are finite; a program needn't handle non-finite values.
Results may differ from a plain program's by a relative error of at most 0.0003.
Values may be sent and summed in bfloat16 or wider, within the bound.
No kernel may reach another device: no remote copies, remote signals or barrier semaphores. Data moves between devices by JAX's collectives and lax.ppermute only.
A program may use at most 64 MiB of HBM per device.

v0:
```python
import math

import jax
import jax.numpy as jnp
from jax import lax
from jax.experimental import pallas as pl
from jax.experimental.pallas import tpu as pltpu
from jax.sharding import PartitionSpec as P

D = 448
STEPS = 2
BLOCK = 512
RIDGE = 0.1
WIDTH_SCALE = 2.0
AXES = ("dp", "feat")
BF16 = jnp.bfloat16
F32 = jnp.float32
ROWS = 37
PANEL = 16
TILE = 512
PICK = 1024
SCALE = WIDTH_SCALE / D * math.log2(math.e)


def permutation(move):
    pairs = []
    for d in range(64):
        for g in range(4):
            y, x, z, h, c = move(d // 16, (d // 4) % 4, d % 4, g // 2, g % 2)
            pairs.append((d * 4 + g, ((y % 4) * 16 + (x % 4) * 4 + z % 4) * 4 + (h % 2) * 2 + c % 2))
    return pairs


def swap(value, dh, dc):
    def move(y, x, z, h, c):
        return y, x, z, h + dh, c + dc

    return lax.ppermute(value, AXES, permutation(move))


PLANE = [[r * 4 + z for r in range(16)] for z in range(4)]
LINE = [[(r * 4 + z) * 4 + h * 2 + c for h in range(2) for z in range(4)] for r in range(16) for c in range(2)]


def split3(value):
    high = value.astype(BF16)
    rest = value - high.astype(F32)
    mid = rest.astype(BF16)
    low = (rest - mid.astype(F32)).astype(BF16)
    return high, mid, low


def dot(a, b):
    return jnp.dot(a, b, preferred_element_type=F32, precision=lax.Precision.HIGHEST)


def invert(mats):
    lane = lax.broadcasted_iota(jnp.int32, (1, PANEL, 128), 2)
    row = lax.broadcasted_iota(jnp.int32, (1, PANEL, 128), 1)
    lane1 = lax.broadcasted_iota(jnp.int32, (1, 128), 1)
    for k in range(4):
        r0 = 128 * k
        block = slice(r0, r0 + 128)
        for p in range(128 // PANEL):
            b = PANEL * p
            rows = slice(r0 + b, r0 + b + PANEL)
            tiles = [mats[:, rows, 128 * q : 128 * q + 128] for q in range(4)]
            old = tiles[k]
            cols = [jnp.broadcast_to(old[:, :, b + j : b + j + 1], (2, PANEL, 128)) for j in range(PANEL)]
            for j in range(PANEL):
                one = jnp.where(row == j, 1.0, 0.0)
                inv = 1.0 / cols[j][:, j : j + 1, :]
                factor = cols[j] - one
                for q in range(j + 1, PANEL):
                    cols[q] = cols[q] - factor * (cols[q][:, j : j + 1, :] * inv)
                tiles[k] = jnp.where(lane == b + j, one, tiles[k])
                for q in range(4):
                    tiles[q] = tiles[q] - factor * (tiles[q][:, j : j + 1, :] * inv)
            new = jnp.concatenate(tiles, axis=2)
            sign = jnp.where(lane1 < b, -1.0, jnp.where(lane1 < b + PANEL, 0.0, 1.0))
            clear = jnp.where((lane1 >= b) & (lane1 < b + PANEL), 0.0, 1.0)
            for s in range(2):
                h, m, l = split3(old[s] * sign)
                nh, nm, nl = split3(new[s])
                lhs = jnp.concatenate([h, h, m, h, l, m], axis=0)
                rhs = jnp.concatenate([nh, nm, nh, nl, nh, nm], axis=0)
                out = lax.dot_general(lhs, rhs, (((0,), (0,)), ((), ())), preferred_element_type=F32)
                for q in range(4):
                    at = slice(128 * q, 128 * q + 128)
                    held = mats[s, block, at]
                    if q == k:
                        held = held * clear
                    mats[s, block, at] = held - out[:, at]
            mats[:, rows, :] = new
        for s in range(2):
            new = mats[s, block, :]
            for i in ((k + 1) % 4, (k + 2) % 4, (k + 3) % 4):
                at_i = slice(128 * i, 128 * i + 128)
                out = dot(mats[s, at_i, block], new)
                for q in range(4):
                    at = slice(128 * q, 128 * q + 128)
                    held = mats[s, at_i, at] if q != k else 0.0
                    mats[s, at_i, at] = held - out[:, at]


def pick_kernel(local, frames, residual, out, total, padded):
    step = pl.program_id(0)
    positions = step * PICK + lax.broadcasted_iota(jnp.int32, (1, PICK), 1)
    select = jnp.where(local[...] == positions, 1.0, 0.0).astype(BF16)
    padded[...] = jnp.zeros_like(padded)
    padded[:ROWS] = residual[...]
    parts = [v.astype(F32) for v in split3(padded[...])] + [jnp.zeros((8, PICK), F32)]
    packed = jnp.concatenate(
        [frames[...], jnp.zeros((16, PICK), BF16), jnp.concatenate(parts, axis=0).astype(BF16)], axis=0
    )
    picked = lax.dot_general(select, packed, (((1,), (1,)), ((), ())), preferred_element_type=F32)

    @pl.when(step == 0)
    def _():
        total[...] = picked

    @pl.when(step > 0)
    def _():
        total[...] += picked

    @pl.when(step == pl.num_programs(0) - 1)
    def _():
        out[...] = total[...].astype(BF16)


def pick(local, frames, residual):
    points = local.shape[0]
    return pl.pallas_call(
        pick_kernel,
        grid=(frames.shape[1] // PICK,),
        in_specs=[
            pl.BlockSpec(memory_space=pltpu.VMEM),
            pl.BlockSpec((112, PICK), lambda i: (0, i)),
            pl.BlockSpec((ROWS, PICK), lambda i: (0, i)),
        ],
        out_specs=pl.BlockSpec((points, 256), lambda i: (0, 0)),
        out_shape=jax.ShapeDtypeStruct((points, 256), BF16),
        scratch_shapes=[pltpu.VMEM((points, 256), F32), pltpu.VMEM((40, PICK), F32)],
        compiler_params=pltpu.CompilerParams(vmem_limit_bytes=60 << 20),
        name="pick",
    )(local, frames, residual)


def add_kernel(held, out):
    total = held[0].astype(F32)
    for i in range(1, 16):
        total = total + held[i].astype(F32)
    total = total.astype(BF16)
    for i in range(8):
        out[i] = total


def add(held):
    return pl.pallas_call(add_kernel, out_shape=jax.ShapeDtypeStruct((8, 64, 256), BF16), name="add")(held)


def mix_kernel(place, held, out):
    def total(at):
        value = held[at].astype(F32)
        for i in range(at + 1, at + 4):
            value = value + held[i].astype(F32)
        return value

    sums = total(0), total(4)
    first = place[0] == 0
    mine = jnp.where(first, sums[0], sums[1])
    other = pltpu.roll(jnp.where(first, sums[1], sums[0])[:, :128], 112, 1)
    lane = lax.broadcasted_iota(jnp.int32, (1, 128), 1)
    near = mine[:, :128] + jnp.where(lane >= 112, other, 0.0)
    tail = jnp.where(lane < 112, other, 0.0)
    value = jnp.concatenate([near, tail, mine[:, 128:]], axis=1).astype(BF16)
    for i in range(16):
        out[i] = value


def mix(place, held):
    return pl.pallas_call(
        mix_kernel,
        in_specs=[pl.BlockSpec(memory_space=pltpu.SMEM), pl.BlockSpec(memory_space=pltpu.VMEM)],
        out_shape=jax.ShapeDtypeStruct((16, 64, 384), BF16),
        name="mix",
    )(place, held)


def solve_kernel(near, far, point_row, point_col, delta_ref, sq_ref, mats):
    eye = lax.broadcasted_iota(jnp.int32, (BLOCK, BLOCK), 0) == lax.broadcasted_iota(jnp.int32, (BLOCK, BLOCK), 1)

    def columns(ref, s, at):
        return ref[:, 32 * s : 32 * s + 32, at].reshape(BLOCK, at.stop - at.start)

    def inner(a, b):
        total = 0.0
        for ref in (near, far):
            total = total + lax.dot_general(
                columns(ref, a, slice(0, 256)),
                columns(ref, b, slice(0, 256)),
                (((1,), (1,)), ((), ())),
                preferred_element_type=F32,
            )
        return total

    rows, cols = [], []
    for s in range(STEPS):
        products = inner(s, s)
        diagonal = jnp.where(eye, products, 0.0)
        rows.append(jnp.sum(diagonal, axis=0, keepdims=True))
        cols.append(jnp.sum(diagonal, axis=1, keepdims=True))
        sq_ref[BLOCK * s : BLOCK * s + BLOCK] = cols[s]
        kern = jnp.exp2(-SCALE * (cols[s] + rows[s] - 2.0 * products))
        mats[s] = kern + jnp.where(eye, RIDGE, 0.0)
    cross = jnp.exp2(-SCALE * (cols[1] + rows[0] - 2.0 * inner(1, 0)))
    cross = cross + jnp.where(point_col[...] == point_row[...], RIDGE, 0.0)
    invert(mats)
    lane = lax.broadcasted_iota(jnp.int32, (1, 128), 1)

    def block_res(s):
        both = []
        for ref in (near, far):
            part = [columns(ref, s, slice(256, 384)).astype(F32)]
            part.append(pltpu.roll(part[0], 128 - 40, 1))
            part.append(pltpu.roll(part[0], 128 - 80, 1))
            both.append(jnp.where(lane < 40, part[0] + (part[1] + part[2]), 0.0))
        return both[0] + pltpu.roll(both[1], 64, 1)

    delta = dot(mats[0], block_res(0))
    for s in range(STEPS):
        if s == 1:
            delta = dot(mats[1], block_res(1) - dot(cross, delta))
        turned = delta.T
        pad = jnp.zeros((8, BLOCK), F32)
        stacked = []
        for at in (0, 64):
            stacked += [v.astype(F32) for v in split3(turned[at : at + 40])] + [pad]
        delta_ref[:, BLOCK * s : BLOCK * s + BLOCK] = jnp.concatenate(stacked, axis=0).astype(BF16)


def solve(near, far, chosen):
    return pl.pallas_call(
        solve_kernel,
        out_shape=(
            jax.ShapeDtypeStruct((256, STEPS * BLOCK), BF16),
            jax.ShapeDtypeStruct((STEPS * BLOCK, 1), F32),
        ),
        scratch_shapes=[pltpu.VMEM((2, BLOCK, BLOCK), F32)],
        compiler_params=pltpu.CompilerParams(vmem_limit_bytes=40 << 20),
        name="solve",
    )(near, far, chosen[0].reshape(1, BLOCK), chosen[1].reshape(BLOCK, 1))


def update_kernel(s0, s1, s2, s3, near, far, delta, sq, local, mine_ref, theirs_ref):
    def squares(ref):
        value = ref[...].astype(F32)
        return jnp.sum(value * value, axis=0, keepdims=True)

    source_sq = squares(s0) + squares(s1) + squares(s2) + squares(s3)
    pad = jnp.zeros((32, TILE), BF16)
    source_near = jnp.concatenate([s0[...], s1[...], pad], axis=0)
    source_far = jnp.concatenate([s2[...], s3[...], pad], axis=0)
    positions = pl.program_id(0) * TILE + lax.broadcasted_iota(jnp.int32, (1, TILE), 1)
    change = jnp.zeros((256, TILE), F32)
    placed = jnp.zeros((256, TILE), F32)
    size = 256
    for c in range(STEPS * BLOCK // size):
        at = slice(size * c, size * c + size)
        s, first = (size * c) // BLOCK, (size * c) % BLOCK // 32
        block = slice(first, first + size // 32), slice(32 * s, 32 * s + 32), slice(0, 256)
        products = jnp.dot(near[block].reshape(size, 256), source_near, preferred_element_type=F32)
        products = products + jnp.dot(far[block].reshape(size, 256), source_far, preferred_element_type=F32)
        kern = jnp.exp2(-SCALE * (sq[at] + source_sq - 2.0 * products))
        here = jnp.where(local[at] == positions, 1.0, 0.0).astype(BF16)
        weights = delta[:, at]
        for part in split3(kern):
            change = change + jnp.dot(weights, part, preferred_element_type=F32)
        placed = placed + jnp.dot(weights, here, preferred_element_type=F32)
    for at, out in ((0, mine_ref), (128, theirs_ref)):
        moved = change[at : at + 40] + (change[at + 40 : at + 80] + change[at + 80 : at + 120])
        added = placed[at : at + 40] + (placed[at + 40 : at + 80] + placed[at + 80 : at + 120])
        out[0] = moved + RIDGE * added
        out[1] = added


def update(sources, near, far, delta, sq, local):
    whole = pl.BlockSpec(memory_space=pltpu.VMEM)
    rows = sources[0].shape[1]
    return pl.pallas_call(
        update_kernel,
        grid=(rows // TILE,),
        in_specs=[pl.BlockSpec((112, TILE), lambda i: (0, i))] * 4 + [whole] * 5,
        out_specs=[pl.BlockSpec((2, 40, TILE), lambda i: (0, 0, i))] * 2,
        out_shape=[jax.ShapeDtypeStruct((2, 40, rows), F32)] * 2,
        compiler_params=pltpu.CompilerParams(vmem_limit_bytes=40 << 20),
        name="update",
    )(*sources, near, far, delta, sq, local)


def finish_kernel(place, residual, coefficients, mine, got, res_out, coef_out):
    own = pl.program_id(0) == place[1]
    value = jnp.where(own, mine[...], got[...])
    res_out[...] = residual[...] - value[0, :ROWS]
    coef_out[...] = coefficients[...] + value[1, :ROWS]


def finish(place, residual, coefficients, mine, got):
    whole = pl.BlockSpec(memory_space=pltpu.VMEM)
    half = pl.BlockSpec((ROWS, residual.shape[1] // 2), lambda i: (0, i))
    return pl.pallas_call(
        finish_kernel,
        grid=(2,),
        in_specs=[pl.BlockSpec(memory_space=pltpu.SMEM), half, half, whole, whole],
        out_specs=[half, half],
        out_shape=[jax.ShapeDtypeStruct(residual.shape, F32)] * 2,
        compiler_params=pltpu.CompilerParams(vmem_limit_bytes=40 << 20),
        name="finish",
    )(place, residual, coefficients, mine, got)


def on_device(frames, residual, coefficients, block_index):
    rows = frames.shape[1]
    dp, feat = lax.axis_index("dp"), lax.axis_index("feat")
    h, c = feat // 2, feat % 2
    place = jnp.stack([h, c]).astype(jnp.int32)
    own_half = lax.dynamic_slice_in_dim(frames, c * (rows // 2), rows // 2, axis=1)
    other_half = lax.dynamic_slice_in_dim(frames, (1 - c) * (rows // 2), rows // 2, axis=1)
    own_half, other_half, block_index = lax.optimization_barrier((own_half, other_half, block_index))
    across = swap(own_half, 1, 0)
    beside = swap(other_half, 0, 1)

    points = block_index.reshape(STEPS, 16, 32).transpose(1, 0, 2).reshape(-1, 1)
    held = pick(points - dp * rows, frames, residual).reshape(16, 64, 256)
    held = add(lax.all_to_all(held, "dp", 0, 0, axis_index_groups=PLANE, tiled=True))
    held, across = lax.optimization_barrier((held, across))
    held = lax.all_to_all(held, AXES, 0, 0, axis_index_groups=LINE, tiled=True)
    held, other_half = lax.optimization_barrier((held, other_half))
    diagonal = swap(other_half, 1, 1)
    near = lax.all_to_all(mix(place, held), "dp", 0, 0, axis_index_groups=PLANE, tiled=True)
    far = swap(near, 0, 1)

    delta, sq = solve(near, far, block_index)
    local = block_index.reshape(-1, 1) - dp * rows - c * (rows // 2)
    mine, theirs = update((own_half, across, beside, diagonal), near, far, delta, sq, local)
    return finish(place, residual, coefficients, mine, swap(theirs, 0, 1))


def solution(mesh):
    return jax.shard_map(
        on_device,
        mesh=mesh,
        in_specs=(P("feat", "dp"), P("feat", "dp"), P("feat", "dp"), P()),
        out_specs=(P("feat", "dp"), P("feat", "dp")),
        check_vma=False,
    )
```

profile of v0, /device:TPU:1, one launch (start us, length us, event | category | flops | bytes accessed | tf_op | source)
XLA Modules:
  0.0 130.7 jit_solution(12441291243768530938)
XLA Ops:
  0.7 0.0 copy-start.5
  0.7 2.0 %constant_dynamic-slice_fusion = (bf16[112,2048]{1,0:T(8,128)(2,1)}, bf16[112,2048]{1,0:T(8,128)(2,1)S(1)}) fusion(bf16[112,4096]{1,0:T(8,128)(2,1)} %frames.1, s32[]{:T(128)S(6)} %select_n.20, s32[]{:T(128)S(6)} %select_n.19), kind=kLoop, calls=%fused_computation.5 | loop fusion | bytes 1835016 | tf_op jit(solution)/shard_map/dynamic_slice | solution.py:328
  2.7 0.0 copy-done.5
  2.7 0.1 sub.42
  2.8 1.3 %sub.48.local = s32[1024,1]{1,0:T(8,128)} reshape(s32[16,2,32]{2,1,0:T(2,128)S(1)} %bitcast.15) | data formatting | bytes 8192 | tf_op jit(solution)/shard_map/sub | solution.py:334
  4.1 5.7 %pick.1 = bf16[1024,256]{1,0:T(8,128)(2,1)} custom-call(s32[1024,1]{1,0:T(8,128)} %sub.48.local, bf16[112,4096]{1,0:T(8,128)(2,1)} %frames.1, f32[37,4096]{1,0:T(8,128)} %residual.3), custom_call_target="tpu_custom_call" | custom-call | tf_op jit(solution)/shard_map/pick/pallas_call | solution.py:133
  9.9 7.6 %all-to-all-start = ((bf16[16,64,256]{2,1,0:T(8,128)(2,1)}), bf16[16,64,256]{2,1,0:T(8,128)(2,1)S(1)}, u32[]{:S(2)}, u32[]{:S(2)}) async-start(bf16[16,64,256]{2,1,0:T(8,128)(2,1)} %bitcast.14), calls=%async_computation | async-start | bytes 1048576 | tf_op jit(solution)/shard_map/all_to_all | solution.py:335
  17.4 7.0 %collective-permute-start = (bf16[112,2048]{1,0:T(8,128)(2,1)S(1)}, bf16[112,2048]{1,0:T(8,128)(2,1)S(1)}, u32[]{:S(2)}, u32[]{:S(2)}) collective-permute-start(bf16[112,2048]{1,0:T(8,128)(2,1)S(1)} %get-tuple-element.13.s0), channel_id=1, source_target_pairs={{0,2},{1,3},{2,0},{3,1},{4,6},{5,7},{6,4},{7,5},{8,10},{9,11},{10,... | collective-permute-start | bytes 1376264 | tf_op jit(solution)/shard_map/ppermute | solution.py:38
  24.5 3.5 %all-to-all-done.held = bf16[16,64,256]{2,1,0:T(8,128)(2,1)S(1)} async-done(((bf16[16,64,256]{2,1,0:T(8,128)(2,1)}), bf16[16,64,256]{2,1,0:T(8,128)(2,1)S(1)}, u32[]{:S(2)}, u32[]{:S(2)}) %all-to-all-start) | async-done | bytes 524320 | tf_op jit(solution)/shard_map/all_to_all | solution.py:335
  28.0 0.0 copy-start.3
  28.0 0.8 copy-done.3
  28.8 1.8 %add.17 = bf16[8,64,256]{2,1,0:T(8,128)(2,1)} custom-call(bf16[16,64,256]{2,1,0:T(8,128)(2,1)} %copy-done.3), custom_call_target="tpu_custom_call" | custom-call | tf_op jit(solution)/shard_map/add/pallas_call | solution.py:159
  30.6 5.9 %collective-permute-done.s1 = bf16[112,2048]{1,0:T(8,128)(2,1)S(1)} collective-permute-done((bf16[112,2048]{1,0:T(8,128)(2,1)S(1)}, bf16[112,2048]{1,0:T(8,128)(2,1)S(1)}, u32[]{:S(2)}, u32[]{:S(2)}) %collective-permute-start) | collective-permute-done | bytes 458784 | tf_op jit(solution)/shard_map/ppermute | solution.py:38
  36.5 13.6 %all-to-all-start.1 = ((bf16[8,64,256]{2,1,0:T(8,128)(2,1)}), bf16[8,64,256]{2,1,0:T(8,128)(2,1)S(1)}, u32[]{:S(2)}, u32[]{:S(2)}) async-start(bf16[8,64,256]{2,1,0:T(8,128)(2,1)} %add.17), calls=%async_computation.1 | async-start | bytes 524288 | tf_op jit(solution)/shard_map/all_to_all | solution.py:337
  50.1 0.7 pad_add_fusion.place
  50.8 8.6 %all-to-all-done.1.held = bf16[8,64,256]{2,1,0:T(8,128)(2,1)S(1)} async-done(((bf16[8,64,256]{2,1,0:T(8,128)(2,1)}), bf16[8,64,256]{2,1,0:T(8,128)(2,1)S(1)}, u32[]{:S(2)}, u32[]{:S(2)}) %all-to-all-start.1) | async-done | bytes 262176 | tf_op jit(solution)/shard_map/all_to_all | solution.py:337
  59.4 0.0 copy-start.4
  59.4 0.7 copy-done.4
  60.1 2.0 %mix.1 = bf16[16,64,384]{2,1,0:T(8,128)(2,1)} custom-call(s32[2]{0:T(128)} %pad_add_fusion.place, bf16[8,64,256]{2,1,0:T(8,128)(2,1)} %copy-done.4), custom_call_target="tpu_custom_call" | custom-call | tf_op jit(solution)/shard_map/mix/pallas_call | solution.py:182
  62.1 17.6 %all_to_all.15.near = bf16[16,64,384]{2,1,0:T(8,128)(2,1)S(1)} all-to-all(bf16[16,64,384]{2,1,0:T(8,128)(2,1)} %mix.1), channel_id=1, replica_groups={{0,16,32,48,64,80,96,112,128,144,160,176,192,208,224,240},{4,20,36,52,6..., dimensions={0} | all-to-all | bytes 1572864 | tf_op jit(solution)/shard_map/all_to_all | solution.py:340
  79.7 4.3 %collective-permute-start.3 = (bf16[16,64,384]{2,1,0:T(8,128)(2,1)S(1)}, bf16[16,64,384]{2,1,0:T(8,128)(2,1)S(1)}, u32[]{:S(2)}, u32[]{:S(2)}) collective-permute-start(bf16[16,64,384]{2,1,0:T(8,128)(2,1)S(1)} %all_to_all.15.near), channel_id=1, source_target_pairs={{0,1},{1,0},{2,3},{3,2},{4,5},{5,4},{6,7},{7,6},{8,9},{9,8},{10,11... | collective-permute-start | bytes 2359304 | tf_op jit(solution)/shard_map/ppermute | solution.py:38
  84.0 0.0 collective-permute-start.1
  84.0 1.1 collective-permute-start.2
  85.1 0.1 copy.9.point_col
  85.2 0.2 copy.12
  85.5 1.1 collective-permute-done.3.far
  86.6 28.7 %solve.1 = (bf16[256,1024]{1,0:T(8,128)(2,1)S(1)}, f32[1024,1]{1,0:T(8,128)S(1)}) custom-call(bf16[16,64,384]{2,1,0:T(8,128)(2,1)S(1)} %all_to_all.15.near, bf16[16,64,384]{2,1,0:T(8,128)(2,1)S(1)} %collective-permute-done.3.far, s32[1,512]{1,0:T(1,128)S(1)} %get-tuple-element.29.point_row, s32[512,1]{1,0:T(8,128)S(1)} %copy.9.point_col), custom_call_target="tpu_custom_call" | custom-call | tf_op jit(solution)/shard_map/solve/pallas_call | solution.py:243
  115.2 0.0 collective-permute-done.1.s2
  115.2 0.0 collective-permute-done.2.s3
  115.3 0.0 copy-start
  115.3 0.0 copy-start.1
  115.3 11.4 %update.1 = (f32[2,40,2048]{2,1,0:T(8,128)S(1)}, f32[2,40,2048]{2,1,0:T(8,128)S(1)}) custom-call(bf16[112,2048]{1,0:T(8,128)(2,1)S(1)} %get-tuple-element.13.s0, bf16[112,2048]{1,0:T(8,128)(2,1)S(1)} %collective-permute-done.s1, bf16[112,2048]{1,0:T(8,128)(2,1)} %collective-permute-done.1.s2, bf16[112,2048]{1,0:T(8,128)(2,1)} %collective-permute-done.2.s3, ...), custom_call_target="tpu_custom_call" | custom-call | tf_op jit(solution)/shard_map/update/pallas_call | solution.py:290
  126.7 0.0 copy-start.2
  126.7 0.5 collective-permute-start.4
  127.2 1.7 %collective-permute-done.4.got = f32[2,40,2048]{2,1,0:T(8,128)S(1)} collective-permute-done((f32[2,40,2048]{2,1,0:T(8,128)S(1)}, f32[2,40,2048]{2,1,0:T(8,128)S(1)}, u32[]{:S(2)}, u32[]{:S(2)}) %collective-permute-start.4) | collective-permute-done | bytes 655392 | tf_op jit(solution)/shard_map/ppermute | solution.py:38
  128.9 0.0 copy-done
  128.9 0.0 copy-done.1
  128.9 0.0 copy-done.2
  128.9 1.8 %finish.1 = (f32[37,4096]{1,0:T(8,128)}, f32[37,4096]{1,0:T(8,128)}) custom-call(s32[2]{0:T(128)S(1)} %copy-done.2, f32[37,4096]{1,0:T(8,128)S(1)} %copy-done, f32[37,4096]{1,0:T(8,128)S(1)} %copy-done.1, f32[2,40,2048]{2,1,0:T(8,128)S(1)} %get-tuple-element.22.mine, f32[2,40,2048]{2,1,0:T(8,128)S(1)} %collective-permute-done.4.got), custom_call_target="tpu_custom_call" | custom-call | tf_op jit(solution)/shard_map/finish/pallas_call | solution.py:311
  (4 shorter events, 0.0 us)
Async XLA Ops:
  0.7 2.0 %copy-start.5 = (s32[2,512]{1,0:T(2,128)S(1)}, s32[2,512]{1,0:T(2,128)}, u32[]{:S(2)}) copy-start(s32[2,512]{1,0:T(2,128)} %param.7) | copy-start | bytes 12292
  9.9 18.1 %all-to-all-start = ((bf16[16,64,256]{2,1,0:T(8,128)(2,1)}), bf16[16,64,256]{2,1,0:T(8,128)(2,1)S(1)}, u32[]{:S(2)}, u32[]{:S(2)}) async-start(bf16[16,64,256]{2,1,0:T(8,128)(2,1)} %bitcast.14), calls=%async_computation | async-start | bytes 1048576 | tf_op jit(solution)/shard_map/all_to_all | solution.py:335
  17.4 19.0 %collective-permute-start = (bf16[112,2048]{1,0:T(8,128)(2,1)S(1)}, bf16[112,2048]{1,0:T(8,128)(2,1)S(1)}, u32[]{:S(2)}, u32[]{:S(2)}) collective-permute-start(bf16[112,2048]{1,0:T(8,128)(2,1)S(1)} %get-tuple-element.13.s0), channel_id=1, source_target_pairs={{0,2},{1,3},{2,0},{3,1},{4,6},{5,7},{6,4},{7,5},{8,10},{9,11},{10,... | collective-permute-start | bytes 1376264 | tf_op jit(solution)/shard_map/ppermute | solution.py:38
  28.0 0.8 copy-start.3
  36.5 22.9 %all-to-all-start.1 = ((bf16[8,64,256]{2,1,0:T(8,128)(2,1)}), bf16[8,64,256]{2,1,0:T(8,128)(2,1)S(1)}, u32[]{:S(2)}, u32[]{:S(2)}) async-start(bf16[8,64,256]{2,1,0:T(8,128)(2,1)} %add.17), calls=%async_computation.1 | async-start | bytes 524288 | tf_op jit(solution)/shard_map/all_to_all | solution.py:337
  59.4 0.7 copy-start.4
  79.7 6.9 %collective-permute-start.3 = (bf16[16,64,384]{2,1,0:T(8,128)(2,1)S(1)}, bf16[16,64,384]{2,1,0:T(8,128)(2,1)S(1)}, u32[]{:S(2)}, u32[]{:S(2)}) collective-permute-start(bf16[16,64,384]{2,1,0:T(8,128)(2,1)S(1)} %all_to_all.15.near), channel_id=1, source_target_pairs={{0,1},{1,0},{2,3},{3,2},{4,5},{5,4},{6,7},{7,6},{8,9},{9,8},{10,11... | collective-permute-start | bytes 2359304 | tf_op jit(solution)/shard_map/ppermute | solution.py:38
  84.0 31.2 %collective-permute-start.1 = (bf16[112,2048]{1,0:T(8,128)(2,1)}, bf16[112,2048]{1,0:T(8,128)(2,1)}, u32[]{:S(2)}, u32[]{:S(2)}) collective-permute-start(bf16[112,2048]{1,0:T(8,128)(2,1)} %get-tuple-element.18), channel_id=1, source_target_pairs={{0,1},{1,0},{2,3},{3,2},{4,5},{5,4},{6,7},{7,6},{8,9},{9,8},{10,11... | collective-permute-start | bytes 1376264 | tf_op jit(solution)/shard_map/ppermute | solution.py:38
  84.0 31.3 %collective-permute-start.2 = (bf16[112,2048]{1,0:T(8,128)(2,1)}, bf16[112,2048]{1,0:T(8,128)(2,1)}, u32[]{:S(2)}, u32[]{:S(2)}) collective-permute-start(bf16[112,2048]{1,0:T(8,128)(2,1)} %get-tuple-element.18), channel_id=1, source_target_pairs={{0,3},{1,2},{2,1},{3,0},{4,7},{5,6},{6,5},{7,4},{8,11},{9,10},{10,... | collective-permute-start | bytes 1376264 | tf_op jit(solution)/shard_map/ppermute | solution.py:38
  115.3 13.6 %copy-start = (f32[37,4096]{1,0:T(8,128)S(1)}, f32[37,4096]{1,0:T(8,128)}, u32[]{:S(2)}) copy-start(f32[37,4096]{1,0:T(8,128)} %residual.3) | copy-start | bytes 1818628
  115.3 13.6 %copy-start.1 = (f32[37,4096]{1,0:T(8,128)S(1)}, f32[37,4096]{1,0:T(8,128)}, u32[]{:S(2)}) copy-start(f32[37,4096]{1,0:T(8,128)} %coefficients.1) | copy-start | bytes 1818628
  126.7 2.2 %copy-start.2 = (s32[2]{0:T(128)S(1)}, s32[2]{0:T(128)}, u32[]{:S(2)}) copy-start(s32[2]{0:T(128)} %pad_add_fusion.place) | copy-start | bytes 28
  126.7 2.2 %collective-permute-start.4 = (f32[2,40,2048]{2,1,0:T(8,128)S(1)}, f32[2,40,2048]{2,1,0:T(8,128)S(1)}, u32[]{:S(2)}, u32[]{:S(2)}) collective-permute-start(f32[2,40,2048]{2,1,0:T(8,128)S(1)} %get-tuple-element.23), channel_id=1, source_target_pairs={{0,1},{1,0},{2,3},{3,2},{4,5},{5,4},{6,7},{7,6},{8,9},{9,8},{10,11... | collective-permute-start | bytes 1966088 | tf_op jit(solution)/shard_map/ppermute | solution.py:38
where the time goes:
time: 131 us
  Pallas kernels  51.4 us (39%)
  starting transfers between devices  34.1 us (26%)
  waiting for transfers between devices  20.9 us (16%)
  blocking collectives  17.6 us (13%)
  local copies, waits for them, and re-layouts  5.35 us (4%)
    pallas_call x1, Pallas kernels, solve(): pl.pallas_call(solve_kernel, out_shape=(jax.ShapeDtypeStruct((256, STEPS...  28.7 us
    all_to_all x1, blocking collectives, on_device(): lax.all_to_all(mix(place, held), 'dp', 0, 0, axis_index_groups=PLANE, til...  17.6 us
    all_to_all x1, starting transfers between devices, on_device(): held = lax.all_to_all(held, AXES, 0, 0, axis_index_groups=LINE, tiled=True)  13.6 us
    ppermute x5, starting transfers between devices, swap(): return lax.ppermute(value, AXES, permutation(move))  12.9 us
    pallas_call x1, Pallas kernels, update(): pl.pallas_call(update_kernel, grid=(rows // TILE,), in_specs=[pl.BlockSpe...  11.4 us
    ppermute x5, waiting for transfers between devices, swap(): return lax.ppermute(value, AXES, permutation(move))  8.74 us
    all_to_all x1, waiting for transfers between devices, on_device(): held = lax.all_to_all(held, AXES, 0, 0, axis_index_groups=LINE, tiled=True)  8.63 us
    all_to_all x1, starting transfers between devices, on_device(): lax.all_to_all(held, 'dp', 0, 0, axis_index_groups=PLANE, tiled=True)  7.58 us
  transfers between devices with their start and end apart: 7, of which 5 were waited for; matrix products, arithmetic and copies ran while one was open for 1% of the time, Pallas kernels for 23%

commit v1 on v0

--- a/solution.py
+++ b/solution.py
@@ -51,56 +51,81 @@
 
 
 def dot(a, b):
-    return jnp.dot(a, b, preferred_element_type=F32, precision=lax.Precision.HIGHEST)
-
-
-def invert(mats):
-    lane = lax.broadcasted_iota(jnp.int32, (1, PANEL, 128), 2)
-    row = lax.broadcasted_iota(jnp.int32, (1, PANEL, 128), 1)
-    lane1 = lax.broadcasted_iota(jnp.int32, (1, 128), 1)
+    ah, am, al = split3(a)
+    bh, bm, bl = split3(b)
+    lhs = jnp.concatenate([al, ah, am, am, ah, ah], axis=1)
+    rhs = jnp.concatenate([bh, bl, bm, bh, bm, bh], axis=0)
+    return jnp.dot(lhs, rhs, preferred_element_type=F32)
+
+
+def dot_rows(a, b):
+    ah, am, al = split3(a)
+    n = a.shape[0]
+    total = 0.0
+    for value, lhs in zip(reversed(split3(b)), ((ah,), (am, ah), (al, am, ah))):
+        out = jnp.dot(jnp.concatenate(lhs, axis=0), value, preferred_element_type=F32)
+        for i in range(len(lhs)):
+            total = total + out[n * i : n * i + n]
+    return total
+
+
+def invert(mats, packed):
+    lane = lax.broadcasted_iota(jnp.int32, (1, 128), 1)
+    lower = lane < 64
+    row = lax.broadcasted_iota(jnp.int32, (PANEL, 128), 0)
+
+    def exchange(one, two):
+        return jnp.where(lower, one, pltpu.roll(two, 64, 1)), jnp.where(lower, pltpu.roll(one, 64, 1), two)
+
     for k in range(4):
         r0 = 128 * k
         block = slice(r0, r0 + 128)
+        packed[0], packed[1] = exchange(mats[0, block, block], mats[1, block, block])
         for p in range(128 // PANEL):
             b = PANEL * p
-            rows = slice(r0 + b, r0 + b + PANEL)
-            tiles = [mats[:, rows, 128 * q : 128 * q + 128] for q in range(4)]
-            old = tiles[k]
-            cols = [jnp.broadcast_to(old[:, :, b + j : b + j + 1], (2, PANEL, 128)) for j in range(PANEL)]
+            half, first = b // 64, b % 64
+            rows = slice(b, b + PANEL)
+            new = [packed[0, rows], packed[1, rows]]
+            old = exchange(*new)
+            cols = []
+            for j in range(first, first + PANEL):
+                pair = [jnp.broadcast_to(new[half][:, i : i + 1], (PANEL, 128)) for i in (j, 64 + j)]
+                cols.append(jnp.where(lower, *pair))
             for j in range(PANEL):
                 one = jnp.where(row == j, 1.0, 0.0)
-                inv = 1.0 / cols[j][:, j : j + 1, :]
-                factor = cols[j] - one
+                factor = (cols[j] - one) * (1.0 / cols[j][j : j + 1])
                 for q in range(j + 1, PANEL):
-                    cols[q] = cols[q] - factor * (cols[q][:, j : j + 1, :] * inv)
-                tiles[k] = jnp.where(lane == b + j, one, tiles[k])
-                for q in range(4):
-                    tiles[q] = tiles[q] - factor * (tiles[q][:, j : j + 1, :] * inv)
-            new = jnp.concatenate(tiles, axis=2)
-            sign = jnp.where(lane1 < b, -1.0, jnp.where(lane1 < b + PANEL, 0.0, 1.0))
-            clear = jnp.where((lane1 >= b) & (lane1 < b + PANEL), 0.0, 1.0)
-            for s in range(2):
-                h, m, l = split3(old[s] * sign)
-                nh, nm, nl = split3(new[s])
+                    cols[q] = cols[q] - factor * cols[q][j : j + 1]
+                new[half] = jnp.where((lane & 63) == first + j, one, new[half])
+                new = [value - factor * value[j : j + 1] for value in new]
+            sign = jnp.where(lane < b, -1.0, jnp.where(lane < b + PANEL, 0.0, 1.0))
+            nh, nm, nl = split3(jnp.concatenate(new, axis=1))
+            rhs = jnp.concatenate([nh, nm, nh, nl, nh, nm], axis=0)
+            outs = []
+            for value in old:
+                h, m, l = split3(value * sign)
                 lhs = jnp.concatenate([h, h, m, h, l, m], axis=0)
-                rhs = jnp.concatenate([nh, nm, nh, nl, nh, nm], axis=0)
-                out = lax.dot_general(lhs, rhs, (((0,), (0,)), ((), ())), preferred_element_type=F32)
-                for q in range(4):
-                    at = slice(128 * q, 128 * q + 128)
-                    held = mats[s, block, at]
-                    if q == k:
-                        held = held * clear
-                    mats[s, block, at] = held - out[:, at]
-            mats[:, rows, :] = new
+                outs.append(lax.dot_general(lhs, rhs, (((0,), (0,)), ((), ())), preferred_element_type=F32))
+            for i in range(2):
+                at = slice(128 * i, 128 * i + 128)
+                held = packed[i]
+                if i == half:
+                    held = jnp.where(((lane & 63) >= first) & ((lane & 63) < first + PANEL), 0.0, held)
+                packed[i] = held - jnp.where(lower, outs[0][:, at], outs[1][:, at])
+                packed[i, rows] = new[i]
+        mats[0, block, block], mats[1, block, block] = exchange(packed[0], packed[1])
+        others = [slice(128 * i, 128 * i + 128) for i in ((k + 1) % 4, (k + 2) % 4, (k + 3) % 4)]
         for s in range(2):
-            new = mats[s, block, :]
-            for i in ((k + 1) % 4, (k + 2) % 4, (k + 3) % 4):
-                at_i = slice(128 * i, 128 * i + 128)
-                out = dot(mats[s, at_i, block], new)
-                for q in range(4):
-                    at = slice(128 * q, 128 * q + 128)
-                    held = mats[s, at_i, at] if q != k else 0.0
-                    mats[s, at_i, at] = held - out[:, at]
+            inverse = mats[s, block, block]
+            rest = dot(inverse, jnp.concatenate([mats[s, block, at] for at in others], axis=1))
+            left = jnp.concatenate([mats[s, at, block] for at in others], axis=0)
+            out = dot(left, jnp.concatenate([inverse, rest], axis=1))
+            for i, at_i in enumerate(others):
+                here = slice(128 * i, 128 * i + 128)
+                mats[s, block, at_i] = rest[:, here]
+                mats[s, at_i, block] = -out[here, :128]
+                for j, at_j in enumerate(others):
+                    mats[s, at_i, at_j] = mats[s, at_i, at_j] - out[here, 128 * j + 128 : 128 * j + 256]
 
 
 def pick_kernel(local, frames, residual, out, total, padded):
@@ -187,7 +212,7 @@
     )(place, held)
 
 
-def solve_kernel(near, far, point_row, point_col, delta_ref, sq_ref, mats):
+def solve_kernel(near, far, point_row, point_col, delta_ref, sq_ref, mats, packed, grams):
     eye = lax.broadcasted_iota(jnp.int32, (BLOCK, BLOCK), 0) == lax.broadcasted_iota(jnp.int32, (BLOCK, BLOCK), 1)
 
     def columns(ref, s, at):
@@ -212,10 +237,9 @@
         cols.append(jnp.sum(diagonal, axis=1, keepdims=True))
         sq_ref[BLOCK * s : BLOCK * s + BLOCK] = cols[s]
         kern = jnp.exp2(-SCALE * (cols[s] + rows[s] - 2.0 * products))
-        mats[s] = kern + jnp.where(eye, RIDGE, 0.0)
-    cross = jnp.exp2(-SCALE * (cols[1] + rows[0] - 2.0 * inner(1, 0)))
+        mats[s] = grams[s] = kern + jnp.where(eye, RIDGE, 0.0)
+    cross = jnp.exp2(-SCALE * (cols[0] + rows[1] - 2.0 * inner(0, 1)))
     cross = cross + jnp.where(point_col[...] == point_row[...], RIDGE, 0.0)
-    invert(mats)
     lane = lax.broadcasted_iota(jnp.int32, (1, 128), 1)
 
     def block_res(s):
@@ -225,17 +249,19 @@
             part.append(pltpu.roll(part[0], 128 - 40, 1))
             part.append(pltpu.roll(part[0], 128 - 80, 1))
             both.append(jnp.where(lane < 40, part[0] + (part[1] + part[2]), 0.0))
-        return both[0] + pltpu.roll(both[1], 64, 1)
-
-    delta = dot(mats[0], block_res(0))
+        return (both[0] + pltpu.roll(both[1], 64, 1)).T
+
+    res = [block_res(s) for s in range(STEPS)]
+    invert(mats, packed)
     for s in range(STEPS):
         if s == 1:
-            delta = dot(mats[1], block_res(1) - dot(cross, delta))
-        turned = delta.T
+            res[1] = res[1] - dot_rows(delta, cross)
+        delta = dot_rows(res[s], mats[s])
+        delta = delta + dot_rows(res[s] - dot_rows(delta, grams[s]), mats[s])
         pad = jnp.zeros((8, BLOCK), F32)
         stacked = []
         for at in (0, 64):
-            stacked += [v.astype(F32) for v in split3(turned[at : at + 40])] + [pad]
+            stacked += [v.astype(F32) for v in split3(delta[at : at + 40])] + [pad]
         delta_ref[:, BLOCK * s : BLOCK * s + BLOCK] = jnp.concatenate(stacked, axis=0).astype(BF16)
 
 
@@ -246,10 +272,15 @@
             jax.ShapeDtypeStruct((256, STEPS * BLOCK), BF16),
             jax.ShapeDtypeStruct((STEPS * BLOCK, 1), F32),
         ),
-        scratch_shapes=[pltpu.VMEM((2, BLOCK, BLOCK), F32)],
+        scratch_shapes=[
+            pltpu.VMEM((2, BLOCK, BLOCK), F32),
+            pltpu.VMEM((2, 128, 128), F32),
+            pltpu.VMEM((2, BLOCK, BLOCK), F32),
+        ],
         compiler_params=pltpu.CompilerParams(vmem_limit_bytes=40 << 20),
+        cost_estimate=pl.CostEstimate(flops=1 << 20, bytes_accessed=1 << 20, transcendentals=0),
         name="solve",
-    )(near, far, chosen[0].reshape(1, BLOCK), chosen[1].reshape(BLOCK, 1))
+    )(near, far, chosen[1].reshape(1, BLOCK), chosen[0].reshape(BLOCK, 1))
 
 
 def update_kernel(s0, s1, s2, s3, near, far, delta, sq, local, mine_ref, theirs_ref):
@@ -326,17 +357,14 @@
     place = jnp.stack([h, c]).astype(jnp.int32)
     own_half = lax.dynamic_slice_in_dim(frames, c * (rows // 2), rows // 2, axis=1)
     other_half = lax.dynamic_slice_in_dim(frames, (1 - c) * (rows // 2), rows // 2, axis=1)
-    own_half, other_half, block_index = lax.optimization_barrier((own_half, other_half, block_index))
-    across = swap(own_half, 1, 0)
     beside = swap(other_half, 0, 1)
 
     points = block_index.reshape(STEPS, 16, 32).transpose(1, 0, 2).reshape(-1, 1)
     held = pick(points - dp * rows, frames, residual).reshape(16, 64, 256)
     held = add(lax.all_to_all(held, "dp", 0, 0, axis_index_groups=PLANE, tiled=True))
-    held, across = lax.optimization_barrier((held, across))
     held = lax.all_to_all(held, AXES, 0, 0, axis_index_groups=LINE, tiled=True)
-    held, other_half = lax.optimization_barrier((held, other_half))
-    diagonal = swap(other_half, 1, 1)
+    held, own_half, other_half = lax.optimization_barrier((held, own_half, other_half))
+    across, diagonal = swap(own_half, 1, 0), swap(other_half, 1, 1)
     near = lax.all_to_all(mix(place, held), "dp", 0, 0, axis_index_groups=PLANE, tiled=True)
     far = swap(near, 0, 1)
 

time: 131 us -> 131 us (level)
  starting transfers between devices: 34.1 us -> 18.9 us
  blocking collectives: 17.6 us -> 32.8 us
  waiting for transfers between devices: 20.9 us -> 24.4 us
  Pallas kernels: 51.4 us -> 48.8 us
    all_to_all x0 -> x1, blocking collectives: none -> 18.2 us  [on_device(): lax.all_to_all(held, 'dp', 0, 0, axis_index_groups=PLANE, tiled=True)]
    ppermute x5, waiting for transfers between devices: 8.74 us -> 16.4 us  [swap(): return lax.ppermute(value, AXES, permutation(move))]
    all_to_all x1 -> x0, starting transfers between devices: 7.58 us -> none  [on_device(): lax.all_to_all(held, 'dp', 0, 0, axis_index_groups=PLANE, tiled=True)]
    all_to_all x1, starting transfers between devices: 13.6 us -> 8.18 us  [on_device(): held = lax.all_to_all(held, AXES, 0, 0, axis_index_groups=LINE, tiled=True)]
    all_to_all x1 -> x0, waiting for transfers between devices: 3.51 us -> none  [on_device(): lax.all_to_all(held, 'dp', 0, 0, axis_index_groups=PLANE, tiled=True)]
    all_to_all x1, blocking collectives: 17.6 us -> 14.6 us  [on_device(): lax.all_to_all(mix(place, held), 'dp', 0, 0, axis_index_groups=PLANE, til...]
    pallas_call x1, Pallas kernels: 28.7 us -> 26 us  [solve(): pl.pallas_call(solve_kernel, out_shape=(jax.ShapeDtypeStruct((256, STEPS...]
    ppermute x5, starting transfers between devices: 12.9 us -> 10.8 us  [swap(): return lax.ppermute(value, AXES, permutation(move))]
  transfers between devices with their start and end apart: 7 -> 6, of which waited for: 5 -> 3; matrix products, arithmetic and copies ran while one was open for 1% -> 1% of each run, Pallas kernels for 23% -> 20%
where the time goes in v1:
time: 131 us; the launch traced here: 130 us
  Pallas kernels  48.8 us (37%)
  blocking collectives  32.8 us (25%)
  waiting for transfers between devices  24.4 us (19%)
  starting transfers between devices  18.9 us (14%)
  local copies, waits for them, and re-layouts  4.04 us (3%)
    pallas_call x1, Pallas kernels, solve(): pl.pallas_call(solve_kernel, out_shape=(jax.ShapeDtypeStruct((256, STEPS...  26 us
    all_to_all x1, blocking collectives, on_device(): lax.all_to_all(held, 'dp', 0, 0, axis_index_groups=PLANE, tiled=True)  18.2 us
    ppermute x5, waiting for transfers between devices, swap(): return lax.ppermute(value, AXES, permutation(move))  16.4 us
    all_to_all x1, blocking collectives, on_device(): lax.all_to_all(mix(place, held), 'dp', 0, 0, axis_index_groups=PLANE, til...  14.6 us
    pallas_call x1, Pallas kernels, update(): pl.pallas_call(update_kernel, grid=(rows // TILE,), in_specs=[pl.BlockSpe...  11.4 us
    ppermute x5, starting transfers between devices, swap(): return lax.ppermute(value, AXES, permutation(move))  10.8 us
    all_to_all x1, starting transfers between devices, on_device(): held = lax.all_to_all(held, AXES, 0, 0, axis_index_groups=LINE, tiled=True)  8.18 us
    all_to_all x1, waiting for transfers between devices, on_device(): held = lax.all_to_all(held, AXES, 0, 0, axis_index_groups=LINE, tiled=True)  8.02 us
  transfers between devices with their start and end apart: 6, of which 3 were waited for; matrix products, arithmetic and copies ran while one was open for 1% of the time, Pallas kernels for 20%

profile of v1, /device:TPU:1, one launch (start us, length us, event | category | flops | bytes accessed | tf_op | source)
XLA Modules:
  0.0 130.3 jit_solution(13357468717904450798)
XLA Ops:
  0.6 0.0 copy-start.5
  0.7 0.7 copy-done.5
  1.3 0.1 sub.41
  1.4 1.3 %sub.48.local = s32[1024,1]{1,0:T(8,128)} reshape(s32[16,2,32]{2,1,0:T(2,128)S(1)} %bitcast.15) | data formatting | bytes 8192 | tf_op jit(solution)/shard_map/sub | solution.py:363
  2.8 5.7 %pick.1 = bf16[1024,256]{1,0:T(8,128)(2,1)} custom-call(s32[1024,1]{1,0:T(8,128)} %sub.48.local, bf16[112,4096]{1,0:T(8,128)(2,1)} %frames.1, f32[37,4096]{1,0:T(8,128)} %residual.3), custom_call_target="tpu_custom_call" | custom-call | tf_op jit(solution)/shard_map/pick/pallas_call | solution.py:158
  8.5 18.2 %all_to_all.15.held = bf16[16,64,256]{2,1,0:T(8,128)(2,1)} all-to-all(bf16[16,64,256]{2,1,0:T(8,128)(2,1)} %bitcast.14), channel_id=1, replica_groups={{0,16,32,48,64,80,96,112,128,144,160,176,192,208,224,240},{4,20,36,52,6..., dimensions={0} | all-to-all | bytes 1048576 | tf_op jit(solution)/shard_map/all_to_all | solution.py:364
  26.7 0.0 copy-start.3
  26.7 1.9 %add.17 = bf16[8,64,256]{2,1,0:T(8,128)(2,1)} custom-call(bf16[16,64,256]{2,1,0:T(8,128)(2,1)} %all_to_all.15.held), custom_call_target="tpu_custom_call" | custom-call | tf_op jit(solution)/shard_map/add/pallas_call | solution.py:184
  28.6 8.2 %all-to-all-start.1 = ((bf16[8,64,256]{2,1,0:T(8,128)(2,1)}), bf16[8,64,256]{2,1,0:T(8,128)(2,1)S(1)}, u32[]{:S(2)}, u32[]{:S(2)}) async-start(bf16[8,64,256]{2,1,0:T(8,128)(2,1)} %add.17), calls=%async_computation.1 | async-start | bytes 524288 | tf_op jit(solution)/shard_map/all_to_all | solution.py:365
  36.8 0.6 pad_add_fusion.place
  37.4 0.0 copy-done.3
  37.4 0.8 constant_dynamic-slice_fusion
  38.2 8.0 %all-to-all-done.1.held = bf16[8,64,256]{2,1,0:T(8,128)(2,1)S(1)} async-done(((bf16[8,64,256]{2,1,0:T(8,128)(2,1)}), bf16[8,64,256]{2,1,0:T(8,128)(2,1)S(1)}, u32[]{:S(2)}, u32[]{:S(2)}) %all-to-all-start.1) | async-done | bytes 262176 | tf_op jit(solution)/shard_map/all_to_all | solution.py:365
  46.3 0.0 copy-start.4
  46.3 0.7 copy-done.4
  47.0 2.0 %mix.1 = bf16[16,64,384]{2,1,0:T(8,128)(2,1)} custom-call(s32[2]{0:T(128)} %pad_add_fusion.place, bf16[8,64,256]{2,1,0:T(8,128)(2,1)} %copy-done.4), custom_call_target="tpu_custom_call" | custom-call | tf_op jit(solution)/shard_map/mix/pallas_call | solution.py:207
  48.9 14.6 %all_to_all.16.near = bf16[16,64,384]{2,1,0:T(8,128)(2,1)S(1)} all-to-all(bf16[16,64,384]{2,1,0:T(8,128)(2,1)} %mix.1), channel_id=1, replica_groups={{0,16,32,48,64,80,96,112,128,144,160,176,192,208,224,240},{4,20,36,52,6..., dimensions={0} | all-to-all | bytes 1572864 | tf_op jit(solution)/shard_map/all_to_all | solution.py:368
  63.5 4.3 %collective-permute-start.3 = (bf16[16,64,384]{2,1,0:T(8,128)(2,1)S(1)}, bf16[16,64,384]{2,1,0:T(8,128)(2,1)S(1)}, u32[]{:S(2)}, u32[]{:S(2)}) collective-permute-start(bf16[16,64,384]{2,1,0:T(8,128)(2,1)S(1)} %all_to_all.16.near), channel_id=1, source_target_pairs={{0,1},{1,0},{2,3},{3,2},{4,5},{5,4},{6,7},{7,6},{8,9},{9,8},{10,11... | collective-permute-start | bytes 2359304 | tf_op jit(solution)/shard_map/ppermute | solution.py:38
  67.8 0.0 collective-permute-start.1
  67.8 1.1 collective-permute-start.2
  68.9 4.7 %collective-permute-start = (bf16[112,2048]{1,0:T(8,128)(2,1)S(1)}, bf16[112,2048]{1,0:T(8,128)(2,1)}, u32[]{:S(2)}, u32[]{:S(2)}) collective-permute-start(bf16[112,2048]{1,0:T(8,128)(2,1)S(1)} %get-tuple-element.9.s0), channel_id=1, source_target_pairs={{0,2},{1,3},{2,0},{3,1},{4,6},{5,7},{6,4},{7,5},{8,10},{9,11},{10,... | collective-permute-start | bytes 1376264 | tf_op jit(solution)/shard_map/ppermute | solution.py:38
  73.6 0.1 copy.9.point_col
  73.7 0.2 copy.12
  74.0 0.0 collective-permute-done.3.far
  74.0 26.0 %solve.1 = (bf16[256,1024]{1,0:T(8,128)(2,1)S(1)}, f32[1024,1]{1,0:T(8,128)S(1)}) custom-call(bf16[16,64,384]{2,1,0:T(8,128)(2,1)S(1)} %all_to_all.16.near, bf16[16,64,384]{2,1,0:T(8,128)(2,1)S(1)} %collective-permute-done.3.far, s32[1,512]{1,0:T(1,128)S(1)} %get-tuple-element.21.point_row, s32[512,1]{1,0:T(8,128)S(1)} %copy.9.point_col), custom_call_target="tpu_custom_call" | custom-call | flops 1048576 | bytes 1048576 | tf_op jit(solution)/shard_map/solve/pallas_call | solution.py:269
  100.0 0.0 collective-permute-done.1.s2
  100.0 0.0 collective-permute-done.2.s3
  100.0 14.7 %collective-permute-done.s1 = bf16[112,2048]{1,0:T(8,128)(2,1)} collective-permute-done((bf16[112,2048]{1,0:T(8,128)(2,1)S(1)}, bf16[112,2048]{1,0:T(8,128)(2,1)}, u32[]{:S(2)}, u32[]{:S(2)}) %collective-permute-start) | collective-permute-done | bytes 458784 | tf_op jit(solution)/shard_map/ppermute | solution.py:38
  114.7 0.0 copy-start
  114.7 0.0 copy-start.1
  114.7 11.4 %update.1 = (f32[2,40,2048]{2,1,0:T(8,128)S(1)}, f32[2,40,2048]{2,1,0:T(8,128)S(1)}) custom-call(bf16[112,2048]{1,0:T(8,128)(2,1)S(1)} %get-tuple-element.9.s0, bf16[112,2048]{1,0:T(8,128)(2,1)} %collective-permute-done.s1, bf16[112,2048]{1,0:T(8,128)(2,1)S(1)} %collective-permute-done.1.s2, bf16[112,2048]{1,0:T(8,128)(2,1)} %collective-permute-done.2.s3, ...), custom_call_target="tpu_custom_call" | custom-call | tf_op jit(solution)/shard_map/update/pallas_call | solution.py:321
  126.1 0.0 copy-start.2
  126.1 0.7 collective-permute-start.4
  126.8 1.7 %collective-permute-done.4.got = f32[2,40,2048]{2,1,0:T(8,128)S(1)} collective-permute-done((f32[2,40,2048]{2,1,0:T(8,128)S(1)}, f32[2,40,2048]{2,1,0:T(8,128)S(1)}, u32[]{:S(2)}, u32[]{:S(2)}) %collective-permute-start.4) | collective-permute-done | bytes 655392 | tf_op jit(solution)/shard_map/ppermute | solution.py:38
  128.6 0.0 copy-done
  128.6 0.0 copy-done.1
  128.6 0.0 copy-done.2
  128.6 1.8 %finish.1 = (f32[37,4096]{1,0:T(8,128)}, f32[37,4096]{1,0:T(8,128)}) custom-call(s32[2]{0:T(128)S(1)} %copy-done.2, f32[37,4096]{1,0:T(8,128)S(1)} %copy-done, f32[37,4096]{1,0:T(8,128)S(1)} %copy-done.1, f32[2,40,2048]{2,1,0:T(8,128)S(1)} %get-tuple-element.14.mine, f32[2,40,2048]{2,1,0:T(8,128)S(1)} %collective-permute-done.4.got), custom_call_target="tpu_custom_call" | custom-call | tf_op jit(solution)/shard_map/finish/pallas_call | solution.py:342
  (4 shorter events, 0.0 us)
Async XLA Ops:
  0.6 0.7 copy-start.5
  26.7 10.7 %copy-start.3 = (bf16[112,4096]{1,0:T(8,128)(2,1)S(1)}, bf16[112,4096]{1,0:T(8,128)(2,1)}, u32[]{:S(2)}) copy-start(bf16[112,4096]{1,0:T(8,128)(2,1)} %frames.1) | copy-start | bytes 2752516
  28.6 17.7 %all-to-all-start.1 = ((bf16[8,64,256]{2,1,0:T(8,128)(2,1)}), bf16[8,64,256]{2,1,0:T(8,128)(2,1)S(1)}, u32[]{:S(2)}, u32[]{:S(2)}) async-start(bf16[8,64,256]{2,1,0:T(8,128)(2,1)} %add.17), calls=%async_computation.1 | async-start | bytes 524288 | tf_op jit(solution)/shard_map/all_to_all | solution.py:365
  46.3 0.7 copy-start.4
  63.5 10.4 %collective-permute-start.3 = (bf16[16,64,384]{2,1,0:T(8,128)(2,1)S(1)}, bf16[16,64,384]{2,1,0:T(8,128)(2,1)S(1)}, u32[]{:S(2)}, u32[]{:S(2)}) collective-permute-start(bf16[16,64,384]{2,1,0:T(8,128)(2,1)S(1)} %all_to_all.16.near), channel_id=1, source_target_pairs={{0,1},{1,0},{2,3},{3,2},{4,5},{5,4},{6,7},{7,6},{8,9},{9,8},{10,11... | collective-permute-start | bytes 2359304 | tf_op jit(solution)/shard_map/ppermute | solution.py:38
  67.8 32.2 %collective-permute-start.1 = (bf16[112,2048]{1,0:T(8,128)(2,1)}, bf16[112,2048]{1,0:T(8,128)(2,1)S(1)}, u32[]{:S(2)}, u32[]{:S(2)}) collective-permute-start(bf16[112,2048]{1,0:T(8,128)(2,1)} %get-tuple-element.10), channel_id=1, source_target_pairs={{0,1},{1,0},{2,3},{3,2},{4,5},{5,4},{6,7},{7,6},{8,9},{9,8},{10,11... | collective-permute-start | bytes 1376264 | tf_op jit(solution)/shard_map/ppermute | solution.py:38
  67.8 32.2 %collective-permute-start.2 = (bf16[112,2048]{1,0:T(8,128)(2,1)}, bf16[112,2048]{1,0:T(8,128)(2,1)}, u32[]{:S(2)}, u32[]{:S(2)}) collective-permute-start(bf16[112,2048]{1,0:T(8,128)(2,1)} %get-tuple-element.10), channel_id=1, source_target_pairs={{0,3},{1,2},{2,1},{3,0},{4,7},{5,6},{6,5},{7,4},{8,11},{9,10},{10,... | collective-permute-start | bytes 1376264 | tf_op jit(solution)/shard_map/ppermute | solution.py:38
  68.9 45.8 %collective-permute-start = (bf16[112,2048]{1,0:T(8,128)(2,1)S(1)}, bf16[112,2048]{1,0:T(8,128)(2,1)}, u32[]{:S(2)}, u32[]{:S(2)}) collective-permute-start(bf16[112,2048]{1,0:T(8,128)(2,1)S(1)} %get-tuple-element.9.s0), channel_id=1, source_target_pairs={{0,2},{1,3},{2,0},{3,1},{4,6},{5,7},{6,4},{7,5},{8,10},{9,11},{10,... | collective-permute-start | bytes 1376264 | tf_op jit(solution)/shard_map/ppermute | solution.py:38
  114.7 13.8 %copy-start = (f32[37,4096]{1,0:T(8,128)S(1)}, f32[37,4096]{1,0:T(8,128)}, u32[]{:S(2)}) copy-start(f32[37,4096]{1,0:T(8,128)} %residual.3) | copy-start | bytes 1818628
  114.7 13.8 %copy-start.1 = (f32[37,4096]{1,0:T(8,128)S(1)}, f32[37,4096]{1,0:T(8,128)}, u32[]{:S(2)}) copy-start(f32[37,4096]{1,0:T(8,128)} %coefficients.1) | copy-start | bytes 1818628
  126.1 2.5 %copy-start.2 = (s32[2]{0:T(128)S(1)}, s32[2]{0:T(128)}, u32[]{:S(2)}) copy-start(s32[2]{0:T(128)} %pad_add_fusion.place) | copy-start | bytes 28
  126.1 2.4 %collective-permute-start.4 = (f32[2,40,2048]{2,1,0:T(8,128)S(1)}, f32[2,40,2048]{2,1,0:T(8,128)S(1)}, u32[]{:S(2)}, u32[]{:S(2)}) collective-permute-start(f32[2,40,2048]{2,1,0:T(8,128)S(1)} %get-tuple-element.15), channel_id=1, source_target_pairs={{0,1},{1,0},{2,3},{3,2},{4,5},{5,4},{6,7},{7,6},{8,9},{9,8},{10,11... | collective-permute-start | bytes 1966088 | tf_op jit(solution)/shard_map/ppermute | solution.py:38

commit v2 on v1

--- a/solution.py
+++ b/solution.py
@@ -17,7 +17,7 @@
 F32 = jnp.float32
 ROWS = 37
 PANEL = 16
-TILE = 512
+TILE = 1024
 PICK = 1024
 SCALE = WIDTH_SCALE / D * math.log2(math.e)
 
@@ -288,21 +288,21 @@
         value = ref[...].astype(F32)
         return jnp.sum(value * value, axis=0, keepdims=True)
 
-    source_sq = squares(s0) + squares(s1) + squares(s2) + squares(s3)
+    source_sq = SCALE * (squares(s0) + squares(s1) + squares(s2) + squares(s3))
     pad = jnp.zeros((32, TILE), BF16)
     source_near = jnp.concatenate([s0[...], s1[...], pad], axis=0)
     source_far = jnp.concatenate([s2[...], s3[...], pad], axis=0)
     positions = pl.program_id(0) * TILE + lax.broadcasted_iota(jnp.int32, (1, TILE), 1)
     change = jnp.zeros((256, TILE), F32)
     placed = jnp.zeros((256, TILE), F32)
-    size = 256
+    size = 512
     for c in range(STEPS * BLOCK // size):
         at = slice(size * c, size * c + size)
         s, first = (size * c) // BLOCK, (size * c) % BLOCK // 32
         block = slice(first, first + size // 32), slice(32 * s, 32 * s + 32), slice(0, 256)
         products = jnp.dot(near[block].reshape(size, 256), source_near, preferred_element_type=F32)
         products = products + jnp.dot(far[block].reshape(size, 256), source_far, preferred_element_type=F32)
-        kern = jnp.exp2(-SCALE * (sq[at] + source_sq - 2.0 * products))
+        kern = jnp.exp2((2.0 * SCALE) * products - (SCALE * sq[at] + source_sq))
         here = jnp.where(local[at] == positions, 1.0, 0.0).astype(BF16)
         weights = delta[:, at]
         for part in split3(kern):
@@ -362,10 +362,13 @@
     points = block_index.reshape(STEPS, 16, 32).transpose(1, 0, 2).reshape(-1, 1)
     held = pick(points - dp * rows, frames, residual).reshape(16, 64, 256)
     held = add(lax.all_to_all(held, "dp", 0, 0, axis_index_groups=PLANE, tiled=True))
+    held, beside = lax.optimization_barrier((held, beside))
     held = lax.all_to_all(held, AXES, 0, 0, axis_index_groups=LINE, tiled=True)
     held, own_half, other_half = lax.optimization_barrier((held, own_half, other_half))
-    across, diagonal = swap(own_half, 1, 0), swap(other_half, 1, 1)
+    across = swap(own_half, 1, 0)
     near = lax.all_to_all(mix(place, held), "dp", 0, 0, axis_index_groups=PLANE, tiled=True)
+    near, across, other_half = lax.optimization_barrier((near, across, other_half))
+    diagonal = swap(other_half, 1, 1)
     far = swap(near, 0, 1)
 
     delta, sq = solve(near, far, block_index)

time: 131 us -> 123 us (0.939)
  blocking collectives: 32.8 us -> 0 us
  waiting for transfers between devices: 24.4 us -> 42.1 us
  starting transfers between devices: 18.9 us -> 26.5 us
  Pallas kernels: 48.8 us -> 46.4 us
  local copies, waits for them, and re-layouts: 4.04 us -> 5.64 us
    all_to_all x2 -> x0, blocking collectives: 32.8 us -> none  [the longest x1 18.2 us: on_device(): lax.all_to_all(held, 'dp', 0, 0, axis_index_groups=PLANE, tiled=True)]
    all_to_all x0 -> x2, starting transfers between devices: none -> 11.3 us  [the longest x1 7.71 us: on_device(): lax.all_to_all(held, 'dp', 0, 0, axis_index_groups=PLANE, tiled=True)]
    all_to_all x0 -> x2, waiting for transfers between devices: none -> 8.65 us  [the longest x1 8.65 us: on_device(): lax.all_to_all(held, 'dp', 0, 0, axis_index_groups=PLANE, tiled=True)]
    ppermute x5, waiting for transfers between devices: 16.4 us -> 24.6 us  [swap(): return lax.ppermute(value, AXES, permutation(move))]
    ppermute x5, starting transfers between devices: 10.8 us -> 6.99 us  [swap(): return lax.ppermute(value, AXES, permutation(move))]
    pallas_call x1, Pallas kernels: 11.4 us -> 9.06 us  [update(): pl.pallas_call(update_kernel, grid=(rows // TILE,), in_specs=[pl.BlockSpe...]
    unnamed x14 -> x20, local copies, waits for them, and re-layouts: 1.62 us -> 3.19 us
  transfers between devices with their start and end apart: 6 -> 8, of which waited for: 3 -> 5; matrix products, arithmetic and copies ran while one was open for 1% -> 2% of each run, Pallas kernels for 20% -> 23%
where the time goes in v2:
time: 123 us; the launch traced here: 122 us
  Pallas kernels  46.4 us (38%)
  waiting for transfers between devices  42.1 us (34%)
  starting transfers between devices  26.5 us (22%)
  local copies, waits for them, and re-layouts  5.64 us (5%)
    pallas_call x1, Pallas kernels, solve(): pl.pallas_call(solve_kernel, out_shape=(jax.ShapeDtypeStruct((256, STEPS...  26 us
    ppermute x5, waiting for transfers between devices, swap(): return lax.ppermute(value, AXES, permutation(move))  24.6 us
    pallas_call x1, Pallas kernels, update(): pl.pallas_call(update_kernel, grid=(rows // TILE,), in_specs=[pl.BlockSpe...  9.06 us
    all_to_all x1, waiting for transfers between devices, on_device(): held = lax.all_to_all(held, AXES, 0, 0, axis_index_groups=LINE, tiled=True)  8.82 us
    all_to_all x1, waiting for transfers between devices, on_device(): lax.all_to_all(held, 'dp', 0, 0, axis_index_groups=PLANE, tiled=True)  8.65 us
    all_to_all x1, starting transfers between devices, on_device(): held = lax.all_to_all(held, AXES, 0, 0, axis_index_groups=LINE, tiled=True)  8.18 us
    all_to_all x1, starting transfers between devices, on_device(): lax.all_to_all(held, 'dp', 0, 0, axis_index_groups=PLANE, tiled=True)  7.71 us
    ppermute x5, starting transfers between devices, swap(): return lax.ppermute(value, AXES, permutation(move))  6.99 us
  transfers between devices with their start and end apart: 8, of which 5 were waited for; matrix products, arithmetic and copies ran while one was open for 2% of the time, Pallas kernels for 23%

profile of v2, /device:TPU:1, one launch (start us, length us, event | category | flops | bytes accessed | tf_op | source)
XLA Modules:
  0.0 122.0 jit_solution(5391961370516894862)
XLA Ops:
  0.6 0.0 copy-start.8
  0.7 0.7 copy-done.8
  1.3 0.1 sub.41
  1.4 1.3 %sub.48.local = s32[1024,1]{1,0:T(8,128)} reshape(s32[16,2,32]{2,1,0:T(2,128)S(1)} %bitcast.15) | data formatting | bytes 8192 | tf_op jit(solution)/shard_map/sub | solution.py:363
  2.8 5.7 %pick.1 = bf16[1024,256]{1,0:T(8,128)(2,1)} custom-call(s32[1024,1]{1,0:T(8,128)} %sub.48.local, bf16[112,4096]{1,0:T(8,128)(2,1)} %frames.1, f32[37,4096]{1,0:T(8,128)} %residual.3), custom_call_target="tpu_custom_call" | custom-call | tf_op jit(solution)/shard_map/pick/pallas_call | solution.py:158
  8.5 0.0 copy-start.5
  8.5 7.7 %all-to-all-start = ((bf16[16,64,256]{2,1,0:T(8,128)(2,1)}), bf16[16,64,256]{2,1,0:T(8,128)(2,1)S(1)}, u32[]{:S(2)}, u32[]{:S(2)}) async-start(bf16[16,64,256]{2,1,0:T(8,128)(2,1)} %bitcast.14), calls=%async_computation | async-start | bytes 1048576 | tf_op jit(solution)/shard_map/all_to_all | solution.py:364
  16.2 0.0 copy-done.5
  16.2 0.9 constant_dynamic-slice_fusion
  17.1 1.0 collective-permute-start
  18.1 8.6 %all-to-all-done.held = bf16[16,64,256]{2,1,0:T(8,128)(2,1)S(1)} async-done(((bf16[16,64,256]{2,1,0:T(8,128)(2,1)}), bf16[16,64,256]{2,1,0:T(8,128)(2,1)S(1)}, u32[]{:S(2)}, u32[]{:S(2)}) %all-to-all-start) | async-done | bytes 524320 | tf_op jit(solution)/shard_map/all_to_all | solution.py:364
  26.7 0.0 copy-start.6
  26.7 0.8 copy-done.6
  27.5 1.8 %add.17 = bf16[8,64,256]{2,1,0:T(8,128)(2,1)} custom-call(bf16[16,64,256]{2,1,0:T(8,128)(2,1)} %copy-done.6), custom_call_target="tpu_custom_call" | custom-call | tf_op jit(solution)/shard_map/add/pallas_call | solution.py:184
  29.3 0.0 collective-permute-done.s2
  29.3 8.2 %all-to-all-start.1 = ((bf16[8,64,256]{2,1,0:T(8,128)(2,1)}), bf16[8,64,256]{2,1,0:T(8,128)(2,1)S(1)}, u32[]{:S(2)}, u32[]{:S(2)}) async-start(bf16[8,64,256]{2,1,0:T(8,128)(2,1)} %add.17), calls=%async_computation.1 | async-start | bytes 524288 | tf_op jit(solution)/shard_map/all_to_all | solution.py:366
  37.5 0.7 pad_add_fusion.place
  38.2 8.8 %all-to-all-done.1.held = bf16[8,64,256]{2,1,0:T(8,128)(2,1)S(1)} async-done(((bf16[8,64,256]{2,1,0:T(8,128)(2,1)}), bf16[8,64,256]{2,1,0:T(8,128)(2,1)S(1)}, u32[]{:S(2)}, u32[]{:S(2)}) %all-to-all-start.1) | async-done | bytes 262176 | tf_op jit(solution)/shard_map/all_to_all | solution.py:366
  47.0 0.0 copy-start.7
  47.0 0.7 copy-done.7
  47.7 2.0 %mix.1 = bf16[16,64,384]{2,1,0:T(8,128)(2,1)} custom-call(s32[2]{0:T(128)} %pad_add_fusion.place, bf16[8,64,256]{2,1,0:T(8,128)(2,1)} %copy-done.7), custom_call_target="tpu_custom_call" | custom-call | tf_op jit(solution)/shard_map/mix/pallas_call | solution.py:207
  49.7 3.6 %all-to-all-start.2 = ((bf16[16,64,384]{2,1,0:T(8,128)(2,1)}), bf16[16,64,384]{2,1,0:T(8,128)(2,1)S(1)}, u32[]{:S(2)}, u32[]{:S(2)}) async-start(bf16[16,64,384]{2,1,0:T(8,128)(2,1)} %mix.1), calls=%async_computation.2 | async-start | bytes 1572864 | tf_op jit(solution)/shard_map/all_to_all | solution.py:369
  53.3 0.8 collective-permute-start.1
  54.1 21.9 %collective-permute-done.1.s1 = bf16[112,2048]{1,0:T(8,128)(2,1)S(1)} collective-permute-done((bf16[112,2048]{1,0:T(8,128)(2,1)S(1)}, bf16[112,2048]{1,0:T(8,128)(2,1)S(1)}, u32[]{:S(2)}, u32[]{:S(2)}) %collective-permute-start.1) | collective-permute-done | bytes 458784 | tf_op jit(solution)/shard_map/ppermute | solution.py:38
  76.0 0.0 copy-start.2
  76.0 0.8 copy-done.2
  76.8 0.0 all-to-all-done.2.near
  76.8 4.2 %collective-permute-start.3 = (bf16[16,64,384]{2,1,0:T(8,128)(2,1)S(1)}, bf16[16,64,384]{2,1,0:T(8,128)(2,1)S(1)}, u32[]{:S(2)}, u32[]{:S(2)}) collective-permute-start(bf16[16,64,384]{2,1,0:T(8,128)(2,1)S(1)} %all-to-all-done.2.near), channel_id=1, source_target_pairs={{0,1},{1,0},{2,3},{3,2},{4,5},{5,4},{6,7},{7,6},{8,9},{9,8},{10,11... | collective-permute-start | bytes 2359304 | tf_op jit(solution)/shard_map/ppermute | solution.py:38
  81.0 0.5 collective-permute-start.2
  81.6 0.1 copy.9.point_col
  81.7 0.2 copy.12
  81.9 1.0 collective-permute-done.3.far
  82.9 0.0 copy-start.3
  82.9 26.0 %solve.1 = (bf16[256,1024]{1,0:T(8,128)(2,1)S(1)}, f32[1024,1]{1,0:T(8,128)S(1)}) custom-call(bf16[16,64,384]{2,1,0:T(8,128)(2,1)S(1)} %all-to-all-done.2.near, bf16[16,64,384]{2,1,0:T(8,128)(2,1)S(1)} %collective-permute-done.3.far, s32[1,512]{1,0:T(1,128)S(1)} %get-tuple-element.31.point_row, s32[512,1]{1,0:T(8,128)S(1)} %copy.9.point_col), custom_call_target="tpu_custom_call" | custom-call | flops 1048576 | bytes 1048576 | tf_op jit(solution)/shard_map/solve/pallas_call | solution.py:269
  108.9 0.0 collective-permute-done.2.s3
  109.0 0.0 copy-done.3
  109.0 0.0 copy-start
  109.0 0.0 copy-start.1
  109.0 9.1 %update.1 = (f32[2,40,2048]{2,1,0:T(8,128)S(1)}, f32[2,40,2048]{2,1,0:T(8,128)S(1)}) custom-call(bf16[112,2048]{1,0:T(8,128)(2,1)S(1)} %get-tuple-element.15.s0, bf16[112,2048]{1,0:T(8,128)(2,1)S(1)} %copy-done.3, bf16[112,2048]{1,0:T(8,128)(2,1)S(1)} %collective-permute-done.s2, bf16[112,2048]{1,0:T(8,128)(2,1)} %collective-permute-done.2.s3, ...), custom_call_target="tpu_custom_call" | custom-call | tf_op jit(solution)/shard_map/update/pallas_call | solution.py:321
  118.1 0.0 copy-start.4
  118.1 0.5 collective-permute-start.4
  118.5 1.7 %collective-permute-done.4.got = f32[2,40,2048]{2,1,0:T(8,128)S(1)} collective-permute-done((f32[2,40,2048]{2,1,0:T(8,128)S(1)}, f32[2,40,2048]{2,1,0:T(8,128)S(1)}, u32[]{:S(2)}, u32[]{:S(2)}) %collective-permute-start.4) | collective-permute-done | bytes 655392 | tf_op jit(solution)/shard_map/ppermute | solution.py:38
  120.3 0.0 copy-done
  120.3 0.0 copy-done.1
  120.3 0.0 copy-done.4
  120.3 1.8 %finish.1 = (f32[37,4096]{1,0:T(8,128)}, f32[37,4096]{1,0:T(8,128)}) custom-call(s32[2]{0:T(128)S(1)} %copy-done.4, f32[37,4096]{1,0:T(8,128)S(1)} %copy-done, f32[37,4096]{1,0:T(8,128)S(1)} %copy-done.1, f32[2,40,2048]{2,1,0:T(8,128)S(1)} %get-tuple-element.24.mine, f32[2,40,2048]{2,1,0:T(8,128)S(1)} %collective-permute-done.4.got), custom_call_target="tpu_custom_call" | custom-call | tf_op jit(solution)/shard_map/finish/pallas_call | solution.py:342
  (4 shorter events, 0.0 us)
Async XLA Ops:
  0.6 0.7 copy-start.8
  8.5 7.7 %copy-start.5 = (bf16[112,4096]{1,0:T(8,128)(2,1)S(1)}, bf16[112,4096]{1,0:T(8,128)(2,1)}, u32[]{:S(2)}) copy-start(bf16[112,4096]{1,0:T(8,128)(2,1)} %frames.1) | copy-start | bytes 2752516
  8.5 18.2 %all-to-all-start = ((bf16[16,64,256]{2,1,0:T(8,128)(2,1)}), bf16[16,64,256]{2,1,0:T(8,128)(2,1)S(1)}, u32[]{:S(2)}, u32[]{:S(2)}) async-start(bf16[16,64,256]{2,1,0:T(8,128)(2,1)} %bitcast.14), calls=%async_computation | async-start | bytes 1048576 | tf_op jit(solution)/shard_map/all_to_all | solution.py:364
  17.1 12.2 %collective-permute-start = (bf16[112,2048]{1,0:T(8,128)(2,1)}, bf16[112,2048]{1,0:T(8,128)(2,1)S(1)}, u32[]{:S(2)}, u32[]{:S(2)}) collective-permute-start(bf16[112,2048]{1,0:T(8,128)(2,1)} %get-tuple-element.20), channel_id=1, source_target_pairs={{0,1},{1,0},{2,3},{3,2},{4,5},{5,4},{6,7},{7,6},{8,9},{9,8},{10,11... | collective-permute-start | bytes 1376264 | tf_op jit(solution)/shard_map/ppermute | solution.py:38
  26.7 0.8 copy-start.6
  29.3 17.7 %all-to-all-start.1 = ((bf16[8,64,256]{2,1,0:T(8,128)(2,1)}), bf16[8,64,256]{2,1,0:T(8,128)(2,1)S(1)}, u32[]{:S(2)}, u32[]{:S(2)}) async-start(bf16[8,64,256]{2,1,0:T(8,128)(2,1)} %add.17), calls=%async_computation.1 | async-start | bytes 524288 | tf_op jit(solution)/shard_map/all_to_all | solution.py:366
  47.0 0.7 copy-start.7
  49.7 27.1 %all-to-all-start.2 = ((bf16[16,64,384]{2,1,0:T(8,128)(2,1)}), bf16[16,64,384]{2,1,0:T(8,128)(2,1)S(1)}, u32[]{:S(2)}, u32[]{:S(2)}) async-start(bf16[16,64,384]{2,1,0:T(8,128)(2,1)} %mix.1), calls=%async_computation.2 | async-start | bytes 1572864 | tf_op jit(solution)/shard_map/all_to_all | solution.py:369
  53.3 22.7 %collective-permute-start.1 = (bf16[112,2048]{1,0:T(8,128)(2,1)S(1)}, bf16[112,2048]{1,0:T(8,128)(2,1)S(1)}, u32[]{:S(2)}, u32[]{:S(2)}) collective-permute-start(bf16[112,2048]{1,0:T(8,128)(2,1)S(1)} %get-tuple-element.15.s0), channel_id=1, source_target_pairs={{0,2},{1,3},{2,0},{3,1},{4,6},{5,7},{6,4},{7,5},{8,10},{9,11},{10,... | collective-permute-start | bytes 1376264 | tf_op jit(solution)/shard_map/ppermute | solution.py:38
  76.0 0.8 copy-start.2
  76.8 6.1 %collective-permute-start.3 = (bf16[16,64,384]{2,1,0:T(8,128)(2,1)S(1)}, bf16[16,64,384]{2,1,0:T(8,128)(2,1)S(1)}, u32[]{:S(2)}, u32[]{:S(2)}) collective-permute-start(bf16[16,64,384]{2,1,0:T(8,128)(2,1)S(1)} %all-to-all-done.2.near), channel_id=1, source_target_pairs={{0,1},{1,0},{2,3},{3,2},{4,5},{5,4},{6,7},{7,6},{8,9},{9,8},{10,11... | collective-permute-start | bytes 2359304 | tf_op jit(solution)/shard_map/ppermute | solution.py:38
  81.0 27.9 %collective-permute-start.2 = (bf16[112,2048]{1,0:T(8,128)(2,1)}, bf16[112,2048]{1,0:T(8,128)(2,1)}, u32[]{:S(2)}, u32[]{:S(2)}) collective-permute-start(bf16[112,2048]{1,0:T(8,128)(2,1)} %get-tuple-element.20), channel_id=1, source_target_pairs={{0,3},{1,2},{2,1},{3,0},{4,7},{5,6},{6,5},{7,4},{8,11},{9,10},{10,... | collective-permute-start | bytes 1376264 | tf_op jit(solution)/shard_map/ppermute | solution.py:38
  82.9 26.0 %copy-start.3 = (bf16[112,2048]{1,0:T(8,128)(2,1)S(1)}, bf16[112,2048]{1,0:T(8,128)(2,1)}, u32[]{:S(2)}) copy-start(bf16[112,2048]{1,0:T(8,128)(2,1)} %copy-done.2) | copy-start | bytes 1376260
  109.0 11.3 %copy-start = (f32[37,4096]{1,0:T(8,128)S(1)}, f32[37,4096]{1,0:T(8,128)}, u32[]{:S(2)}) copy-start(f32[37,4096]{1,0:T(8,128)} %residual.3) | copy-start | bytes 1818628
  109.0 11.3 %copy-start.1 = (f32[37,4096]{1,0:T(8,128)S(1)}, f32[37,4096]{1,0:T(8,128)}, u32[]{:S(2)}) copy-start(f32[37,4096]{1,0:T(8,128)} %coefficients.1) | copy-start | bytes 1818628
  118.1 2.2 %copy-start.4 = (s32[2]{0:T(128)S(1)}, s32[2]{0:T(128)}, u32[]{:S(2)}) copy-start(s32[2]{0:T(128)} %pad_add_fusion.place) | copy-start | bytes 28
  118.1 2.2 %collective-permute-start.4 = (f32[2,40,2048]{2,1,0:T(8,128)S(1)}, f32[2,40,2048]{2,1,0:T(8,128)S(1)}, u32[]{:S(2)}, u32[]{:S(2)}) collective-permute-start(f32[2,40,2048]{2,1,0:T(8,128)S(1)} %get-tuple-element.25), channel_id=1, source_target_pairs={{0,1},{1,0},{2,3},{3,2},{4,5},{5,4},{6,7},{7,6},{8,9},{9,8},{10,11... | collective-permute-start | bytes 1966088 | tf_op jit(solution)/shard_map/ppermute | solution.py:38

commit v3 on v2

--- a/solution.py
+++ b/solution.py
@@ -77,20 +77,27 @@
     def exchange(one, two):
         return jnp.where(lower, one, pltpu.roll(two, 64, 1)), jnp.where(lower, pltpu.roll(one, 64, 1), two)
 
+    def spread(value, first):
+        pairs = [[jnp.broadcast_to(value[:, i : i + 1], (PANEL, 128)) for i in (j, 64 + j)] for j in range(first, first + PANEL)]
+        return [jnp.where(lower, *pair) for pair in pairs]
+
     for k in range(4):
         r0 = 128 * k
         block = slice(r0, r0 + 128)
         packed[0], packed[1] = exchange(mats[0, block, block], mats[1, block, block])
+        ahead = [packed[0, :PANEL], packed[1, :PANEL]]
         for p in range(128 // PANEL):
             b = PANEL * p
             half, first = b // 64, b % 64
-            rows = slice(b, b + PANEL)
-            new = [packed[0, rows], packed[1, rows]]
+            rows, after = slice(b, b + PANEL), slice(b + PANEL, b + 2 * PANEL)
+            inside = ((lane & 63) >= first) & ((lane & 63) < first + PANEL)
+            new = ahead
             old = exchange(*new)
-            cols = []
-            for j in range(first, first + PANEL):
-                pair = [jnp.broadcast_to(new[half][:, i : i + 1], (PANEL, 128)) for i in (j, 64 + j)]
-                cols.append(jnp.where(lower, *pair))
+            cols = spread(new[half], first)
+            if b + PANEL < 128:
+                ahead = [packed[0, after], packed[1, after]]
+                left = spread(ahead[half], first)
+                ahead[half] = jnp.where(inside, 0.0, ahead[half])
             for j in range(PANEL):
                 one = jnp.where(row == j, 1.0, 0.0)
                 factor = (cols[j] - one) * (1.0 / cols[j][j : j + 1])
@@ -98,6 +105,9 @@
                     cols[q] = cols[q] - factor * cols[q][j : j + 1]
                 new[half] = jnp.where((lane & 63) == first + j, one, new[half])
                 new = [value - factor * value[j : j + 1] for value in new]
+            if b + PANEL < 128:
+                for j in range(PANEL):
+                    ahead = [value - left[j] * add[j : j + 1] for value, add in zip(ahead, new)]
             sign = jnp.where(lane < b, -1.0, jnp.where(lane < b + PANEL, 0.0, 1.0))
             nh, nm, nl = split3(jnp.concatenate(new, axis=1))
             rhs = jnp.concatenate([nh, nm, nh, nl, nh, nm], axis=0)
@@ -110,9 +120,11 @@
                 at = slice(128 * i, 128 * i + 128)
                 held = packed[i]
                 if i == half:
-                    held = jnp.where(((lane & 63) >= first) & ((lane & 63) < first + PANEL), 0.0, held)
+                    held = jnp.where(inside, 0.0, held)
                 packed[i] = held - jnp.where(lower, outs[0][:, at], outs[1][:, at])
                 packed[i, rows] = new[i]
+                if b + PANEL < 128:
+                    packed[i, after] = ahead[i]
         mats[0, block, block], mats[1, block, block] = exchange(packed[0], packed[1])
         others = [slice(128 * i, 128 * i + 128) for i in ((k + 1) % 4, (k + 2) % 4, (k + 3) % 4)]
         for s in range(2):
@@ -283,14 +295,16 @@
     )(near, far, chosen[1].reshape(1, BLOCK), chosen[0].reshape(BLOCK, 1))
 
 
-def update_kernel(s0, s1, s2, s3, near, far, delta, sq, local, mine_ref, theirs_ref):
+def update_kernel(s0, s2, s3, a0, a1, near, far, delta, sq, local, mine_ref, theirs_ref):
+    s1 = jnp.where(pl.program_id(0) == 0, a0[...], a1[...])
+
     def squares(ref):
         value = ref[...].astype(F32)
         return jnp.sum(value * value, axis=0, keepdims=True)
 
     source_sq = SCALE * (squares(s0) + squares(s1) + squares(s2) + squares(s3))
     pad = jnp.zeros((32, TILE), BF16)
-    source_near = jnp.concatenate([s0[...], s1[...], pad], axis=0)
+    source_near = jnp.concatenate([s0[...], s1, pad], axis=0)
     source_far = jnp.concatenate([s2[...], s3[...], pad], axis=0)
     positions = pl.program_id(0) * TILE + lax.broadcasted_iota(jnp.int32, (1, TILE), 1)
     change = jnp.zeros((256, TILE), F32)
@@ -315,18 +329,18 @@
         out[1] = added
 
 
-def update(sources, near, far, delta, sq, local):
+def update(sources, across, near, far, delta, sq, local):
     whole = pl.BlockSpec(memory_space=pltpu.VMEM)
     rows = sources[0].shape[1]
     return pl.pallas_call(
         update_kernel,
         grid=(rows // TILE,),
-        in_specs=[pl.BlockSpec((112, TILE), lambda i: (0, i))] * 4 + [whole] * 5,
+        in_specs=[pl.BlockSpec((112, TILE), lambda i: (0, i))] * 3 + [whole] * 7,
         out_specs=[pl.BlockSpec((2, 40, TILE), lambda i: (0, 0, i))] * 2,
         out_shape=[jax.ShapeDtypeStruct((2, 40, rows), F32)] * 2,
         compiler_params=pltpu.CompilerParams(vmem_limit_bytes=40 << 20),
         name="update",
-    )(*sources, near, far, delta, sq, local)
+    )(*sources, *across, near, far, delta, sq, local)
 
 
 def finish_kernel(place, residual, coefficients, mine, got, res_out, coef_out):
@@ -358,14 +372,16 @@
     own_half = lax.dynamic_slice_in_dim(frames, c * (rows // 2), rows // 2, axis=1)
     other_half = lax.dynamic_slice_in_dim(frames, (1 - c) * (rows // 2), rows // 2, axis=1)
     beside = swap(other_half, 0, 1)
+    piece = rows // 4
+    across = [swap(own_half[:, :piece], 1, 0)]
 
     points = block_index.reshape(STEPS, 16, 32).transpose(1, 0, 2).reshape(-1, 1)
     held = pick(points - dp * rows, frames, residual).reshape(16, 64, 256)
     held = add(lax.all_to_all(held, "dp", 0, 0, axis_index_groups=PLANE, tiled=True))
-    held, beside = lax.optimization_barrier((held, beside))
+    held, beside, across, own_half, other_half = lax.optimization_barrier((held, beside, across, own_half, other_half))
     held = lax.all_to_all(held, AXES, 0, 0, axis_index_groups=LINE, tiled=True)
     held, own_half, other_half = lax.optimization_barrier((held, own_half, other_half))
-    across = swap(own_half, 1, 0)
+    across.append(swap(own_half[:, piece:], 1, 0))
     near = lax.all_to_all(mix(place, held), "dp", 0, 0, axis_index_groups=PLANE, tiled=True)
     near, across, other_half = lax.optimization_barrier((near, across, other_half))
     diagonal = swap(other_half, 1, 1)
@@ -373,7 +389,7 @@
 
     delta, sq = solve(near, far, block_index)
     local = block_index.reshape(-1, 1) - dp * rows - c * (rows // 2)
-    mine, theirs = update((own_half, across, beside, diagonal), near, far, delta, sq, local)
+    mine, theirs = update((own_half, beside, diagonal), across, near, far, delta, sq, local)
     return finish(place, residual, coefficients, mine, swap(theirs, 0, 1))
 
 

time: 123 us -> 119 us (0.967)
  waiting for transfers between devices: 42.1 us -> 27.1 us
  starting transfers between devices: 26.5 us -> 41.1 us
  Pallas kernels: 46.4 us -> 43.3 us
    ppermute x5 -> x6, starting transfers between devices: 6.99 us -> 16.6 us  [swap(): return lax.ppermute(value, AXES, permutation(move))]
    ppermute x5 -> x6, waiting for transfers between devices: 24.6 us -> 15.9 us  [swap(): return lax.ppermute(value, AXES, permutation(move))]
    all_to_all x1, waiting for transfers between devices: 8.65 us -> 1.64 us  [on_device(): lax.all_to_all(held, 'dp', 0, 0, axis_index_groups=PLANE, tiled=True)]
    all_to_all x1, starting transfers between devices: 3.61 us -> 6.92 us  [on_device(): lax.all_to_all(mix(place, held), 'dp', 0, 0, axis_index_groups=PLANE, til...]
    pallas_call x1, Pallas kernels: 26 us -> 23 us  [solve(): pl.pallas_call(solve_kernel, out_shape=(jax.ShapeDtypeStruct((256, STEPS...]
    all_to_all x1, starting transfers between devices: 8.18 us -> 9.93 us  [on_device(): held = lax.all_to_all(held, AXES, 0, 0, axis_index_groups=LINE, tiled=True)]
  transfers between devices with their start and end apart: 8 -> 9, of which waited for: 5 -> 6; matrix products, arithmetic and copies ran while one was open for 2% -> 2% of each run, Pallas kernels for 23% -> 21%
where the time goes in v3:
time: 119 us
  Pallas kernels  43.3 us (36%)
  starting transfers between devices  41.1 us (35%)
  waiting for transfers between devices  27.1 us (23%)
  local copies, waits for them, and re-layouts  5.58 us (5%)
    pallas_call x1, Pallas kernels, solve(): pl.pallas_call(solve_kernel, out_shape=(jax.ShapeDtypeStruct((256, STEPS...  23 us
    ppermute x6, starting transfers between devices, swap(): return lax.ppermute(value, AXES, permutation(move))  16.6 us
    ppermute x6, waiting for transfers between devices, swap(): return lax.ppermute(value, AXES, permutation(move))  15.9 us
    all_to_all x1, starting transfers between devices, on_device(): held = lax.all_to_all(held, AXES, 0, 0, axis_index_groups=LINE, tiled=True)  9.93 us
    all_to_all x1, waiting for transfers between devices, on_device(): held = lax.all_to_all(held, AXES, 0, 0, axis_index_groups=LINE, tiled=True)  9.6 us
    pallas_call x1, Pallas kernels, update(): pl.pallas_call(update_kernel, grid=(rows // TILE,), in_specs=[pl.BlockSpe...  9.03 us
    all_to_all x1, starting transfers between devices, on_device(): lax.all_to_all(held, 'dp', 0, 0, axis_index_groups=PLANE, tiled=True)  7.71 us
    all_to_all x1, starting transfers between devices, on_device(): lax.all_to_all(mix(place, held), 'dp', 0, 0, axis_index_groups=PLANE, til...  6.92 us
  transfers between devices with their start and end apart: 9, of which 6 were waited for; matrix products, arithmetic and copies ran while one was open for 2% of the time, Pallas kernels for 21%

profile of v3, /device:TPU:1, one launch (start us, length us, event | category | flops | bytes accessed | tf_op | source)
XLA Modules:
  0.0 118.5 jit_solution(233434426512139617)
XLA Ops:
  0.6 0.0 copy-start.8
  0.7 0.7 copy-done.8
  1.3 0.1 sub.41
  1.4 1.3 %sub.48.local = s32[1024,1]{1,0:T(8,128)} reshape(s32[16,2,32]{2,1,0:T(2,128)S(1)} %bitcast.15) | data formatting | bytes 8192 | tf_op jit(solution)/shard_map/sub | solution.py:379
  2.8 5.7 %pick.1 = bf16[1024,256]{1,0:T(8,128)(2,1)} custom-call(s32[1024,1]{1,0:T(8,128)} %sub.48.local, bf16[112,4096]{1,0:T(8,128)(2,1)} %frames.1, f32[37,4096]{1,0:T(8,128)} %residual.3), custom_call_target="tpu_custom_call" | custom-call | tf_op jit(solution)/shard_map/pick/pallas_call | solution.py:170
  8.5 0.0 copy-start.5
  8.5 7.7 %all-to-all-start = ((bf16[16,64,256]{2,1,0:T(8,128)(2,1)}), bf16[16,64,256]{2,1,0:T(8,128)(2,1)S(1)}, u32[]{:S(2)}, u32[]{:S(2)}) async-start(bf16[16,64,256]{2,1,0:T(8,128)(2,1)} %bitcast.14), calls=%async_computation | async-start | bytes 1048576 | tf_op jit(solution)/shard_map/all_to_all | solution.py:380
  16.2 0.0 copy-done.5
  16.2 0.9 constant_dynamic-slice_fusion.1
  17.1 1.0 collective-permute-start
  18.1 7.0 %collective-permute-start.1 = (bf16[112,1024]{1,0:T(8,128)(2,1)S(1)}, bf16[112,1024]{1,0:T(8,128)(2,1)S(1)}, u32[]{:S(2)}, u32[]{:S(2)}) collective-permute-start(bf16[112,1024]{1,0:T(8,128)(2,1)S(1)} %constant_dynamic-slice_fusion), channel_id=1, source_target_pairs={{0,2},{1,3},{2,0},{3,1},{4,6},{5,7},{6,4},{7,5},{8,10},{9,11},{10,... | collective-permute-start | bytes 688136 | tf_op jit(solution)/shard_map/ppermute | solution.py:38
  25.1 1.6 %all-to-all-done.held = bf16[16,64,256]{2,1,0:T(8,128)(2,1)S(1)} async-done(((bf16[16,64,256]{2,1,0:T(8,128)(2,1)}), bf16[16,64,256]{2,1,0:T(8,128)(2,1)S(1)}, u32[]{:S(2)}, u32[]{:S(2)}) %all-to-all-start) | async-done | bytes 524320 | tf_op jit(solution)/shard_map/all_to_all | solution.py:380
  26.7 0.0 copy-start.6
  26.7 0.8 copy-done.6
  27.5 1.8 %add.17 = bf16[8,64,256]{2,1,0:T(8,128)(2,1)} custom-call(bf16[16,64,256]{2,1,0:T(8,128)(2,1)} %copy-done.6), custom_call_target="tpu_custom_call" | custom-call | tf_op jit(solution)/shard_map/add/pallas_call | solution.py:196
  29.3 2.7 %collective-permute-done.1.a0 = bf16[112,1024]{1,0:T(8,128)(2,1)S(1)} collective-permute-done((bf16[112,1024]{1,0:T(8,128)(2,1)S(1)}, bf16[112,1024]{1,0:T(8,128)(2,1)S(1)}, u32[]{:S(2)}, u32[]{:S(2)}) %collective-permute-start.1) | collective-permute-done | bytes 229408 | tf_op jit(solution)/shard_map/ppermute | solution.py:38
  32.0 0.0 collective-permute-done.s2
  32.0 9.9 %all-to-all-start.1 = ((bf16[8,64,256]{2,1,0:T(8,128)(2,1)}), bf16[8,64,256]{2,1,0:T(8,128)(2,1)S(1)}, u32[]{:S(2)}, u32[]{:S(2)}) async-start(bf16[8,64,256]{2,1,0:T(8,128)(2,1)} %add.17), calls=%async_computation.1 | async-start | bytes 524288 | tf_op jit(solution)/shard_map/all_to_all | solution.py:382
  42.0 0.6 pad_add_fusion.place
  42.6 9.6 %all-to-all-done.1.held = bf16[8,64,256]{2,1,0:T(8,128)(2,1)S(1)} async-done(((bf16[8,64,256]{2,1,0:T(8,128)(2,1)}), bf16[8,64,256]{2,1,0:T(8,128)(2,1)S(1)}, u32[]{:S(2)}, u32[]{:S(2)}) %all-to-all-start.1) | async-done | bytes 262176 | tf_op jit(solution)/shard_map/all_to_all | solution.py:382
  52.2 0.0 copy-start.7
  52.2 0.7 copy-done.7
  52.9 2.0 %mix.1 = bf16[16,64,384]{2,1,0:T(8,128)(2,1)} custom-call(s32[2]{0:T(128)} %pad_add_fusion.place, bf16[8,64,256]{2,1,0:T(8,128)(2,1)} %copy-done.7), custom_call_target="tpu_custom_call" | custom-call | tf_op jit(solution)/shard_map/mix/pallas_call | solution.py:219
  54.9 6.9 %all-to-all-start.2 = ((bf16[16,64,384]{2,1,0:T(8,128)(2,1)}), bf16[16,64,384]{2,1,0:T(8,128)(2,1)S(1)}, u32[]{:S(2)}, u32[]{:S(2)}) async-start(bf16[16,64,384]{2,1,0:T(8,128)(2,1)} %mix.1), calls=%async_computation.2 | async-start | bytes 1572864 | tf_op jit(solution)/shard_map/all_to_all | solution.py:385
  61.8 1.7 %collective-permute-start.2 = (bf16[112,1024]{1,0:T(8,128)(2,1)S(1)}, bf16[112,1024]{1,0:T(8,128)(2,1)S(1)}, u32[]{:S(2)}, u32[]{:S(2)}) collective-permute-start(bf16[112,1024]{1,0:T(8,128)(2,1)S(1)} %slice.13), channel_id=1, source_target_pairs={{0,2},{1,3},{2,0},{3,1},{4,6},{5,7},{6,4},{7,5},{8,10},{9,11},{10,... | collective-permute-start | bytes 688136 | tf_op jit(solution)/shard_map/ppermute | solution.py:38
  63.5 10.3 %collective-permute-done.2.a1 = bf16[112,1024]{1,0:T(8,128)(2,1)S(1)} collective-permute-done((bf16[112,1024]{1,0:T(8,128)(2,1)S(1)}, bf16[112,1024]{1,0:T(8,128)(2,1)S(1)}, u32[]{:S(2)}, u32[]{:S(2)}) %collective-permute-start.2) | collective-permute-done | bytes 229408 | tf_op jit(solution)/shard_map/ppermute | solution.py:38
  73.7 0.0 copy-start.2
  73.7 0.7 copy-done.2
  74.4 0.0 all-to-all-done.2.near
  74.4 5.0 %collective-permute-start.4 = (bf16[16,64,384]{2,1,0:T(8,128)(2,1)S(1)}, bf16[16,64,384]{2,1,0:T(8,128)(2,1)S(1)}, u32[]{:S(2)}, u32[]{:S(2)}) collective-permute-start(bf16[16,64,384]{2,1,0:T(8,128)(2,1)S(1)} %all-to-all-done.2.near), channel_id=1, source_target_pairs={{0,1},{1,0},{2,3},{3,2},{4,5},{5,4},{6,7},{7,6},{8,9},{9,8},{10,11... | collective-permute-start | bytes 2359304 | tf_op jit(solution)/shard_map/ppermute | solution.py:38
  79.4 1.5 %collective-permute-start.3 = (bf16[112,2048]{1,0:T(8,128)(2,1)}, bf16[112,2048]{1,0:T(8,128)(2,1)}, u32[]{:S(2)}, u32[]{:S(2)}) collective-permute-start(bf16[112,2048]{1,0:T(8,128)(2,1)} %get-tuple-element.26), channel_id=1, source_target_pairs={{0,3},{1,2},{2,1},{3,0},{4,7},{5,6},{6,5},{7,4},{8,11},{9,10},{10,... | collective-permute-start | bytes 1376264 | tf_op jit(solution)/shard_map/ppermute | solution.py:38
  80.9 0.1 copy.9.point_col
  81.1 0.2 copy.12
  81.3 0.0 collective-permute-done.4.far
  81.3 0.0 copy-start.3
  81.3 23.0 %solve.1 = (bf16[256,1024]{1,0:T(8,128)(2,1)S(1)}, f32[1024,1]{1,0:T(8,128)S(1)}) custom-call(bf16[16,64,384]{2,1,0:T(8,128)(2,1)S(1)} %all-to-all-done.2.near, bf16[16,64,384]{2,1,0:T(8,128)(2,1)S(1)} %collective-permute-done.4.far, s32[1,512]{1,0:T(1,128)S(1)} %get-tuple-element.39.point_row, s32[512,1]{1,0:T(8,128)S(1)} %copy.9.point_col), custom_call_target="tpu_custom_call" | custom-call | flops 1048576 | bytes 1048576 | tf_op jit(solution)/shard_map/solve/pallas_call | solution.py:281
  104.3 1.2 collective-permute-done.3.s3
  105.5 0.0 copy-done.3
  105.5 0.0 copy-start
  105.5 0.0 copy-start.1
  105.5 9.0 %update.1 = (f32[2,40,2048]{2,1,0:T(8,128)S(1)}, f32[2,40,2048]{2,1,0:T(8,128)S(1)}) custom-call(bf16[112,2048]{1,0:T(8,128)(2,1)S(1)} %get-tuple-element.21.s0, bf16[112,2048]{1,0:T(8,128)(2,1)S(1)} %collective-permute-done.s2, bf16[112,2048]{1,0:T(8,128)(2,1)} %collective-permute-done.3.s3, bf16[112,1024]{1,0:T(8,128)(2,1)S(1)} %collective-permute-done.1.a0, ...), custom_call_target="tpu_custom_call" | custom-call | tf_op jit(solution)/shard_map/update/pallas_call | solution.py:335
  114.6 0.0 copy-start.4
  114.6 0.5 collective-permute-start.5
  115.1 1.7 %collective-permute-done.5.got = f32[2,40,2048]{2,1,0:T(8,128)S(1)} collective-permute-done((f32[2,40,2048]{2,1,0:T(8,128)S(1)}, f32[2,40,2048]{2,1,0:T(8,128)S(1)}, u32[]{:S(2)}, u32[]{:S(2)}) %collective-permute-start.5) | collective-permute-done | bytes 655392 | tf_op jit(solution)/shard_map/ppermute | solution.py:38
  116.8 0.0 copy-done
  116.8 0.0 copy-done.1
  116.8 0.0 copy-done.4
  116.8 1.8 %finish.1 = (f32[37,4096]{1,0:T(8,128)}, f32[37,4096]{1,0:T(8,128)}) custom-call(s32[2]{0:T(128)S(1)} %copy-done.4, f32[37,4096]{1,0:T(8,128)S(1)} %copy-done, f32[37,4096]{1,0:T(8,128)S(1)} %copy-done.1, f32[2,40,2048]{2,1,0:T(8,128)S(1)} %get-tuple-element.32.mine, f32[2,40,2048]{2,1,0:T(8,128)S(1)} %collective-permute-done.5.got), custom_call_target="tpu_custom_call" | custom-call | tf_op jit(solution)/shard_map/finish/pallas_call | solution.py:356
  (6 shorter events, 0.1 us)
Async XLA Ops:
  0.6 0.7 copy-start.8
  8.5 7.7 %copy-start.5 = (bf16[112,4096]{1,0:T(8,128)(2,1)S(1)}, bf16[112,4096]{1,0:T(8,128)(2,1)}, u32[]{:S(2)}) copy-start(bf16[112,4096]{1,0:T(8,128)(2,1)} %frames.1) | copy-start | bytes 2752516
  8.5 18.2 %all-to-all-start = ((bf16[16,64,256]{2,1,0:T(8,128)(2,1)}), bf16[16,64,256]{2,1,0:T(8,128)(2,1)S(1)}, u32[]{:S(2)}, u32[]{:S(2)}) async-start(bf16[16,64,256]{2,1,0:T(8,128)(2,1)} %bitcast.14), calls=%async_computation | async-start | bytes 1048576 | tf_op jit(solution)/shard_map/all_to_all | solution.py:380
  17.1 14.9 %collective-permute-start = (bf16[112,2048]{1,0:T(8,128)(2,1)}, bf16[112,2048]{1,0:T(8,128)(2,1)S(1)}, u32[]{:S(2)}, u32[]{:S(2)}) collective-permute-start(bf16[112,2048]{1,0:T(8,128)(2,1)} %get-tuple-element.26), channel_id=1, source_target_pairs={{0,1},{1,0},{2,3},{3,2},{4,5},{5,4},{6,7},{7,6},{8,9},{9,8},{10,11... | collective-permute-start | bytes 1376264 | tf_op jit(solution)/shard_map/ppermute | solution.py:38
  18.1 14.0 %collective-permute-start.1 = (bf16[112,1024]{1,0:T(8,128)(2,1)S(1)}, bf16[112,1024]{1,0:T(8,128)(2,1)S(1)}, u32[]{:S(2)}, u32[]{:S(2)}) collective-permute-start(bf16[112,1024]{1,0:T(8,128)(2,1)S(1)} %constant_dynamic-slice_fusion), channel_id=1, source_target_pairs={{0,2},{1,3},{2,0},{3,1},{4,6},{5,7},{6,4},{7,5},{8,10},{9,11},{10,... | collective-permute-start | bytes 688136 | tf_op jit(solution)/shard_map/ppermute | solution.py:38
  26.7 0.8 copy-start.6
  32.0 20.1 %all-to-all-start.1 = ((bf16[8,64,256]{2,1,0:T(8,128)(2,1)}), bf16[8,64,256]{2,1,0:T(8,128)(2,1)S(1)}, u32[]{:S(2)}, u32[]{:S(2)}) async-start(bf16[8,64,256]{2,1,0:T(8,128)(2,1)} %add.17), calls=%async_computation.1 | async-start | bytes 524288 | tf_op jit(solution)/shard_map/all_to_all | solution.py:382
  52.2 0.7 copy-start.7
  54.9 19.6 %all-to-all-start.2 = ((bf16[16,64,384]{2,1,0:T(8,128)(2,1)}), bf16[16,64,384]{2,1,0:T(8,128)(2,1)S(1)}, u32[]{:S(2)}, u32[]{:S(2)}) async-start(bf16[16,64,384]{2,1,0:T(8,128)(2,1)} %mix.1), calls=%async_computation.2 | async-start | bytes 1572864 | tf_op jit(solution)/shard_map/all_to_all | solution.py:385
  61.8 11.9 %collective-permute-start.2 = (bf16[112,1024]{1,0:T(8,128)(2,1)S(1)}, bf16[112,1024]{1,0:T(8,128)(2,1)S(1)}, u32[]{:S(2)}, u32[]{:S(2)}) collective-permute-start(bf16[112,1024]{1,0:T(8,128)(2,1)S(1)} %slice.13), channel_id=1, source_target_pairs={{0,2},{1,3},{2,0},{3,1},{4,6},{5,7},{6,4},{7,5},{8,10},{9,11},{10,... | collective-permute-start | bytes 688136 | tf_op jit(solution)/shard_map/ppermute | solution.py:38
  73.7 0.7 copy-start.2
  74.4 6.9 %collective-permute-start.4 = (bf16[16,64,384]{2,1,0:T(8,128)(2,1)S(1)}, bf16[16,64,384]{2,1,0:T(8,128)(2,1)S(1)}, u32[]{:S(2)}, u32[]{:S(2)}) collective-permute-start(bf16[16,64,384]{2,1,0:T(8,128)(2,1)S(1)} %all-to-all-done.2.near), channel_id=1, source_target_pairs={{0,1},{1,0},{2,3},{3,2},{4,5},{5,4},{6,7},{7,6},{8,9},{9,8},{10,11... | collective-permute-start | bytes 2359304 | tf_op jit(solution)/shard_map/ppermute | solution.py:38
  79.4 26.1 %collective-permute-start.3 = (bf16[112,2048]{1,0:T(8,128)(2,1)}, bf16[112,2048]{1,0:T(8,128)(2,1)}, u32[]{:S(2)}, u32[]{:S(2)}) collective-permute-start(bf16[112,2048]{1,0:T(8,128)(2,1)} %get-tuple-element.26), channel_id=1, source_target_pairs={{0,3},{1,2},{2,1},{3,0},{4,7},{5,6},{6,5},{7,4},{8,11},{9,10},{10,... | collective-permute-start | bytes 1376264 | tf_op jit(solution)/shard_map/ppermute | solution.py:38
  81.3 24.2 %copy-start.3 = (bf16[112,1024]{1,0:T(8,128)(2,1)S(1)}, bf16[112,1024]{1,0:T(8,128)(2,1)}, u32[]{:S(2)}) copy-start(bf16[112,1024]{1,0:T(8,128)(2,1)} %copy-done.2) | copy-start | bytes 688132
  105.5 11.3 %copy-start = (f32[37,4096]{1,0:T(8,128)S(1)}, f32[37,4096]{1,0:T(8,128)}, u32[]{:S(2)}) copy-start(f32[37,4096]{1,0:T(8,128)} %residual.3) | copy-start | bytes 1818628
  105.5 11.3 %copy-start.1 = (f32[37,4096]{1,0:T(8,128)S(1)}, f32[37,4096]{1,0:T(8,128)}, u32[]{:S(2)}) copy-start(f32[37,4096]{1,0:T(8,128)} %coefficients.1) | copy-start | bytes 1818628
  114.6 2.2 %copy-start.4 = (s32[2]{0:T(128)S(1)}, s32[2]{0:T(128)}, u32[]{:S(2)}) copy-start(s32[2]{0:T(128)} %pad_add_fusion.place) | copy-start | bytes 28
  114.6 2.2 %collective-permute-start.5 = (f32[2,40,2048]{2,1,0:T(8,128)S(1)}, f32[2,40,2048]{2,1,0:T(8,128)S(1)}, u32[]{:S(2)}, u32[]{:S(2)}) collective-permute-start(f32[2,40,2048]{2,1,0:T(8,128)S(1)} %get-tuple-element.33), channel_id=1, source_target_pairs={{0,1},{1,0},{2,3},{3,2},{4,5},{5,4},{6,7},{7,6},{8,9},{9,8},{10,11... | collective-permute-start | bytes 1966088 | tf_op jit(solution)/shard_map/ppermute | solution.py:38

commit v4 on v3

--- a/solution.py
+++ b/solution.py
@@ -140,47 +140,52 @@
                     mats[s, at_i, at_j] = mats[s, at_i, at_j] - out[here, 128 * j + 128 : 128 * j + 256]
 
 
-def pick_kernel(local, frames, residual, out, total, padded):
+def pick_kernel(place, index, frames, residual, out, total, padded):
     step = pl.program_id(0)
-    positions = step * PICK + lax.broadcasted_iota(jnp.int32, (1, PICK), 1)
-    select = jnp.where(local[...] == positions, 1.0, 0.0).astype(BF16)
+    positions = place[2] + step * PICK + lax.broadcasted_iota(jnp.int32, (PICK, BLOCK), 0)
     padded[...] = jnp.zeros_like(padded)
     padded[:ROWS] = residual[...]
     parts = [v.astype(F32) for v in split3(padded[...])] + [jnp.zeros((8, PICK), F32)]
     packed = jnp.concatenate(
         [frames[...], jnp.zeros((16, PICK), BF16), jnp.concatenate(parts, axis=0).astype(BF16)], axis=0
     )
-    picked = lax.dot_general(select, packed, (((1,), (1,)), ((), ())), preferred_element_type=F32)
+    picked = []
+    for s in range(STEPS):
+        select = jnp.where(index[s : s + 1] == positions, 1.0, 0.0).astype(BF16)
+        picked.append(jnp.dot(packed, select, preferred_element_type=F32))
 
     @pl.when(step == 0)
     def _():
-        total[...] = picked
+        for s in range(STEPS):
+            total[s] = picked[s]
 
     @pl.when(step > 0)
     def _():
-        total[...] += picked
+        for s in range(STEPS):
+            total[s] += picked[s]
 
     @pl.when(step == pl.num_programs(0) - 1)
     def _():
-        out[...] = total[...].astype(BF16)
-
-
-def pick(local, frames, residual):
-    points = local.shape[0]
+        for s in range(STEPS):
+            out[:, 32 * s : 32 * s + 32] = total[s].T.astype(BF16).reshape(16, 32, 256)
+
+
+def pick(place, index, frames, residual):
     return pl.pallas_call(
         pick_kernel,
         grid=(frames.shape[1] // PICK,),
         in_specs=[
+            pl.BlockSpec(memory_space=pltpu.SMEM),
             pl.BlockSpec(memory_space=pltpu.VMEM),
             pl.BlockSpec((112, PICK), lambda i: (0, i)),
             pl.BlockSpec((ROWS, PICK), lambda i: (0, i)),
         ],
-        out_specs=pl.BlockSpec((points, 256), lambda i: (0, 0)),
-        out_shape=jax.ShapeDtypeStruct((points, 256), BF16),
-        scratch_shapes=[pltpu.VMEM((points, 256), F32), pltpu.VMEM((40, PICK), F32)],
+        out_specs=pl.BlockSpec((16, 64, 256), lambda i: (0, 0, 0)),
+        out_shape=jax.ShapeDtypeStruct((16, 64, 256), BF16),
+        scratch_shapes=[pltpu.VMEM((STEPS, 256, BLOCK), F32), pltpu.VMEM((40, PICK), F32)],
         compiler_params=pltpu.CompilerParams(vmem_limit_bytes=60 << 20),
         name="pick",
-    )(local, frames, residual)
+    )(place, index, frames, residual)
 
 
 def add_kernel(held, out):
@@ -295,8 +300,9 @@
     )(near, far, chosen[1].reshape(1, BLOCK), chosen[0].reshape(BLOCK, 1))
 
 
-def update_kernel(s0, s2, s3, a0, a1, near, far, delta, sq, local, mine_ref, theirs_ref):
-    s1 = jnp.where(pl.program_id(0) == 0, a0[...], a1[...])
+def update_kernel(s0, s2, s3, a0, a1, a2, a3, near, far, delta, sq, local, mine_ref, theirs_ref):
+    pieces = [jnp.concatenate([one[...], two[...]], axis=1) for one, two in ((a0, a1), (a2, a3))]
+    s1 = jnp.where(pl.program_id(0) == 0, *pieces)
 
     def squares(ref):
         value = ref[...].astype(F32)
@@ -335,7 +341,7 @@
     return pl.pallas_call(
         update_kernel,
         grid=(rows // TILE,),
-        in_specs=[pl.BlockSpec((112, TILE), lambda i: (0, i))] * 3 + [whole] * 7,
+        in_specs=[pl.BlockSpec((112, TILE), lambda i: (0, i))] * 3 + [whole] * 9,
         out_specs=[pl.BlockSpec((2, 40, TILE), lambda i: (0, 0, i))] * 2,
         out_shape=[jax.ShapeDtypeStruct((2, 40, rows), F32)] * 2,
         compiler_params=pltpu.CompilerParams(vmem_limit_bytes=40 << 20),
@@ -368,24 +374,27 @@
     rows = frames.shape[1]
     dp, feat = lax.axis_index("dp"), lax.axis_index("feat")
     h, c = feat // 2, feat % 2
-    place = jnp.stack([h, c]).astype(jnp.int32)
+    place = jnp.stack([h, c, dp * rows]).astype(jnp.int32)
     own_half = lax.dynamic_slice_in_dim(frames, c * (rows // 2), rows // 2, axis=1)
     other_half = lax.dynamic_slice_in_dim(frames, (1 - c) * (rows // 2), rows // 2, axis=1)
     beside = swap(other_half, 0, 1)
-    piece = rows // 4
-    across = [swap(own_half[:, :piece], 1, 0)]
-
-    points = block_index.reshape(STEPS, 16, 32).transpose(1, 0, 2).reshape(-1, 1)
-    held = pick(points - dp * rows, frames, residual).reshape(16, 64, 256)
+    size = rows // 8
+    own = [lax.dynamic_slice_in_dim(frames, c * (rows // 2) + i * size, size, axis=1) for i in range(4)]
+    across = [swap(own[0], 1, 0)]
+
+    held = pick(place, block_index, frames, residual)
+    held, across, own = lax.optimization_barrier((held, across, own))
+    across.append(swap(own[1], 1, 0))
     held = add(lax.all_to_all(held, "dp", 0, 0, axis_index_groups=PLANE, tiled=True))
-    held, beside, across, own_half, other_half = lax.optimization_barrier((held, beside, across, own_half, other_half))
+    held, beside, across, own, other_half = lax.optimization_barrier((held, beside, across, own, other_half))
     held = lax.all_to_all(held, AXES, 0, 0, axis_index_groups=LINE, tiled=True)
-    held, own_half, other_half = lax.optimization_barrier((held, own_half, other_half))
-    across.append(swap(own_half[:, piece:], 1, 0))
+    held, own, other_half = lax.optimization_barrier((held, own, other_half))
+    across.append(swap(own[2], 1, 0))
     near = lax.all_to_all(mix(place, held), "dp", 0, 0, axis_index_groups=PLANE, tiled=True)
-    near, across, other_half = lax.optimization_barrier((near, across, other_half))
+    near, across, own, other_half = lax.optimization_barrier((near, across, own, other_half))
+    far = swap(near, 0, 1)
+    across.append(swap(own[3], 1, 0))
     diagonal = swap(other_half, 1, 1)
-    far = swap(near, 0, 1)
 
     delta, sq = solve(near, far, block_index)
     local = block_index.reshape(-1, 1) - dp * rows - c * (rows // 2)

time: 119 us -> 122 us (1.025)
  blocking collectives: 0 us -> 15.8 us
  waiting for transfers between devices: 27.1 us -> 18.6 us
  starting transfers between devices: 41.1 us -> 38.4 us
    all_to_all x0 -> x1, blocking collectives: none -> 15.8 us  [on_device(): held = lax.all_to_all(held, AXES, 0, 0, axis_index_groups=LINE, tiled=True)]
    all_to_all x1 -> x0, starting transfers between devices: 9.93 us -> none  [on_device(): held = lax.all_to_all(held, AXES, 0, 0, axis_index_groups=LINE, tiled=True)]
    all_to_all x1 -> x0, waiting for transfers between devices: 9.6 us -> none  [on_device(): held = lax.all_to_all(held, AXES, 0, 0, axis_index_groups=LINE, tiled=True)]
    ppermute x6 -> x8, starting transfers between devices: 16.6 us -> 23.7 us  [swap(): return lax.ppermute(value, AXES, permutation(move))]
    ppermute x6 -> x8, waiting for transfers between devices: 15.9 us -> 10.4 us  [swap(): return lax.ppermute(value, AXES, permutation(move))]
    all_to_all x1, waiting for transfers between devices: 0.01 us -> 3.85 us  [on_device(): lax.all_to_all(mix(place, held), 'dp', 0, 0, axis_index_groups=PLANE, til...]
    all_to_all x1, waiting for transfers between devices: 1.64 us -> 4.33 us  [on_device(): lax.all_to_all(held, 'dp', 0, 0, axis_index_groups=PLANE, tiled=True)]
    dynamic_slice x1 -> x2, local copies, waits for them, and re-layouts: 0.87 us -> 2.61 us  [the longest x1 1.76 us: on_device(): lax.dynamic_slice_in_dim(frames, c * (rows // 2) + i * size, size, axis=1)]
  transfers between devices with their start and end apart: 9 -> 10, of which waited for: 6 -> 5; matrix products, arithmetic and copies ran while one was open for 2% -> 2% of each run, Pallas kernels for 21% -> 25%
where the time goes in v4:
time: 122 us
  Pallas kernels  43.2 us (35%)
  starting transfers between devices  38.4 us (31%)
  waiting for transfers between devices  18.6 us (15%)
  blocking collectives  15.8 us (13%)
  local copies, waits for them, and re-layouts  4.46 us (4%)
    ppermute x8, starting transfers between devices, swap(): return lax.ppermute(value, AXES, permutation(move))  23.7 us
    pallas_call x1, Pallas kernels, solve(): pl.pallas_call(solve_kernel, out_shape=(jax.ShapeDtypeStruct((256, STEPS...  22.9 us
    all_to_all x1, blocking collectives, on_device(): held = lax.all_to_all(held, AXES, 0, 0, axis_index_groups=LINE, tiled=True)  15.8 us
    ppermute x8, waiting for transfers between devices, swap(): return lax.ppermute(value, AXES, permutation(move))  10.4 us
    pallas_call x1, Pallas kernels, update(): pl.pallas_call(update_kernel, grid=(rows // TILE,), in_specs=[pl.BlockSpe...  9.14 us
    all_to_all x1, starting transfers between devices, on_device(): lax.all_to_all(mix(place, held), 'dp', 0, 0, axis_index_groups=PLANE, til...  7.78 us
    all_to_all x1, starting transfers between devices, on_device(): lax.all_to_all(held, 'dp', 0, 0, axis_index_groups=PLANE, tiled=True)  6.9 us
    pallas_call x1, Pallas kernels, pick(): pl.pallas_call(pick_kernel, grid=(frames.shape[1] // PICK,), in_specs=[pl...  5.58 us
  transfers between devices with their start and end apart: 10, of which 5 were waited for; matrix products, arithmetic and copies ran while one was open for 2% of the time, Pallas kernels for 25%

profile of v4, /device:TPU:1, one launch (start us, length us, event | category | flops | bytes accessed | tf_op | source)
XLA Modules:
  0.0 121.8 jit_solution(18223956775213939025)
XLA Ops:
  0.7 1.8 %constant_dynamic-slice_fusion.1 = (bf16[112,512]{1,0:T(8,128)(2,1)}, bf16[112,512]{1,0:T(8,128)(2,1)S(1)}, bf16[112,512]{1,0:T(8,128)(2,1)S(1)}, bf16[112,512]{1,0:T(8,128)(2,1)S(1)}) fusion(bf16[112,4096]{1,0:T(8,128)(2,1)} %frames.1, s32[]{:T(128)S(6)} %select_n.32, s32[]{:T(128)S(6)} %select_n.31, s32[]{:T(128)S(6)} %select_n.30, s32[]{:T(128)S(6)} %select_n.29), kind=kLoop, calls=%fused_computation.3 | loop fusion | bytes 917520 | tf_op jit(solution)/shard_map/dynamic_slice | solution.py:382
  2.4 7.7 %collective-permute-start = (bf16[112,512]{1,0:T(8,128)(2,1)S(1)}, bf16[112,512]{1,0:T(8,128)(2,1)S(1)}, u32[]{:S(2)}, u32[]{:S(2)}) collective-permute-start(bf16[112,512]{1,0:T(8,128)(2,1)S(1)} %get-tuple-element.59), channel_id=1, source_target_pairs={{0,2},{1,3},{2,0},{3,1},{4,6},{5,7},{6,4},{7,5},{8,10},{9,11},{10,... | collective-permute-start | bytes 344072 | tf_op jit(solution)/shard_map/ppermute | solution.py:38
  10.2 0.6 pad_add_fusion.place
  10.8 5.6 %pick.1 = bf16[16,64,256]{2,1,0:T(8,128)(2,1)} custom-call(s32[3]{0:T(128)} %pad_add_fusion.place, s32[2,512]{1,0:T(2,128)} %index.1, bf16[112,4096]{1,0:T(8,128)(2,1)} %frames.1, f32[37,4096]{1,0:T(8,128)} %residual.3), custom_call_target="tpu_custom_call" | custom-call | tf_op jit(solution)/shard_map/pick/pallas_call | solution.py:174
  16.4 0.0 copy-start.5
  16.4 0.0 collective-permute-done.a0
  16.4 6.9 %all-to-all-start = ((bf16[16,64,256]{2,1,0:T(8,128)(2,1)}), bf16[16,64,256]{2,1,0:T(8,128)(2,1)S(1)}, u32[]{:S(2)}, u32[]{:S(2)}) async-start(bf16[16,64,256]{2,1,0:T(8,128)(2,1)} %pick.1), calls=%async_computation | async-start | bytes 1048576 | tf_op jit(solution)/shard_map/all_to_all | solution.py:388
  23.3 0.0 copy-done.5
  23.3 0.9 constant_dynamic-slice_fusion
  24.1 1.2 %collective-permute-start.1 = (bf16[112,2048]{1,0:T(8,128)(2,1)}, bf16[112,2048]{1,0:T(8,128)(2,1)S(1)}, u32[]{:S(2)}, u32[]{:S(2)}) collective-permute-start(bf16[112,2048]{1,0:T(8,128)(2,1)} %get-tuple-element.44), channel_id=1, source_target_pairs={{0,1},{1,0},{2,3},{3,2},{4,5},{5,4},{6,7},{7,6},{8,9},{9,8},{10,11... | collective-permute-start | bytes 1376264 | tf_op jit(solution)/shard_map/ppermute | solution.py:38
  25.4 3.9 %collective-permute-start.2 = (bf16[112,512]{1,0:T(8,128)(2,1)S(1)}, bf16[112,512]{1,0:T(8,128)(2,1)S(1)}, u32[]{:S(2)}, u32[]{:S(2)}) collective-permute-start(bf16[112,512]{1,0:T(8,128)(2,1)S(1)} %get-tuple-element.30), channel_id=1, source_target_pairs={{0,2},{1,3},{2,0},{3,1},{4,6},{5,7},{6,4},{7,5},{8,10},{9,11},{10,... | collective-permute-start | bytes 344072 | tf_op jit(solution)/shard_map/ppermute | solution.py:38
  29.3 4.3 %all-to-all-done.held = bf16[16,64,256]{2,1,0:T(8,128)(2,1)S(1)} async-done(((bf16[16,64,256]{2,1,0:T(8,128)(2,1)}), bf16[16,64,256]{2,1,0:T(8,128)(2,1)S(1)}, u32[]{:S(2)}, u32[]{:S(2)}) %all-to-all-start) | async-done | bytes 524320 | tf_op jit(solution)/shard_map/all_to_all | solution.py:388
  33.6 0.0 copy-start.6
  33.6 0.8 copy-done.6
  34.4 1.8 %add.50 = bf16[8,64,256]{2,1,0:T(8,128)(2,1)} custom-call(bf16[16,64,256]{2,1,0:T(8,128)(2,1)} %copy-done.6), custom_call_target="tpu_custom_call" | custom-call | tf_op jit(solution)/shard_map/add/pallas_call | solution.py:201
  36.3 0.0 collective-permute-done.2.a1
  36.3 0.0 collective-permute-done.1.s2
  36.3 15.8 %all_to_all.15.held = bf16[8,64,256]{2,1,0:T(8,128)(2,1)} all-to-all(bf16[8,64,256]{2,1,0:T(8,128)(2,1)} %add.50), channel_id=1, replica_groups={{0,4,8,12,2,6,10,14},{1,5,9,13,3,7,11,15},{16,20,24,28,18,22,26,30},{17..., dimensions={0} | all-to-all | bytes 524288 | tf_op jit(solution)/shard_map/all_to_all | solution.py:390
  52.0 2.0 %mix.1 = bf16[16,64,384]{2,1,0:T(8,128)(2,1)} custom-call(s32[3]{0:T(128)} %pad_add_fusion.place, bf16[8,64,256]{2,1,0:T(8,128)(2,1)} %all_to_all.15.held), custom_call_target="tpu_custom_call" | custom-call | tf_op jit(solution)/shard_map/mix/pallas_call | solution.py:224
  54.0 0.0 copy-start.7
  54.0 7.8 %all-to-all-start.2 = ((bf16[16,64,384]{2,1,0:T(8,128)(2,1)}), bf16[16,64,384]{2,1,0:T(8,128)(2,1)S(1)}, u32[]{:S(2)}, u32[]{:S(2)}) async-start(bf16[16,64,384]{2,1,0:T(8,128)(2,1)} %mix.1), calls=%async_computation.2 | async-start | bytes 1572864 | tf_op jit(solution)/shard_map/all_to_all | solution.py:393
  61.8 1.0 collective-permute-start.3
  62.8 6.8 %collective-permute-done.3.a2 = bf16[112,512]{1,0:T(8,128)(2,1)S(1)} collective-permute-done((bf16[112,512]{1,0:T(8,128)(2,1)S(1)}, bf16[112,512]{1,0:T(8,128)(2,1)S(1)}, u32[]{:S(2)}, u32[]{:S(2)}) %collective-permute-start.3) | collective-permute-done | bytes 114720 | tf_op jit(solution)/shard_map/ppermute | solution.py:38
  69.5 0.0 copy-start.2
  69.5 0.6 copy-done.2
  70.2 3.9 %all-to-all-done.2.near = bf16[16,64,384]{2,1,0:T(8,128)(2,1)S(1)} async-done(((bf16[16,64,384]{2,1,0:T(8,128)(2,1)}), bf16[16,64,384]{2,1,0:T(8,128)(2,1)S(1)}, u32[]{:S(2)}, u32[]{:S(2)}) %all-to-all-start.2) | async-done | bytes 786464 | tf_op jit(solution)/shard_map/all_to_all | solution.py:393
  74.0 3.1 %collective-permute-start.6 = (bf16[16,64,384]{2,1,0:T(8,128)(2,1)S(1)}, bf16[16,64,384]{2,1,0:T(8,128)(2,1)S(1)}, u32[]{:S(2)}, u32[]{:S(2)}) collective-permute-start(bf16[16,64,384]{2,1,0:T(8,128)(2,1)S(1)} %all-to-all-done.2.near), channel_id=1, source_target_pairs={{0,1},{1,0},{2,3},{3,2},{4,5},{5,4},{6,7},{7,6},{8,9},{9,8},{10,11... | collective-permute-start | bytes 2359304 | tf_op jit(solution)/shard_map/ppermute | solution.py:38
  77.2 0.7 collective-permute-start.4
  77.9 0.0 copy-done.7
  77.9 4.8 %collective-permute-start.5 = (bf16[112,512]{1,0:T(8,128)(2,1)}, bf16[112,512]{1,0:T(8,128)(2,1)}, u32[]{:S(2)}, u32[]{:S(2)}) collective-permute-start(bf16[112,512]{1,0:T(8,128)(2,1)} %get-tuple-element.48), channel_id=1, source_target_pairs={{0,2},{1,3},{2,0},{3,1},{4,6},{5,7},{6,4},{7,5},{8,10},{9,11},{10,... | collective-permute-start | bytes 344072 | tf_op jit(solution)/shard_map/ppermute | solution.py:38
  82.7 0.1 copy.6.point_col
  82.9 0.2 copy.9
  83.1 0.0 collective-permute-done.6.far
  83.1 0.0 copy-start.3
  83.1 22.9 %solve.1 = (bf16[256,1024]{1,0:T(8,128)(2,1)S(1)}, f32[1024,1]{1,0:T(8,128)S(1)}) custom-call(bf16[16,64,384]{2,1,0:T(8,128)(2,1)S(1)} %all-to-all-done.2.near, bf16[16,64,384]{2,1,0:T(8,128)(2,1)S(1)} %collective-permute-done.6.far, s32[1,512]{1,0:T(1,128)S(1)} %get-tuple-element.61.point_row, s32[512,1]{1,0:T(8,128)S(1)} %copy.6.point_col), custom_call_target="tpu_custom_call" | custom-call | flops 1048576 | bytes 1048576 | tf_op jit(solution)/shard_map/solve/pallas_call | solution.py:286
  106.1 1.9 %collective-permute-done.5.a3 = bf16[112,512]{1,0:T(8,128)(2,1)} collective-permute-done((bf16[112,512]{1,0:T(8,128)(2,1)}, bf16[112,512]{1,0:T(8,128)(2,1)}, u32[]{:S(2)}, u32[]{:S(2)}) %collective-permute-start.5) | collective-permute-done | bytes 114720 | tf_op jit(solution)/shard_map/ppermute | solution.py:38
  108.0 0.0 collective-permute-done.4.s3
  108.0 0.0 copy-done.3
  108.0 0.0 copy-start
  108.0 0.0 copy-start.1
  108.0 9.1 %update.1 = (f32[2,40,2048]{2,1,0:T(8,128)S(1)}, f32[2,40,2048]{2,1,0:T(8,128)S(1)}) custom-call(bf16[112,2048]{1,0:T(8,128)(2,1)S(1)} %get-tuple-element.55.s0, bf16[112,2048]{1,0:T(8,128)(2,1)S(1)} %collective-permute-done.1.s2, bf16[112,2048]{1,0:T(8,128)(2,1)} %collective-permute-done.4.s3, bf16[112,512]{1,0:T(8,128)(2,1)S(1)} %collective-permute-done.a0, ...), custom_call_target="tpu_custom_call" | custom-call | tf_op jit(solution)/shard_map/update/pallas_call | solution.py:341
  117.2 0.0 copy-start.4
  117.2 1.2 collective-permute-start.7
  118.4 1.7 %collective-permute-done.7.got = f32[2,40,2048]{2,1,0:T(8,128)S(1)} collective-permute-done((f32[2,40,2048]{2,1,0:T(8,128)S(1)}, f32[2,40,2048]{2,1,0:T(8,128)S(1)}, u32[]{:S(2)}, u32[]{:S(2)}) %collective-permute-start.7) | collective-permute-done | bytes 655392 | tf_op jit(solution)/shard_map/ppermute | solution.py:38
  120.1 0.0 copy-done
  120.1 0.0 copy-done.1
  120.1 0.0 copy-done.4
  120.1 1.8 %finish.1 = (f32[37,4096]{1,0:T(8,128)}, f32[37,4096]{1,0:T(8,128)}) custom-call(s32[3]{0:T(128)S(1)} %copy-done.4, f32[37,4096]{1,0:T(8,128)S(1)} %copy-done, f32[37,4096]{1,0:T(8,128)S(1)} %copy-done.1, f32[2,40,2048]{2,1,0:T(8,128)S(1)} %get-tuple-element.52.mine, f32[2,40,2048]{2,1,0:T(8,128)S(1)} %collective-permute-done.7.got), custom_call_target="tpu_custom_call" | custom-call | tf_op jit(solution)/shard_map/finish/pallas_call | solution.py:362
  (3 shorter events, 0.0 us)
Async XLA Ops:
  2.4 13.9 %collective-permute-start = (bf16[112,512]{1,0:T(8,128)(2,1)S(1)}, bf16[112,512]{1,0:T(8,128)(2,1)S(1)}, u32[]{:S(2)}, u32[]{:S(2)}) collective-permute-start(bf16[112,512]{1,0:T(8,128)(2,1)S(1)} %get-tuple-element.59), channel_id=1, source_target_pairs={{0,2},{1,3},{2,0},{3,1},{4,6},{5,7},{6,4},{7,5},{8,10},{9,11},{10,... | collective-permute-start | bytes 344072 | tf_op jit(solution)/shard_map/ppermute | solution.py:38
  16.4 6.9 %copy-start.5 = (bf16[112,4096]{1,0:T(8,128)(2,1)S(1)}, bf16[112,4096]{1,0:T(8,128)(2,1)}, u32[]{:S(2)}) copy-start(bf16[112,4096]{1,0:T(8,128)(2,1)} %frames.1) | copy-start | bytes 2752516
  16.4 17.3 %all-to-all-start = ((bf16[16,64,256]{2,1,0:T(8,128)(2,1)}), bf16[16,64,256]{2,1,0:T(8,128)(2,1)S(1)}, u32[]{:S(2)}, u32[]{:S(2)}) async-start(bf16[16,64,256]{2,1,0:T(8,128)(2,1)} %pick.1), calls=%async_computation | async-start | bytes 1048576 | tf_op jit(solution)/shard_map/all_to_all | solution.py:388
  24.1 12.1 %collective-permute-start.1 = (bf16[112,2048]{1,0:T(8,128)(2,1)}, bf16[112,2048]{1,0:T(8,128)(2,1)S(1)}, u32[]{:S(2)}, u32[]{:S(2)}) collective-permute-start(bf16[112,2048]{1,0:T(8,128)(2,1)} %get-tuple-element.44), channel_id=1, source_target_pairs={{0,1},{1,0},{2,3},{3,2},{4,5},{5,4},{6,7},{7,6},{8,9},{9,8},{10,11... | collective-permute-start | bytes 1376264 | tf_op jit(solution)/shard_map/ppermute | solution.py:38
  25.4 10.9 %collective-permute-start.2 = (bf16[112,512]{1,0:T(8,128)(2,1)S(1)}, bf16[112,512]{1,0:T(8,128)(2,1)S(1)}, u32[]{:S(2)}, u32[]{:S(2)}) collective-permute-start(bf16[112,512]{1,0:T(8,128)(2,1)S(1)} %get-tuple-element.30), channel_id=1, source_target_pairs={{0,2},{1,3},{2,0},{3,1},{4,6},{5,7},{6,4},{7,5},{8,10},{9,11},{10,... | collective-permute-start | bytes 344072 | tf_op jit(solution)/shard_map/ppermute | solution.py:38
  33.6 0.8 copy-start.6
  54.0 23.9 %copy-start.7 = (s32[2,512]{1,0:T(2,128)S(1)}, s32[2,512]{1,0:T(2,128)}, u32[]{:S(2)}) copy-start(s32[2,512]{1,0:T(2,128)} %index.1) | copy-start | bytes 12292
  54.0 20.0 %all-to-all-start.2 = ((bf16[16,64,384]{2,1,0:T(8,128)(2,1)}), bf16[16,64,384]{2,1,0:T(8,128)(2,1)S(1)}, u32[]{:S(2)}, u32[]{:S(2)}) async-start(bf16[16,64,384]{2,1,0:T(8,128)(2,1)} %mix.1), calls=%async_computation.2 | async-start | bytes 1572864 | tf_op jit(solution)/shard_map/all_to_all | solution.py:393
  61.8 7.7 %collective-permute-start.3 = (bf16[112,512]{1,0:T(8,128)(2,1)S(1)}, bf16[112,512]{1,0:T(8,128)(2,1)S(1)}, u32[]{:S(2)}, u32[]{:S(2)}) collective-permute-start(bf16[112,512]{1,0:T(8,128)(2,1)S(1)} %get-tuple-element.41), channel_id=1, source_target_pairs={{0,2},{1,3},{2,0},{3,1},{4,6},{5,7},{6,4},{7,5},{8,10},{9,11},{10,... | collective-permute-start | bytes 344072 | tf_op jit(solution)/shard_map/ppermute | solution.py:38
  69.5 0.6 copy-start.2
  74.0 9.1 %collective-permute-start.6 = (bf16[16,64,384]{2,1,0:T(8,128)(2,1)S(1)}, bf16[16,64,384]{2,1,0:T(8,128)(2,1)S(1)}, u32[]{:S(2)}, u32[]{:S(2)}) collective-permute-start(bf16[16,64,384]{2,1,0:T(8,128)(2,1)S(1)} %all-to-all-done.2.near), channel_id=1, source_target_pairs={{0,1},{1,0},{2,3},{3,2},{4,5},{5,4},{6,7},{7,6},{8,9},{9,8},{10,11... | collective-permute-start | bytes 2359304 | tf_op jit(solution)/shard_map/ppermute | solution.py:38
  77.2 30.8 %collective-permute-start.4 = (bf16[112,2048]{1,0:T(8,128)(2,1)}, bf16[112,2048]{1,0:T(8,128)(2,1)}, u32[]{:S(2)}, u32[]{:S(2)}) collective-permute-start(bf16[112,2048]{1,0:T(8,128)(2,1)} %get-tuple-element.44), channel_id=1, source_target_pairs={{0,3},{1,2},{2,1},{3,0},{4,7},{5,6},{6,5},{7,4},{8,11},{9,10},{10,... | collective-permute-start | bytes 1376264 | tf_op jit(solution)/shard_map/ppermute | solution.py:38
  77.9 30.1 %collective-permute-start.5 = (bf16[112,512]{1,0:T(8,128)(2,1)}, bf16[112,512]{1,0:T(8,128)(2,1)}, u32[]{:S(2)}, u32[]{:S(2)}) collective-permute-start(bf16[112,512]{1,0:T(8,128)(2,1)} %get-tuple-element.48), channel_id=1, source_target_pairs={{0,2},{1,3},{2,0},{3,1},{4,6},{5,7},{6,4},{7,5},{8,10},{9,11},{10,... | collective-permute-start | bytes 344072 | tf_op jit(solution)/shard_map/ppermute | solution.py:38
  83.1 24.9 %copy-start.3 = (bf16[112,512]{1,0:T(8,128)(2,1)S(1)}, bf16[112,512]{1,0:T(8,128)(2,1)}, u32[]{:S(2)}) copy-start(bf16[112,512]{1,0:T(8,128)(2,1)} %copy-done.2) | copy-start | bytes 344068
  108.0 12.1 %copy-start = (f32[37,4096]{1,0:T(8,128)S(1)}, f32[37,4096]{1,0:T(8,128)}, u32[]{:S(2)}) copy-start(f32[37,4096]{1,0:T(8,128)} %residual.3) | copy-start | bytes 1818628
  108.0 12.1 %copy-start.1 = (f32[37,4096]{1,0:T(8,128)S(1)}, f32[37,4096]{1,0:T(8,128)}, u32[]{:S(2)}) copy-start(f32[37,4096]{1,0:T(8,128)} %coefficients.1) | copy-start | bytes 1818628
  117.2 2.9 %copy-start.4 = (s32[3]{0:T(128)S(1)}, s32[3]{0:T(128)}, u32[]{:S(2)}) copy-start(s32[3]{0:T(128)} %pad_add_fusion.place) | copy-start | bytes 40
  117.2 2.9 %collective-permute-start.7 = (f32[2,40,2048]{2,1,0:T(8,128)S(1)}, f32[2,40,2048]{2,1,0:T(8,128)S(1)}, u32[]{:S(2)}, u32[]{:S(2)}) collective-permute-start(f32[2,40,2048]{2,1,0:T(8,128)S(1)} %get-tuple-element.53), channel_id=1, source_target_pairs={{0,1},{1,0},{2,3},{3,2},{4,5},{5,4},{6,7},{7,6},{8,9},{9,8},{10,11... | collective-permute-start | bytes 1966088 | tf_op jit(solution)/shard_map/ppermute | solution.py:38

commit v5 on v4

--- a/solution.py
+++ b/solution.py
@@ -300,9 +300,8 @@
     )(near, far, chosen[1].reshape(1, BLOCK), chosen[0].reshape(BLOCK, 1))
 
 
-def update_kernel(s0, s2, s3, a0, a1, a2, a3, near, far, delta, sq, local, mine_ref, theirs_ref):
-    pieces = [jnp.concatenate([one[...], two[...]], axis=1) for one, two in ((a0, a1), (a2, a3))]
-    s1 = jnp.where(pl.program_id(0) == 0, *pieces)
+def update_kernel(s0, s2, s3, a0, a1, a2, near, far, delta, sq, local, mine_ref, theirs_ref):
+    s1 = jnp.where(pl.program_id(0) == 0, jnp.concatenate([a0[...], a1[...]], axis=1), a2[...])
 
     def squares(ref):
         value = ref[...].astype(F32)
@@ -341,7 +340,7 @@
     return pl.pallas_call(
         update_kernel,
         grid=(rows // TILE,),
-        in_specs=[pl.BlockSpec((112, TILE), lambda i: (0, i))] * 3 + [whole] * 9,
+        in_specs=[pl.BlockSpec((112, TILE), lambda i: (0, i))] * 3 + [whole] * 8,
         out_specs=[pl.BlockSpec((2, 40, TILE), lambda i: (0, 0, i))] * 2,
         out_shape=[jax.ShapeDtypeStruct((2, 40, rows), F32)] * 2,
         compiler_params=pltpu.CompilerParams(vmem_limit_bytes=40 << 20),
@@ -379,21 +378,19 @@
     other_half = lax.dynamic_slice_in_dim(frames, (1 - c) * (rows // 2), rows // 2, axis=1)
     beside = swap(other_half, 0, 1)
     size = rows // 8
-    own = [lax.dynamic_slice_in_dim(frames, c * (rows // 2) + i * size, size, axis=1) for i in range(4)]
+    own = [own_half[:, :size], own_half[:, size : 2 * size], own_half[:, 2 * size :]]
     across = [swap(own[0], 1, 0)]
 
     held = pick(place, block_index, frames, residual)
-    held, across, own = lax.optimization_barrier((held, across, own))
-    across.append(swap(own[1], 1, 0))
     held = add(lax.all_to_all(held, "dp", 0, 0, axis_index_groups=PLANE, tiled=True))
     held, beside, across, own, other_half = lax.optimization_barrier((held, beside, across, own, other_half))
     held = lax.all_to_all(held, AXES, 0, 0, axis_index_groups=LINE, tiled=True)
     held, own, other_half = lax.optimization_barrier((held, own, other_half))
-    across.append(swap(own[2], 1, 0))
+    across.append(swap(own[1], 1, 0))
     near = lax.all_to_all(mix(place, held), "dp", 0, 0, axis_index_groups=PLANE, tiled=True)
     near, across, own, other_half = lax.optimization_barrier((near, across, own, other_half))
     far = swap(near, 0, 1)
-    across.append(swap(own[3], 1, 0))
+    across.append(swap(own[2], 1, 0))
     diagonal = swap(other_half, 1, 1)
 
     delta, sq = solve(near, far, block_index)

time: 122 us -> 120 us (0.984)
  starting transfers between devices: 38.4 us -> 34.6 us
  blocking collectives: 15.8 us -> 17.8 us
    ppermute x8 -> x7, waiting for transfers between devices: 10.4 us -> 14.7 us  [swap(): return lax.ppermute(value, AXES, permutation(move))]
    ppermute x8 -> x7, starting transfers between devices: 23.7 us -> 19.6 us  [swap(): return lax.ppermute(value, AXES, permutation(move))]
    all_to_all x1, waiting for transfers between devices: 4.33 us -> 0.97 us  [on_device(): lax.all_to_all(held, 'dp', 0, 0, axis_index_groups=PLANE, tiled=True)]
    all_to_all x1, blocking collectives: 15.8 us -> 17.8 us  [on_device(): held = lax.all_to_all(held, AXES, 0, 0, axis_index_groups=LINE, tiled=True)]
    dynamic_slice x1 -> x0, local copies, waits for them, and re-layouts: 1.76 us -> none  [on_device(): lax.dynamic_slice_in_dim(frames, c * (rows // 2) + i * size, size, axis=1)]
  transfers between devices with their start and end apart: 10 -> 9, of which waited for: 5 -> 5; matrix products, arithmetic and copies ran while one was open for 2% -> 2% of each run, Pallas kernels for 25% -> 21%
where the time goes in v5:
time: 120 us
  Pallas kernels  43.1 us (36%)
  starting transfers between devices  34.6 us (29%)
  waiting for transfers between devices  19.2 us (16%)
  blocking collectives  17.8 us (15%)
  local copies, waits for them, and re-layouts  3.43 us (3%)
    pallas_call x1, Pallas kernels, solve(): pl.pallas_call(solve_kernel, out_shape=(jax.ShapeDtypeStruct((256, STEPS...  23 us
    ppermute x7, starting transfers between devices, swap(): return lax.ppermute(value, AXES, permutation(move))  19.6 us
    all_to_all x1, blocking collectives, on_device(): held = lax.all_to_all(held, AXES, 0, 0, axis_index_groups=LINE, tiled=True)  17.8 us
    ppermute x7, waiting for transfers between devices, swap(): return lax.ppermute(value, AXES, permutation(move))  14.7 us
    pallas_call x1, Pallas kernels, update(): pl.pallas_call(update_kernel, grid=(rows // TILE,), in_specs=[pl.BlockSpe...  9.05 us
    all_to_all x1, starting transfers between devices, on_device(): lax.all_to_all(held, 'dp', 0, 0, axis_index_groups=PLANE, tiled=True)  7.72 us
    all_to_all x1, starting transfers between devices, on_device(): lax.all_to_all(mix(place, held), 'dp', 0, 0, axis_index_groups=PLANE, til...  7.27 us
    pallas_call x1, Pallas kernels, pick(): pl.pallas_call(pick_kernel, grid=(frames.shape[1] // PICK,), in_specs=[pl...  5.58 us
  transfers between devices with their start and end apart: 9, of which 5 were waited for; matrix products, arithmetic and copies ran while one was open for 2% of the time, Pallas kernels for 21%

profile of v5, /device:TPU:1, one launch (start us, length us, event | category | flops | bytes accessed | tf_op | source)
XLA Modules:
  0.0 119.6 jit_solution(8093147374167644282)
XLA Ops:
  0.6 0.6 pad_add_fusion.place
  1.3 5.6 %pick.1 = bf16[16,64,256]{2,1,0:T(8,128)(2,1)} custom-call(s32[3]{0:T(128)} %pad_add_fusion.place, s32[2,512]{1,0:T(2,128)} %index.1, bf16[112,4096]{1,0:T(8,128)(2,1)} %frames.1, f32[37,4096]{1,0:T(8,128)} %residual.3), custom_call_target="tpu_custom_call" | custom-call | tf_op jit(solution)/shard_map/pick/pallas_call | solution.py:174
  6.8 0.0 copy-start.7
  6.8 7.7 %all-to-all-start = ((bf16[16,64,256]{2,1,0:T(8,128)(2,1)}), bf16[16,64,256]{2,1,0:T(8,128)(2,1)S(1)}, u32[]{:S(2)}, u32[]{:S(2)}) async-start(bf16[16,64,256]{2,1,0:T(8,128)(2,1)} %pick.1), calls=%async_computation | async-start | bytes 1048576 | tf_op jit(solution)/shard_map/all_to_all | solution.py:385
  14.6 0.0 copy-done.7
  14.6 0.9 constant_dynamic-slice_fusion.3
  15.4 1.0 collective-permute-start
  16.4 7.0 %collective-permute-start.1 = (bf16[112,512]{1,0:T(8,128)(2,1)S(1)}, bf16[112,512]{1,0:T(8,128)(2,1)S(1)}, u32[]{:S(2)}, u32[]{:S(2)}) collective-permute-start(bf16[112,512]{1,0:T(8,128)(2,1)S(1)} %get-tuple-element.41), channel_id=1, source_target_pairs={{0,2},{1,3},{2,0},{3,1},{4,6},{5,7},{6,4},{7,5},{8,10},{9,11},{10,... | collective-permute-start | bytes 344072 | tf_op jit(solution)/shard_map/ppermute | solution.py:38
  23.4 0.7 constant_dynamic-slice_fusion
  24.1 1.0 all-to-all-done.held
  25.1 0.0 copy-start.8
  25.1 0.8 copy-done.8
  25.9 1.8 %add.21 = bf16[8,64,256]{2,1,0:T(8,128)(2,1)} custom-call(bf16[16,64,256]{2,1,0:T(8,128)(2,1)} %copy-done.8), custom_call_target="tpu_custom_call" | custom-call | tf_op jit(solution)/shard_map/add/pallas_call | solution.py:201
  27.7 0.0 collective-permute-done.1.a0
  27.7 0.0 copy-start.2
  27.7 0.0 collective-permute-done.s2
  27.7 17.8 %all_to_all.15.held = bf16[8,64,256]{2,1,0:T(8,128)(2,1)} all-to-all(bf16[8,64,256]{2,1,0:T(8,128)(2,1)} %add.21), channel_id=1, replica_groups={{0,4,8,12,2,6,10,14},{1,5,9,13,3,7,11,15},{16,20,24,28,18,22,26,30},{17..., dimensions={0} | all-to-all | bytes 524288 | tf_op jit(solution)/shard_map/all_to_all | solution.py:387
  45.5 0.0 copy-done.2
  45.5 2.0 %mix.1 = bf16[16,64,384]{2,1,0:T(8,128)(2,1)} custom-call(s32[3]{0:T(128)} %pad_add_fusion.place, bf16[8,64,256]{2,1,0:T(8,128)(2,1)} %all_to_all.15.held), custom_call_target="tpu_custom_call" | custom-call | tf_op jit(solution)/shard_map/mix/pallas_call | solution.py:224
  47.5 7.3 %all-to-all-start.2 = ((bf16[16,64,384]{2,1,0:T(8,128)(2,1)}), bf16[16,64,384]{2,1,0:T(8,128)(2,1)S(1)}, u32[]{:S(2)}, u32[]{:S(2)}) async-start(bf16[16,64,384]{2,1,0:T(8,128)(2,1)} %mix.1), calls=%async_computation.2 | async-start | bytes 1572864 | tf_op jit(solution)/shard_map/all_to_all | solution.py:390
  54.7 1.7 %collective-permute-start.2 = (bf16[112,512]{1,0:T(8,128)(2,1)S(1)}, bf16[112,512]{1,0:T(8,128)(2,1)S(1)}, u32[]{:S(2)}, u32[]{:S(2)}) collective-permute-start(bf16[112,512]{1,0:T(8,128)(2,1)S(1)} %get-tuple-element.28), channel_id=1, source_target_pairs={{0,2},{1,3},{2,0},{3,1},{4,6},{5,7},{6,4},{7,5},{8,10},{9,11},{10,... | collective-permute-start | bytes 344072 | tf_op jit(solution)/shard_map/ppermute | solution.py:38
  56.4 6.0 %collective-permute-done.2.a1 = bf16[112,512]{1,0:T(8,128)(2,1)S(1)} collective-permute-done((bf16[112,512]{1,0:T(8,128)(2,1)S(1)}, bf16[112,512]{1,0:T(8,128)(2,1)S(1)}, u32[]{:S(2)}, u32[]{:S(2)}) %collective-permute-start.2) | collective-permute-done | bytes 114720 | tf_op jit(solution)/shard_map/ppermute | solution.py:38
  62.4 0.7 copy-done.4
  63.0 3.5 %all-to-all-done.2.near = bf16[16,64,384]{2,1,0:T(8,128)(2,1)S(1)} async-done(((bf16[16,64,384]{2,1,0:T(8,128)(2,1)}), bf16[16,64,384]{2,1,0:T(8,128)(2,1)S(1)}, u32[]{:S(2)}, u32[]{:S(2)}) %all-to-all-start.2) | async-done | bytes 786464 | tf_op jit(solution)/shard_map/all_to_all | solution.py:390
  66.6 3.6 %collective-permute-start.5 = (bf16[16,64,384]{2,1,0:T(8,128)(2,1)S(1)}, bf16[16,64,384]{2,1,0:T(8,128)(2,1)S(1)}, u32[]{:S(2)}, u32[]{:S(2)}) collective-permute-start(bf16[16,64,384]{2,1,0:T(8,128)(2,1)S(1)} %all-to-all-done.2.near), channel_id=1, source_target_pairs={{0,1},{1,0},{2,3},{3,2},{4,5},{5,4},{6,7},{7,6},{8,9},{9,8},{10,11... | collective-permute-start | bytes 2359304 | tf_op jit(solution)/shard_map/ppermute | solution.py:38
  70.1 1.4 %collective-permute-start.3 = (bf16[112,2048]{1,0:T(8,128)(2,1)}, bf16[112,2048]{1,0:T(8,128)(2,1)}, u32[]{:S(2)}, u32[]{:S(2)}) collective-permute-start(bf16[112,2048]{1,0:T(8,128)(2,1)} %get-tuple-element.31), channel_id=1, source_target_pairs={{0,3},{1,2},{2,1},{3,0},{4,7},{5,6},{6,5},{7,4},{8,11},{9,10},{10,... | collective-permute-start | bytes 1376264 | tf_op jit(solution)/shard_map/ppermute | solution.py:38
  71.5 3.9 %collective-permute-start.4 = (bf16[112,1024]{1,0:T(8,128)(2,1)}, bf16[112,1024]{1,0:T(8,128)(2,1)S(1)}, u32[]{:S(2)}, u32[]{:S(2)}) collective-permute-start(bf16[112,1024]{1,0:T(8,128)(2,1)} %constant_dynamic-slice_fusion), channel_id=1, source_target_pairs={{0,2},{1,3},{2,0},{3,1},{4,6},{5,7},{6,4},{7,5},{8,10},{9,11},{10,... | collective-permute-start | bytes 688136 | tf_op jit(solution)/shard_map/ppermute | solution.py:38
  75.4 0.0 copy-done.9
  75.4 0.1 copy.6.point_col
  75.6 0.2 copy.9
  75.8 0.0 collective-permute-done.5.far
  75.8 0.0 copy-start.3
  75.8 0.0 copy-start.5
  75.8 23.0 %solve.1 = (bf16[256,1024]{1,0:T(8,128)(2,1)S(1)}, f32[1024,1]{1,0:T(8,128)S(1)}) custom-call(bf16[16,64,384]{2,1,0:T(8,128)(2,1)S(1)} %all-to-all-done.2.near, bf16[16,64,384]{2,1,0:T(8,128)(2,1)S(1)} %collective-permute-done.5.far, s32[1,512]{1,0:T(1,128)S(1)} %get-tuple-element.45.point_row, s32[512,1]{1,0:T(8,128)S(1)} %copy.6.point_col), custom_call_target="tpu_custom_call" | custom-call | flops 1048576 | bytes 1048576 | tf_op jit(solution)/shard_map/solve/pallas_call | solution.py:286
  98.8 7.0 %collective-permute-done.4.a2 = bf16[112,1024]{1,0:T(8,128)(2,1)S(1)} collective-permute-done((bf16[112,1024]{1,0:T(8,128)(2,1)}, bf16[112,1024]{1,0:T(8,128)(2,1)S(1)}, u32[]{:S(2)}, u32[]{:S(2)}) %collective-permute-start.4) | collective-permute-done | bytes 229408 | tf_op jit(solution)/shard_map/ppermute | solution.py:38
  105.8 0.0 collective-permute-done.3.s3
  105.8 0.0 copy-done.3
  105.8 0.0 copy-done.5
  105.8 0.0 copy-start
  105.8 0.0 copy-start.1
  105.8 9.0 %update.1 = (f32[2,40,2048]{2,1,0:T(8,128)S(1)}, f32[2,40,2048]{2,1,0:T(8,128)S(1)}) custom-call(bf16[112,2048]{1,0:T(8,128)(2,1)S(1)} %get-tuple-element.43.s0, bf16[112,2048]{1,0:T(8,128)(2,1)S(1)} %collective-permute-done.s2, bf16[112,2048]{1,0:T(8,128)(2,1)} %collective-permute-done.3.s3, bf16[112,512]{1,0:T(8,128)(2,1)S(1)} %copy-done.3, ...), custom_call_target="tpu_custom_call" | custom-call | tf_op jit(solution)/shard_map/update/pallas_call | solution.py:340
  114.9 0.0 copy-start.6
  114.9 1.2 collective-permute-start.6
  116.1 1.7 %collective-permute-done.6.got = f32[2,40,2048]{2,1,0:T(8,128)S(1)} collective-permute-done((f32[2,40,2048]{2,1,0:T(8,128)S(1)}, f32[2,40,2048]{2,1,0:T(8,128)S(1)}, u32[]{:S(2)}, u32[]{:S(2)}) %collective-permute-start.6) | collective-permute-done | bytes 655392 | tf_op jit(solution)/shard_map/ppermute | solution.py:38
  117.8 0.0 copy-done
  117.8 0.0 copy-done.1
  117.8 0.0 copy-done.6
  117.8 1.8 %finish.1 = (f32[37,4096]{1,0:T(8,128)}, f32[37,4096]{1,0:T(8,128)}) custom-call(s32[3]{0:T(128)S(1)} %copy-done.6, f32[37,4096]{1,0:T(8,128)S(1)} %copy-done, f32[37,4096]{1,0:T(8,128)S(1)} %copy-done.1, f32[2,40,2048]{2,1,0:T(8,128)S(1)} %get-tuple-element.38.mine, f32[2,40,2048]{2,1,0:T(8,128)S(1)} %collective-permute-done.6.got), custom_call_target="tpu_custom_call" | custom-call | tf_op jit(solution)/shard_map/finish/pallas_call | solution.py:361
  (6 shorter events, 0.0 us)
Async XLA Ops:
  6.8 7.7 %copy-start.7 = (bf16[112,4096]{1,0:T(8,128)(2,1)S(1)}, bf16[112,4096]{1,0:T(8,128)(2,1)}, u32[]{:S(2)}) copy-start(bf16[112,4096]{1,0:T(8,128)(2,1)} %frames.1) | copy-start | bytes 2752516
  6.8 18.2 %all-to-all-start = ((bf16[16,64,256]{2,1,0:T(8,128)(2,1)}), bf16[16,64,256]{2,1,0:T(8,128)(2,1)S(1)}, u32[]{:S(2)}, u32[]{:S(2)}) async-start(bf16[16,64,256]{2,1,0:T(8,128)(2,1)} %pick.1), calls=%async_computation | async-start | bytes 1048576 | tf_op jit(solution)/shard_map/all_to_all | solution.py:385
  15.4 12.3 %collective-permute-start = (bf16[112,2048]{1,0:T(8,128)(2,1)}, bf16[112,2048]{1,0:T(8,128)(2,1)S(1)}, u32[]{:S(2)}, u32[]{:S(2)}) collective-permute-start(bf16[112,2048]{1,0:T(8,128)(2,1)} %get-tuple-element.31), channel_id=1, source_target_pairs={{0,1},{1,0},{2,3},{3,2},{4,5},{5,4},{6,7},{7,6},{8,9},{9,8},{10,11... | collective-permute-start | bytes 1376264 | tf_op jit(solution)/shard_map/ppermute | solution.py:38
  16.4 11.3 %collective-permute-start.1 = (bf16[112,512]{1,0:T(8,128)(2,1)S(1)}, bf16[112,512]{1,0:T(8,128)(2,1)S(1)}, u32[]{:S(2)}, u32[]{:S(2)}) collective-permute-start(bf16[112,512]{1,0:T(8,128)(2,1)S(1)} %get-tuple-element.41), channel_id=1, source_target_pairs={{0,2},{1,3},{2,0},{3,1},{4,6},{5,7},{6,4},{7,5},{8,10},{9,11},{10,... | collective-permute-start | bytes 344072 | tf_op jit(solution)/shard_map/ppermute | solution.py:38
  25.1 0.8 copy-start.8
  27.7 17.8 %copy-start.2 = (bf16[112,512]{1,0:T(8,128)(2,1)}, bf16[112,512]{1,0:T(8,128)(2,1)S(1)}, u32[]{:S(2)}) copy-start(bf16[112,512]{1,0:T(8,128)(2,1)S(1)} %collective-permute-done.1.a0) | copy-start | bytes 344068
  47.5 27.9 %copy-start.9 = (s32[2,512]{1,0:T(2,128)S(1)}, s32[2,512]{1,0:T(2,128)}, u32[]{:S(2)}) copy-start(s32[2,512]{1,0:T(2,128)} %index.1) | copy-start | bytes 12292
  47.5 19.1 %all-to-all-start.2 = ((bf16[16,64,384]{2,1,0:T(8,128)(2,1)}), bf16[16,64,384]{2,1,0:T(8,128)(2,1)S(1)}, u32[]{:S(2)}, u32[]{:S(2)}) async-start(bf16[16,64,384]{2,1,0:T(8,128)(2,1)} %mix.1), calls=%async_computation.2 | async-start | bytes 1572864 | tf_op jit(solution)/shard_map/all_to_all | solution.py:390
  54.7 7.6 %collective-permute-start.2 = (bf16[112,512]{1,0:T(8,128)(2,1)S(1)}, bf16[112,512]{1,0:T(8,128)(2,1)S(1)}, u32[]{:S(2)}, u32[]{:S(2)}) collective-permute-start(bf16[112,512]{1,0:T(8,128)(2,1)S(1)} %get-tuple-element.28), channel_id=1, source_target_pairs={{0,2},{1,3},{2,0},{3,1},{4,6},{5,7},{6,4},{7,5},{8,10},{9,11},{10,... | collective-permute-start | bytes 344072 | tf_op jit(solution)/shard_map/ppermute | solution.py:38
  62.4 0.7 copy-start.4
  66.6 9.2 %collective-permute-start.5 = (bf16[16,64,384]{2,1,0:T(8,128)(2,1)S(1)}, bf16[16,64,384]{2,1,0:T(8,128)(2,1)S(1)}, u32[]{:S(2)}, u32[]{:S(2)}) collective-permute-start(bf16[16,64,384]{2,1,0:T(8,128)(2,1)S(1)} %all-to-all-done.2.near), channel_id=1, source_target_pairs={{0,1},{1,0},{2,3},{3,2},{4,5},{5,4},{6,7},{7,6},{8,9},{9,8},{10,11... | collective-permute-start | bytes 2359304 | tf_op jit(solution)/shard_map/ppermute | solution.py:38
  70.1 35.7 %collective-permute-start.3 = (bf16[112,2048]{1,0:T(8,128)(2,1)}, bf16[112,2048]{1,0:T(8,128)(2,1)}, u32[]{:S(2)}, u32[]{:S(2)}) collective-permute-start(bf16[112,2048]{1,0:T(8,128)(2,1)} %get-tuple-element.31), channel_id=1, source_target_pairs={{0,3},{1,2},{2,1},{3,0},{4,7},{5,6},{6,5},{7,4},{8,11},{9,10},{10,... | collective-permute-start | bytes 1376264 | tf_op jit(solution)/shard_map/ppermute | solution.py:38
  71.5 34.3 %collective-permute-start.4 = (bf16[112,1024]{1,0:T(8,128)(2,1)}, bf16[112,1024]{1,0:T(8,128)(2,1)S(1)}, u32[]{:S(2)}, u32[]{:S(2)}) collective-permute-start(bf16[112,1024]{1,0:T(8,128)(2,1)} %constant_dynamic-slice_fusion), channel_id=1, source_target_pairs={{0,2},{1,3},{2,0},{3,1},{4,6},{5,7},{6,4},{7,5},{8,10},{9,11},{10,... | collective-permute-start | bytes 688136 | tf_op jit(solution)/shard_map/ppermute | solution.py:38
  75.8 30.0 %copy-start.3 = (bf16[112,512]{1,0:T(8,128)(2,1)S(1)}, bf16[112,512]{1,0:T(8,128)(2,1)}, u32[]{:S(2)}) copy-start(bf16[112,512]{1,0:T(8,128)(2,1)} %copy-done.2) | copy-start | bytes 344068
  75.8 30.0 %copy-start.5 = (bf16[112,512]{1,0:T(8,128)(2,1)S(1)}, bf16[112,512]{1,0:T(8,128)(2,1)}, u32[]{:S(2)}) copy-start(bf16[112,512]{1,0:T(8,128)(2,1)} %copy-done.4) | copy-start | bytes 344068
  105.8 12.0 %copy-start = (f32[37,4096]{1,0:T(8,128)S(1)}, f32[37,4096]{1,0:T(8,128)}, u32[]{:S(2)}) copy-start(f32[37,4096]{1,0:T(8,128)} %residual.3) | copy-start | bytes 1818628
  105.8 12.0 %copy-start.1 = (f32[37,4096]{1,0:T(8,128)S(1)}, f32[37,4096]{1,0:T(8,128)}, u32[]{:S(2)}) copy-start(f32[37,4096]{1,0:T(8,128)} %coefficients.1) | copy-start | bytes 1818628
  114.9 2.9 %copy-start.6 = (s32[3]{0:T(128)S(1)}, s32[3]{0:T(128)}, u32[]{:S(2)}) copy-start(s32[3]{0:T(128)} %pad_add_fusion.place) | copy-start | bytes 40
  114.9 2.9 %collective-permute-start.6 = (f32[2,40,2048]{2,1,0:T(8,128)S(1)}, f32[2,40,2048]{2,1,0:T(8,128)S(1)}, u32[]{:S(2)}, u32[]{:S(2)}) collective-permute-start(f32[2,40,2048]{2,1,0:T(8,128)S(1)} %get-tuple-element.39), channel_id=1, source_target_pairs={{0,1},{1,0},{2,3},{3,2},{4,5},{5,4},{6,7},{7,6},{8,9},{9,8},{10,11... | collective-permute-start | bytes 1966088 | tf_op jit(solution)/shard_map/ppermute | solution.py:38

commit v6 on v5

--- a/solution.py
+++ b/solution.py
@@ -1,3 +1,4 @@
+import functools
 import math
 
 import jax
@@ -300,8 +301,9 @@
     )(near, far, chosen[1].reshape(1, BLOCK), chosen[0].reshape(BLOCK, 1))
 
 
-def update_kernel(s0, s2, s3, a0, a1, a2, near, far, delta, sq, local, mine_ref, theirs_ref):
-    s1 = jnp.where(pl.program_id(0) == 0, jnp.concatenate([a0[...], a1[...]], axis=1), a2[...])
+def update_kernel(part, s0, s2, s3, *refs):
+    *across, near, far, delta, sq, local, mine_ref, theirs_ref = refs
+    s1 = across[0][...] if len(across) == 1 else jnp.concatenate([one[...] for one in across], axis=1)
 
     def squares(ref):
         value = ref[...].astype(F32)
@@ -311,7 +313,7 @@
     pad = jnp.zeros((32, TILE), BF16)
     source_near = jnp.concatenate([s0[...], s1, pad], axis=0)
     source_far = jnp.concatenate([s2[...], s3[...], pad], axis=0)
-    positions = pl.program_id(0) * TILE + lax.broadcasted_iota(jnp.int32, (1, TILE), 1)
+    positions = part * TILE + lax.broadcasted_iota(jnp.int32, (1, TILE), 1)
     change = jnp.zeros((256, TILE), F32)
     placed = jnp.zeros((256, TILE), F32)
     size = 512
@@ -334,39 +336,40 @@
         out[1] = added
 
 
-def update(sources, across, near, far, delta, sq, local):
+def update(part, sources, across, near, far, delta, sq, local):
     whole = pl.BlockSpec(memory_space=pltpu.VMEM)
-    rows = sources[0].shape[1]
     return pl.pallas_call(
-        update_kernel,
-        grid=(rows // TILE,),
-        in_specs=[pl.BlockSpec((112, TILE), lambda i: (0, i))] * 3 + [whole] * 8,
-        out_specs=[pl.BlockSpec((2, 40, TILE), lambda i: (0, 0, i))] * 2,
-        out_shape=[jax.ShapeDtypeStruct((2, 40, rows), F32)] * 2,
+        functools.partial(update_kernel, part),
+        grid=(1,),
+        in_specs=[pl.BlockSpec((112, TILE), lambda i: (0, part))] * 3 + [whole] * (len(across) + 5),
+        out_specs=[whole] * 2,
+        out_shape=[jax.ShapeDtypeStruct((2, 40, TILE), F32)] * 2,
         compiler_params=pltpu.CompilerParams(vmem_limit_bytes=40 << 20),
         name="update",
     )(*sources, *across, near, far, delta, sq, local)
 
 
-def finish_kernel(place, residual, coefficients, mine, got, res_out, coef_out):
+def finish_kernel(place, residual, coefficients, mine0, mine1, got0, got1, res_out, coef_out):
     own = pl.program_id(0) == place[1]
-    value = jnp.where(own, mine[...], got[...])
-    res_out[...] = residual[...] - value[0, :ROWS]
-    coef_out[...] = coefficients[...] + value[1, :ROWS]
-
-
-def finish(place, residual, coefficients, mine, got):
+    for i, (mine, got) in enumerate(((mine0, got0), (mine1, got1))):
+        at = slice(TILE * i, TILE * i + TILE)
+        value = jnp.where(own, mine[...], got[...])
+        res_out[:, at] = residual[:, at] - value[0, :ROWS]
+        coef_out[:, at] = coefficients[:, at] + value[1, :ROWS]
+
+
+def finish(place, residual, coefficients, *parts):
     whole = pl.BlockSpec(memory_space=pltpu.VMEM)
     half = pl.BlockSpec((ROWS, residual.shape[1] // 2), lambda i: (0, i))
     return pl.pallas_call(
         finish_kernel,
         grid=(2,),
-        in_specs=[pl.BlockSpec(memory_space=pltpu.SMEM), half, half, whole, whole],
+        in_specs=[pl.BlockSpec(memory_space=pltpu.SMEM), half, half] + [whole] * 4,
         out_specs=[half, half],
         out_shape=[jax.ShapeDtypeStruct(residual.shape, F32)] * 2,
         compiler_params=pltpu.CompilerParams(vmem_limit_bytes=40 << 20),
         name="finish",
-    )(place, residual, coefficients, mine, got)
+    )(place, residual, coefficients, *parts)
 
 
 def on_device(frames, residual, coefficients, block_index):
@@ -395,8 +398,13 @@
 
     delta, sq = solve(near, far, block_index)
     local = block_index.reshape(-1, 1) - dp * rows - c * (rows // 2)
-    mine, theirs = update((own_half, beside, diagonal), across, near, far, delta, sq, local)
-    return finish(place, residual, coefficients, mine, swap(theirs, 0, 1))
+    sources = own_half, beside, diagonal
+    mine0, theirs0 = update(0, sources, across[:2], near, far, delta, sq, local)
+    near, mine0, theirs0 = lax.optimization_barrier((near, mine0, theirs0))
+    got0 = swap(theirs0, 0, 1)
+    mine1, theirs1 = update(1, sources, across[2:], near, far, delta, sq, local)
+    got1 = swap(theirs1, 0, 1)
+    return finish(place, residual, coefficients, mine0, mine1, got0, got1)
 
 
 def solution(mesh):

time: 120 us -> 116 us (0.967)
  waiting for transfers between devices: 19.2 us -> 13.6 us
  local copies, waits for them, and re-layouts: 3.43 us -> 5.06 us
    ppermute x7 -> x8, waiting for transfers between devices: 14.7 us -> 9.1 us  [swap(): return lax.ppermute(value, AXES, permutation(move))]
    unnamed x22 -> x24, local copies, waits for them, and re-layouts: 1.72 us -> 2.63 us
    ppermute x7 -> x8, starting transfers between devices: 19.6 us -> 19.7 us  [swap(): return lax.ppermute(value, AXES, permutation(move))]
    pallas_call x1 -> x2, Pallas kernels: 9.05 us -> 9.09 us  [update(): pl.pallas_call(functools.partial(update_kernel, part), grid=(1,), in_spec...]
  transfers between devices with their start and end apart: 9 -> 10, of which waited for: 5 -> 6; matrix products, arithmetic and copies ran while one was open for 2% -> 2% of each run, Pallas kernels for 21% -> 25%
where the time goes in v6:
time: 116 us
  Pallas kernels  43.2 us (37%)
  starting transfers between devices  34.6 us (30%)
  blocking collectives  17.8 us (15%)
  waiting for transfers between devices  13.6 us (12%)
  local copies, waits for them, and re-layouts  5.06 us (4%)
    pallas_call x1, Pallas kernels, solve(): pl.pallas_call(solve_kernel, out_shape=(jax.ShapeDtypeStruct((256, STEPS...  23 us
    ppermute x8, starting transfers between devices, swap(): return lax.ppermute(value, AXES, permutation(move))  19.7 us
    all_to_all x1, blocking collectives, on_device(): held = lax.all_to_all(held, AXES, 0, 0, axis_index_groups=LINE, tiled=True)  17.8 us
    ppermute x8, waiting for transfers between devices, swap(): return lax.ppermute(value, AXES, permutation(move))  9.1 us
    pallas_call x2, Pallas kernels, update(): pl.pallas_call(functools.partial(update_kernel, part), grid=(1,), in_spec...  9.09 us
    all_to_all x1, starting transfers between devices, on_device(): lax.all_to_all(held, 'dp', 0, 0, axis_index_groups=PLANE, tiled=True)  7.72 us
    all_to_all x1, starting transfers between devices, on_device(): lax.all_to_all(mix(place, held), 'dp', 0, 0, axis_index_groups=PLANE, til...  7.25 us
    pallas_call x1, Pallas kernels, pick(): pl.pallas_call(pick_kernel, grid=(frames.shape[1] // PICK,), in_specs=[pl...  5.58 us
  transfers between devices with their start and end apart: 10, of which 6 were waited for; matrix products, arithmetic and copies ran while one was open for 2% of the time, Pallas kernels for 25%

profile of v6, /device:TPU:1, one launch (start us, length us, event | category | flops | bytes accessed | tf_op | source)
XLA Modules:
  0.0 115.8 jit_solution(3618627244776065129)
XLA Ops:
  0.6 0.7 pad_add_fusion.place
  1.3 5.6 %pick.1 = bf16[16,64,256]{2,1,0:T(8,128)(2,1)} custom-call(s32[3]{0:T(128)} %pad_add_fusion.place, s32[2,512]{1,0:T(2,128)} %index.1, bf16[112,4096]{1,0:T(8,128)(2,1)} %frames.1, f32[37,4096]{1,0:T(8,128)} %residual.3), custom_call_target="tpu_custom_call" | custom-call | tf_op jit(solution)/shard_map/pick/pallas_call | solution.py:175
  6.9 7.7 %all-to-all-start = ((bf16[16,64,256]{2,1,0:T(8,128)(2,1)}), bf16[16,64,256]{2,1,0:T(8,128)(2,1)S(1)}, u32[]{:S(2)}, u32[]{:S(2)}) async-start(bf16[16,64,256]{2,1,0:T(8,128)(2,1)} %pick.1), calls=%async_computation | async-start | bytes 1048576 | tf_op jit(solution)/shard_map/all_to_all | solution.py:388
  14.6 0.0 copy-done.8
  14.6 0.9 constant_dynamic-slice_fusion.3
  15.5 1.0 collective-permute-start
  16.5 7.0 %collective-permute-start.1 = (bf16[112,512]{1,0:T(8,128)(2,1)S(1)}, bf16[112,512]{1,0:T(8,128)(2,1)S(1)}, u32[]{:S(2)}, u32[]{:S(2)}) collective-permute-start(bf16[112,512]{1,0:T(8,128)(2,1)S(1)} %get-tuple-element.53), channel_id=1, source_target_pairs={{0,2},{1,3},{2,0},{3,1},{4,6},{5,7},{6,4},{7,5},{8,10},{9,11},{10,... | collective-permute-start | bytes 344072 | tf_op jit(solution)/shard_map/ppermute | solution.py:39
  23.5 0.7 constant_dynamic-slice_fusion
  24.2 1.0 all-to-all-done.held
  25.1 0.8 copy-done.9
  25.9 1.8 %add.21 = bf16[8,64,256]{2,1,0:T(8,128)(2,1)} custom-call(bf16[16,64,256]{2,1,0:T(8,128)(2,1)} %copy-done.9), custom_call_target="tpu_custom_call" | custom-call | tf_op jit(solution)/shard_map/add/pallas_call | solution.py:202
  27.8 0.0 collective-permute-done.1.refs_0_
  27.8 0.0 collective-permute-done.s2
  27.8 17.8 %all_to_all.15.held = bf16[8,64,256]{2,1,0:T(8,128)(2,1)} all-to-all(bf16[8,64,256]{2,1,0:T(8,128)(2,1)} %add.21), channel_id=1, replica_groups={{0,4,8,12,2,6,10,14},{1,5,9,13,3,7,11,15},{16,20,24,28,18,22,26,30},{17..., dimensions={0} | all-to-all | bytes 524288 | tf_op jit(solution)/shard_map/all_to_all | solution.py:390
  45.6 0.0 copy-done.3
  45.6 2.0 %mix.1 = bf16[16,64,384]{2,1,0:T(8,128)(2,1)} custom-call(s32[3]{0:T(128)} %pad_add_fusion.place, bf16[8,64,256]{2,1,0:T(8,128)(2,1)} %all_to_all.15.held), custom_call_target="tpu_custom_call" | custom-call | tf_op jit(solution)/shard_map/mix/pallas_call | solution.py:225
  47.6 7.2 %all-to-all-start.2 = ((bf16[16,64,384]{2,1,0:T(8,128)(2,1)}), bf16[16,64,384]{2,1,0:T(8,128)(2,1)S(1)}, u32[]{:S(2)}, u32[]{:S(2)}) async-start(bf16[16,64,384]{2,1,0:T(8,128)(2,1)} %mix.1), calls=%async_computation.2 | async-start | bytes 1572864 | tf_op jit(solution)/shard_map/all_to_all | solution.py:393
  54.8 1.7 %collective-permute-start.2 = (bf16[112,512]{1,0:T(8,128)(2,1)S(1)}, bf16[112,512]{1,0:T(8,128)(2,1)S(1)}, u32[]{:S(2)}, u32[]{:S(2)}) collective-permute-start(bf16[112,512]{1,0:T(8,128)(2,1)S(1)} %get-tuple-element.32), channel_id=1, source_target_pairs={{0,2},{1,3},{2,0},{3,1},{4,6},{5,7},{6,4},{7,5},{8,10},{9,11},{10,... | collective-permute-start | bytes 344072 | tf_op jit(solution)/shard_map/ppermute | solution.py:39
  56.5 6.0 %collective-permute-done.2.refs_1_ = bf16[112,512]{1,0:T(8,128)(2,1)S(1)} collective-permute-done((bf16[112,512]{1,0:T(8,128)(2,1)S(1)}, bf16[112,512]{1,0:T(8,128)(2,1)S(1)}, u32[]{:S(2)}, u32[]{:S(2)}) %collective-permute-start.2) | collective-permute-done | bytes 114720 | tf_op jit(solution)/shard_map/ppermute | solution.py:39
  62.5 0.6 copy-done.5
  63.1 3.6 %all-to-all-done.2.near.refs_2_.refs_1_ = bf16[16,64,384]{2,1,0:T(8,128)(2,1)S(1)} async-done(((bf16[16,64,384]{2,1,0:T(8,128)(2,1)}), bf16[16,64,384]{2,1,0:T(8,128)(2,1)S(1)}, u32[]{:S(2)}, u32[]{:S(2)}) %all-to-all-start.2) | async-done | bytes 786464 | tf_op jit(solution)/shard_map/all_to_all | solution.py:393
  66.6 3.6 %collective-permute-start.4 = (bf16[16,64,384]{2,1,0:T(8,128)(2,1)S(1)}, bf16[16,64,384]{2,1,0:T(8,128)(2,1)S(1)}, u32[]{:S(2)}, u32[]{:S(2)}) collective-permute-start(bf16[16,64,384]{2,1,0:T(8,128)(2,1)S(1)} %all-to-all-done.2.near.refs_2_.refs_1_), channel_id=1, source_target_pairs={{0,1},{1,0},{2,3},{3,2},{4,5},{5,4},{6,7},{7,6},{8,9},{9,8},{10,11... | collective-permute-start | bytes 2359304 | tf_op jit(solution)/shard_map/ppermute | solution.py:39
  70.2 1.4 %collective-permute-start.3 = (bf16[112,2048]{1,0:T(8,128)(2,1)}, bf16[112,2048]{1,0:T(8,128)(2,1)S(1)}, u32[]{:S(2)}, u32[]{:S(2)}) collective-permute-start(bf16[112,2048]{1,0:T(8,128)(2,1)} %get-tuple-element.37), channel_id=1, source_target_pairs={{0,3},{1,2},{2,1},{3,0},{4,7},{5,6},{6,5},{7,4},{8,11},{9,10},{10,... | collective-permute-start | bytes 1376264 | tf_op jit(solution)/shard_map/ppermute | solution.py:39
  71.6 3.9 %collective-permute-start.5 = (bf16[112,1024]{1,0:T(8,128)(2,1)}, bf16[112,1024]{1,0:T(8,128)(2,1)}, u32[]{:S(2)}, u32[]{:S(2)}) collective-permute-start(bf16[112,1024]{1,0:T(8,128)(2,1)} %constant_dynamic-slice_fusion), channel_id=1, source_target_pairs={{0,2},{1,3},{2,0},{3,1},{4,6},{5,7},{6,4},{7,5},{8,10},{9,11},{10,... | collective-permute-start | bytes 688136 | tf_op jit(solution)/shard_map/ppermute | solution.py:39
  75.5 0.0 copy-done.10
  75.5 0.9 copy.6.point_col
  76.3 0.2 copy.10
  76.6 0.0 collective-permute-done.4.far.refs_3_.refs_2_
  76.6 0.0 copy-start.1
  76.6 0.9 copy-done.1
  77.5 23.0 %solve.1 = (bf16[256,1024]{1,0:T(8,128)(2,1)S(1)}, f32[1024,1]{1,0:T(8,128)S(1)}) custom-call(bf16[16,64,384]{2,1,0:T(8,128)(2,1)S(1)} %all-to-all-done.2.near.refs_2_.refs_1_, bf16[16,64,384]{2,1,0:T(8,128)(2,1)S(1)} %collective-permute-done.4.far.refs_3_.refs_2_, s32[1,512]{1,0:T(1,128)S(1)} %get-tuple-element.55.point_row, s32[512,1]{1,0:T(8,128)S(1)} %copy-done.1), custom_call_target="tpu_custom_call" | custom-call | flops 1048576 | bytes 1048576 | tf_op jit(solution)/shard_map/solve/pallas_call | solution.py:287
  100.5 0.0 collective-permute-done.3.s3
  100.5 0.0 copy-done.4
  100.5 0.0 copy-done.6
  100.5 3.9 %update.2 = (f32[2,40,1024]{2,1,0:T(8,128)S(1)}, f32[2,40,1024]{2,1,0:T(8,128)S(1)}) custom-call(bf16[112,2048]{1,0:T(8,128)(2,1)S(1)} %get-tuple-element.50.s0, bf16[112,2048]{1,0:T(8,128)(2,1)S(1)} %collective-permute-done.s2, bf16[112,2048]{1,0:T(8,128)(2,1)S(1)} %collective-permute-done.3.s3, bf16[112,512]{1,0:T(8,128)(2,1)S(1)} %copy-done.4, ...), custom_call_target="tpu_custom_call" | custom-call | tf_op jit(solution)/shard_map/update/pallas_call | solution.py:341
  104.5 0.0 copy-start
  104.5 0.0 copy-start.2
  104.5 1.5 %collective-permute-done.5.refs_0_ = bf16[112,1024]{1,0:T(8,128)(2,1)} collective-permute-done((bf16[112,1024]{1,0:T(8,128)(2,1)}, bf16[112,1024]{1,0:T(8,128)(2,1)}, u32[]{:S(2)}, u32[]{:S(2)}) %collective-permute-start.5) | collective-permute-done | bytes 229408 | tf_op jit(solution)/shard_map/ppermute | solution.py:39
  106.0 5.1 %update.3 = (f32[2,40,1024]{2,1,0:T(8,128)S(1)}, f32[2,40,1024]{2,1,0:T(8,128)S(1)}) custom-call(bf16[112,2048]{1,0:T(8,128)(2,1)S(1)} %get-tuple-element.50.s0, bf16[112,2048]{1,0:T(8,128)(2,1)S(1)} %collective-permute-done.s2, bf16[112,2048]{1,0:T(8,128)(2,1)S(1)} %collective-permute-done.3.s3, bf16[112,1024]{1,0:T(8,128)(2,1)} %collective-permute-done.5.refs_0_, ...), custom_call_target="tpu_custom_call" | custom-call | tf_op jit(solution)/shard_map/update/pallas_call | solution.py:341
  111.1 0.0 copy-start.7
  111.1 1.2 %collective-permute-start.7 = (f32[2,40,1024]{2,1,0:T(8,128)S(1)}, f32[2,40,1024]{2,1,0:T(8,128)S(1)}, u32[]{:S(2)}, u32[]{:S(2)}) collective-permute-start(f32[2,40,1024]{2,1,0:T(8,128)S(1)} %get-tuple-element.49), channel_id=1, source_target_pairs={{0,1},{1,0},{2,3},{3,2},{4,5},{5,4},{6,7},{7,6},{8,9},{9,8},{10,11... | collective-permute-start | bytes 983048 | tf_op jit(solution)/shard_map/ppermute | solution.py:39
  112.3 0.1 collective-permute-start.6
  112.4 1.2 collective-permute-done.7.got1
  113.6 0.5 collective-permute-done.6.got0
  114.0 0.0 copy-done
  114.0 0.0 copy-done.2
  114.0 0.0 copy-done.7
  114.0 1.8 %finish.1 = (f32[37,4096]{1,0:T(8,128)}, f32[37,4096]{1,0:T(8,128)}) custom-call(s32[3]{0:T(128)S(1)} %copy-done.7, f32[37,4096]{1,0:T(8,128)S(1)} %copy-done, f32[37,4096]{1,0:T(8,128)S(1)} %copy-done.2, f32[2,40,1024]{2,1,0:T(8,128)S(1)} %get-tuple-element.44.mine0, f32[2,40,1024]{2,1,0:T(8,128)S(1)} %get-tuple-element.47.mine1, ...), custom_call_target="tpu_custom_call" | custom-call | tf_op jit(solution)/shard_map/finish/pallas_call | solution.py:364
  (11 shorter events, 0.0 us)
Async XLA Ops:
  6.9 7.7 %copy-start.8 = (bf16[112,4096]{1,0:T(8,128)(2,1)S(1)}, bf16[112,4096]{1,0:T(8,128)(2,1)}, u32[]{:S(2)}) copy-start(bf16[112,4096]{1,0:T(8,128)(2,1)} %frames.1) | copy-start | bytes 2752516
  6.9 18.2 %all-to-all-start = ((bf16[16,64,256]{2,1,0:T(8,128)(2,1)}), bf16[16,64,256]{2,1,0:T(8,128)(2,1)S(1)}, u32[]{:S(2)}, u32[]{:S(2)}) async-start(bf16[16,64,256]{2,1,0:T(8,128)(2,1)} %pick.1), calls=%async_computation | async-start | bytes 1048576 | tf_op jit(solution)/shard_map/all_to_all | solution.py:388
  15.5 12.3 %collective-permute-start = (bf16[112,2048]{1,0:T(8,128)(2,1)}, bf16[112,2048]{1,0:T(8,128)(2,1)S(1)}, u32[]{:S(2)}, u32[]{:S(2)}) collective-permute-start(bf16[112,2048]{1,0:T(8,128)(2,1)} %get-tuple-element.37), channel_id=1, source_target_pairs={{0,1},{1,0},{2,3},{3,2},{4,5},{5,4},{6,7},{7,6},{8,9},{9,8},{10,11... | collective-permute-start | bytes 1376264 | tf_op jit(solution)/shard_map/ppermute | solution.py:39
  16.5 11.3 %collective-permute-start.1 = (bf16[112,512]{1,0:T(8,128)(2,1)S(1)}, bf16[112,512]{1,0:T(8,128)(2,1)S(1)}, u32[]{:S(2)}, u32[]{:S(2)}) collective-permute-start(bf16[112,512]{1,0:T(8,128)(2,1)S(1)} %get-tuple-element.53), channel_id=1, source_target_pairs={{0,2},{1,3},{2,0},{3,1},{4,6},{5,7},{6,4},{7,5},{8,10},{9,11},{10,... | collective-permute-start | bytes 344072 | tf_op jit(solution)/shard_map/ppermute | solution.py:39
  25.1 0.8 copy-start.9
  27.8 17.8 %copy-start.3 = (bf16[112,512]{1,0:T(8,128)(2,1)}, bf16[112,512]{1,0:T(8,128)(2,1)S(1)}, u32[]{:S(2)}) copy-start(bf16[112,512]{1,0:T(8,128)(2,1)S(1)} %collective-permute-done.1.refs_0_) | copy-start | bytes 344068
  47.5 27.9 %copy-start.10 = (s32[2,512]{1,0:T(2,128)S(1)}, s32[2,512]{1,0:T(2,128)}, u32[]{:S(2)}) copy-start(s32[2,512]{1,0:T(2,128)} %index.1) | copy-start | bytes 12292
  47.6 19.1 %all-to-all-start.2 = ((bf16[16,64,384]{2,1,0:T(8,128)(2,1)}), bf16[16,64,384]{2,1,0:T(8,128)(2,1)S(1)}, u32[]{:S(2)}, u32[]{:S(2)}) async-start(bf16[16,64,384]{2,1,0:T(8,128)(2,1)} %mix.1), calls=%async_computation.2 | async-start | bytes 1572864 | tf_op jit(solution)/shard_map/all_to_all | solution.py:393
  54.8 7.6 %collective-permute-start.2 = (bf16[112,512]{1,0:T(8,128)(2,1)S(1)}, bf16[112,512]{1,0:T(8,128)(2,1)S(1)}, u32[]{:S(2)}, u32[]{:S(2)}) collective-permute-start(bf16[112,512]{1,0:T(8,128)(2,1)S(1)} %get-tuple-element.32), channel_id=1, source_target_pairs={{0,2},{1,3},{2,0},{3,1},{4,6},{5,7},{6,4},{7,5},{8,10},{9,11},{10,... | collective-permute-start | bytes 344072 | tf_op jit(solution)/shard_map/ppermute | solution.py:39
  62.5 0.6 copy-start.5
  66.6 9.9 %collective-permute-start.4 = (bf16[16,64,384]{2,1,0:T(8,128)(2,1)S(1)}, bf16[16,64,384]{2,1,0:T(8,128)(2,1)S(1)}, u32[]{:S(2)}, u32[]{:S(2)}) collective-permute-start(bf16[16,64,384]{2,1,0:T(8,128)(2,1)S(1)} %all-to-all-done.2.near.refs_2_.refs_1_), channel_id=1, source_target_pairs={{0,1},{1,0},{2,3},{3,2},{4,5},{5,4},{6,7},{7,6},{8,9},{9,8},{10,11... | collective-permute-start | bytes 2359304 | tf_op jit(solution)/shard_map/ppermute | solution.py:39
  70.2 30.3 %collective-permute-start.3 = (bf16[112,2048]{1,0:T(8,128)(2,1)}, bf16[112,2048]{1,0:T(8,128)(2,1)S(1)}, u32[]{:S(2)}, u32[]{:S(2)}) collective-permute-start(bf16[112,2048]{1,0:T(8,128)(2,1)} %get-tuple-element.37), channel_id=1, source_target_pairs={{0,3},{1,2},{2,1},{3,0},{4,7},{5,6},{6,5},{7,4},{8,11},{9,10},{10,... | collective-permute-start | bytes 1376264 | tf_op jit(solution)/shard_map/ppermute | solution.py:39
  71.6 34.4 %collective-permute-start.5 = (bf16[112,1024]{1,0:T(8,128)(2,1)}, bf16[112,1024]{1,0:T(8,128)(2,1)}, u32[]{:S(2)}, u32[]{:S(2)}) collective-permute-start(bf16[112,1024]{1,0:T(8,128)(2,1)} %constant_dynamic-slice_fusion), channel_id=1, source_target_pairs={{0,2},{1,3},{2,0},{3,1},{4,6},{5,7},{6,4},{7,5},{8,10},{9,11},{10,... | collective-permute-start | bytes 688136 | tf_op jit(solution)/shard_map/ppermute | solution.py:39
  76.6 1.0 copy-start.1
  77.5 23.0 %copy-start.4 = (bf16[112,512]{1,0:T(8,128)(2,1)S(1)}, bf16[112,512]{1,0:T(8,128)(2,1)}, u32[]{:S(2)}) copy-start(bf16[112,512]{1,0:T(8,128)(2,1)} %copy-done.3) | copy-start | bytes 344068
  77.5 23.0 %copy-start.6 = (bf16[112,512]{1,0:T(8,128)(2,1)S(1)}, bf16[112,512]{1,0:T(8,128)(2,1)}, u32[]{:S(2)}) copy-start(bf16[112,512]{1,0:T(8,128)(2,1)} %copy-done.5) | copy-start | bytes 344068
  104.5 9.6 %copy-start = (f32[37,4096]{1,0:T(8,128)S(1)}, f32[37,4096]{1,0:T(8,128)}, u32[]{:S(2)}) copy-start(f32[37,4096]{1,0:T(8,128)} %residual.3) | copy-start | bytes 1818628
  104.5 9.5 %copy-start.2 = (f32[37,4096]{1,0:T(8,128)S(1)}, f32[37,4096]{1,0:T(8,128)}, u32[]{:S(2)}) copy-start(f32[37,4096]{1,0:T(8,128)} %coefficients.1) | copy-start | bytes 1818628
  111.1 2.9 %copy-start.7 = (s32[3]{0:T(128)S(1)}, s32[3]{0:T(128)}, u32[]{:S(2)}) copy-start(s32[3]{0:T(128)} %pad_add_fusion.place) | copy-start | bytes 40
  111.1 2.4 %collective-permute-start.7 = (f32[2,40,1024]{2,1,0:T(8,128)S(1)}, f32[2,40,1024]{2,1,0:T(8,128)S(1)}, u32[]{:S(2)}, u32[]{:S(2)}) collective-permute-start(f32[2,40,1024]{2,1,0:T(8,128)S(1)} %get-tuple-element.49), channel_id=1, source_target_pairs={{0,1},{1,0},{2,3},{3,2},{4,5},{5,4},{6,7},{7,6},{8,9},{9,8},{10,11... | collective-permute-start | bytes 983048 | tf_op jit(solution)/shard_map/ppermute | solution.py:39
  112.3 1.7 %collective-permute-start.6 = (f32[2,40,1024]{2,1,0:T(8,128)S(1)}, f32[2,40,1024]{2,1,0:T(8,128)S(1)}, u32[]{:S(2)}, u32[]{:S(2)}) collective-permute-start(f32[2,40,1024]{2,1,0:T(8,128)S(1)} %get-tuple-element.48), channel_id=1, source_target_pairs={{0,1},{1,0},{2,3},{3,2},{4,5},{5,4},{6,7},{7,6},{8,9},{9,8},{10,11... | collective-permute-start | bytes 983048 | tf_op jit(solution)/shard_map/ppermute | solution.py:39

commit v7 on v6

--- a/solution.py
+++ b/solution.py
@@ -230,7 +230,7 @@
     )(place, held)
 
 
-def solve_kernel(near, far, point_row, point_col, delta_ref, sq_ref, mats, packed, grams):
+def solve_kernel(near, far, index, delta_ref, sq_ref, index_ref, mats, packed, grams):
     eye = lax.broadcasted_iota(jnp.int32, (BLOCK, BLOCK), 0) == lax.broadcasted_iota(jnp.int32, (BLOCK, BLOCK), 1)
 
     def columns(ref, s, at):
@@ -247,17 +247,19 @@
             )
         return total
 
-    rows, cols = [], []
+    rows, cols, points = [], [], []
     for s in range(STEPS):
         products = inner(s, s)
         diagonal = jnp.where(eye, products, 0.0)
         rows.append(jnp.sum(diagonal, axis=0, keepdims=True))
         cols.append(jnp.sum(diagonal, axis=1, keepdims=True))
         sq_ref[BLOCK * s : BLOCK * s + BLOCK] = cols[s]
+        points.append(jnp.broadcast_to(index[s : s + 1].astype(F32), (128, BLOCK)))
+        index_ref[BLOCK * s : BLOCK * s + BLOCK] = points[s].T[:, :1]
         kern = jnp.exp2(-SCALE * (cols[s] + rows[s] - 2.0 * products))
         mats[s] = grams[s] = kern + jnp.where(eye, RIDGE, 0.0)
     cross = jnp.exp2(-SCALE * (cols[0] + rows[1] - 2.0 * inner(0, 1)))
-    cross = cross + jnp.where(point_col[...] == point_row[...], RIDGE, 0.0)
+    cross = cross + jnp.where(points[0].T[:, :1] == points[1][:1], RIDGE, 0.0)
     lane = lax.broadcasted_iota(jnp.int32, (1, 128), 1)
 
     def block_res(s):
@@ -289,6 +291,7 @@
         out_shape=(
             jax.ShapeDtypeStruct((256, STEPS * BLOCK), BF16),
             jax.ShapeDtypeStruct((STEPS * BLOCK, 1), F32),
+            jax.ShapeDtypeStruct((STEPS * BLOCK, 1), F32),
         ),
         scratch_shapes=[
             pltpu.VMEM((2, BLOCK, BLOCK), F32),
@@ -298,10 +301,10 @@
         compiler_params=pltpu.CompilerParams(vmem_limit_bytes=40 << 20),
         cost_estimate=pl.CostEstimate(flops=1 << 20, bytes_accessed=1 << 20, transcendentals=0),
         name="solve",
-    )(near, far, chosen[1].reshape(1, BLOCK), chosen[0].reshape(BLOCK, 1))
-
-
-def update_kernel(part, s0, s2, s3, *refs):
+    )(near, far, chosen)
+
+
+def update_kernel(part, place, s0, s2, s3, *refs):
     *across, near, far, delta, sq, local, mine_ref, theirs_ref = refs
     s1 = across[0][...] if len(across) == 1 else jnp.concatenate([one[...] for one in across], axis=1)
 
@@ -313,7 +316,7 @@
     pad = jnp.zeros((32, TILE), BF16)
     source_near = jnp.concatenate([s0[...], s1, pad], axis=0)
     source_far = jnp.concatenate([s2[...], s3[...], pad], axis=0)
-    positions = part * TILE + lax.broadcasted_iota(jnp.int32, (1, TILE), 1)
+    positions = (place[3] + part * TILE + lax.broadcasted_iota(jnp.int32, (1, TILE), 1)).astype(F32)
     change = jnp.zeros((256, TILE), F32)
     placed = jnp.zeros((256, TILE), F32)
     size = 512
@@ -336,17 +339,19 @@
         out[1] = added
 
 
-def update(part, sources, across, near, far, delta, sq, local):
+def update(part, place, sources, across, near, far, delta, sq, local):
     whole = pl.BlockSpec(memory_space=pltpu.VMEM)
     return pl.pallas_call(
         functools.partial(update_kernel, part),
         grid=(1,),
-        in_specs=[pl.BlockSpec((112, TILE), lambda i: (0, part))] * 3 + [whole] * (len(across) + 5),
+        in_specs=[pl.BlockSpec(memory_space=pltpu.SMEM)]
+        + [pl.BlockSpec((112, TILE), lambda i: (0, part))] * 3
+        + [whole] * (len(across) + 5),
         out_specs=[whole] * 2,
         out_shape=[jax.ShapeDtypeStruct((2, 40, TILE), F32)] * 2,
         compiler_params=pltpu.CompilerParams(vmem_limit_bytes=40 << 20),
         name="update",
-    )(*sources, *across, near, far, delta, sq, local)
+    )(place, *sources, *across, near, far, delta, sq, local)
 
 
 def finish_kernel(place, residual, coefficients, mine0, mine1, got0, got1, res_out, coef_out):
@@ -376,7 +381,7 @@
     rows = frames.shape[1]
     dp, feat = lax.axis_index("dp"), lax.axis_index("feat")
     h, c = feat // 2, feat % 2
-    place = jnp.stack([h, c, dp * rows]).astype(jnp.int32)
+    place = jnp.stack([h, c, dp * rows, dp * rows + c * (rows // 2)]).astype(jnp.int32)
     own_half = lax.dynamic_slice_in_dim(frames, c * (rows // 2), rows // 2, axis=1)
     other_half = lax.dynamic_slice_in_dim(frames, (1 - c) * (rows // 2), rows // 2, axis=1)
     beside = swap(other_half, 0, 1)
@@ -396,13 +401,12 @@
     across.append(swap(own[2], 1, 0))
     diagonal = swap(other_half, 1, 1)
 
-    delta, sq = solve(near, far, block_index)
-    local = block_index.reshape(-1, 1) - dp * rows - c * (rows // 2)
+    delta, sq, local = solve(near, far, block_index)
     sources = own_half, beside, diagonal
-    mine0, theirs0 = update(0, sources, across[:2], near, far, delta, sq, local)
+    mine0, theirs0 = update(0, place, sources, across[:2], near, far, delta, sq, local)
     near, mine0, theirs0 = lax.optimization_barrier((near, mine0, theirs0))
     got0 = swap(theirs0, 0, 1)
-    mine1, theirs1 = update(1, sources, across[2:], near, far, delta, sq, local)
+    mine1, theirs1 = update(1, place, sources, across[2:], near, far, delta, sq, local)
     got1 = swap(theirs1, 0, 1)
     return finish(place, residual, coefficients, mine0, mine1, got0, got1)
 

time: 116 us -> 115 us (level)
  local copies, waits for them, and re-layouts: 5.06 us -> 1.58 us
  waiting for transfers between devices: 13.6 us -> 16.4 us
    all_to_all x1, waiting for transfers between devices: 0.97 us -> 2.32 us  [on_device(): lax.all_to_all(held, 'dp', 0, 0, axis_index_groups=PLANE, tiled=True)]
    unnamed x24 -> x12, local copies, waits for them, and re-layouts: 2.63 us -> 1.47 us
  transfers between devices with their start and end apart: 10 -> 10, of which waited for: 6 -> 7; matrix products, arithmetic and copies ran while one was open for 2% -> 0% of each run, Pallas kernels for 25% -> 26%
where the time goes in v7:
time: 115 us; the launch traced here: 114 us
  Pallas kernels  43.3 us (38%)
  starting transfers between devices  34 us (30%)
  blocking collectives  17.8 us (15%)
  waiting for transfers between devices  16.4 us (14%)
  local copies, waits for them, and re-layouts  1.58 us (1%)
    pallas_call x1, Pallas kernels, solve(): pl.pallas_call(solve_kernel, out_shape=(jax.ShapeDtypeStruct((256, STEPS...  22.9 us
    ppermute x8, starting transfers between devices, swap(): return lax.ppermute(value, AXES, permutation(move))  19.7 us
    all_to_all x1, blocking collectives, on_device(): held = lax.all_to_all(held, AXES, 0, 0, axis_index_groups=LINE, tiled=True)  17.8 us
    ppermute x8, waiting for transfers between devices, swap(): return lax.ppermute(value, AXES, permutation(move))  9.86 us
    pallas_call x2, Pallas kernels, update(): pl.pallas_call(functools.partial(update_kernel, part), grid=(1,), in_spec...  9.23 us
    all_to_all x1, starting transfers between devices, on_device(): lax.all_to_all(held, 'dp', 0, 0, axis_index_groups=PLANE, tiled=True)  7.71 us
    all_to_all x1, starting transfers between devices, on_device(): lax.all_to_all(mix(place, held), 'dp', 0, 0, axis_index_groups=PLANE, til...  6.55 us
    pallas_call x1, Pallas kernels, pick(): pl.pallas_call(pick_kernel, grid=(frames.shape[1] // PICK,), in_specs=[pl...  5.58 us
  transfers between devices with their start and end apart: 10, of which 7 were waited for; matrix products, arithmetic and copies ran while one was open for 0% of the time, Pallas kernels for 26%

profile of v7, /device:TPU:1, one launch (start us, length us, event | category | flops | bytes accessed | tf_op | source)
XLA Modules:
  0.0 114.4 jit_solution(14230112468994137152)
XLA Ops:
  0.7 0.7 pad_add_fusion.place
  1.3 5.6 %pick.1 = bf16[16,64,256]{2,1,0:T(8,128)(2,1)} custom-call(s32[4]{0:T(128)} %pad_add_fusion.place, s32[2,512]{1,0:T(2,128)} %index.3, bf16[112,4096]{1,0:T(8,128)(2,1)} %frames.1, f32[37,4096]{1,0:T(8,128)} %residual.3), custom_call_target="tpu_custom_call" | custom-call | tf_op jit(solution)/shard_map/pick/pallas_call | solution.py:175
  6.9 0.0 copy-start.4
  6.9 7.7 %all-to-all-start = ((bf16[16,64,256]{2,1,0:T(8,128)(2,1)}), bf16[16,64,256]{2,1,0:T(8,128)(2,1)S(1)}, u32[]{:S(2)}, u32[]{:S(2)}) async-start(bf16[16,64,256]{2,1,0:T(8,128)(2,1)} %pick.1), calls=%async_computation | async-start | bytes 1048576 | tf_op jit(solution)/shard_map/all_to_all | solution.py:393
  14.6 0.0 copy-done.4
  14.6 0.1 constant_dynamic-slice_fusion.3
  14.7 1.0 collective-permute-start
  15.8 7.0 %collective-permute-start.1 = (bf16[112,512]{1,0:T(8,128)(2,1)S(1)}, bf16[112,512]{1,0:T(8,128)(2,1)S(1)}, u32[]{:S(2)}, u32[]{:S(2)}) collective-permute-start(bf16[112,512]{1,0:T(8,128)(2,1)S(1)} %get-tuple-element.55), channel_id=1, source_target_pairs={{0,2},{1,3},{2,0},{3,1},{4,6},{5,7},{6,4},{7,5},{8,10},{9,11},{10,... | collective-permute-start | bytes 344072 | tf_op jit(solution)/shard_map/ppermute | solution.py:39
  22.8 2.3 %all-to-all-done.held = bf16[16,64,256]{2,1,0:T(8,128)(2,1)S(1)} async-done(((bf16[16,64,256]{2,1,0:T(8,128)(2,1)}), bf16[16,64,256]{2,1,0:T(8,128)(2,1)S(1)}, u32[]{:S(2)}, u32[]{:S(2)}) %all-to-all-start) | async-done | bytes 524320 | tf_op jit(solution)/shard_map/all_to_all | solution.py:393
  25.1 0.0 copy-start.5
  25.1 0.8 copy-done.5
  25.9 1.8 %add.27 = bf16[8,64,256]{2,1,0:T(8,128)(2,1)} custom-call(bf16[16,64,256]{2,1,0:T(8,128)(2,1)} %copy-done.5), custom_call_target="tpu_custom_call" | custom-call | tf_op jit(solution)/shard_map/add/pallas_call | solution.py:202
  27.7 0.0 collective-permute-done.1.refs_0_
  27.7 0.0 collective-permute-done.s2
  27.7 17.8 %all_to_all.15.held = bf16[8,64,256]{2,1,0:T(8,128)(2,1)} all-to-all(bf16[8,64,256]{2,1,0:T(8,128)(2,1)} %add.27), channel_id=1, replica_groups={{0,4,8,12,2,6,10,14},{1,5,9,13,3,7,11,15},{16,20,24,28,18,22,26,30},{17..., dimensions={0} | all-to-all | bytes 524288 | tf_op jit(solution)/shard_map/all_to_all | solution.py:395
  45.5 2.0 %mix.1 = bf16[16,64,384]{2,1,0:T(8,128)(2,1)} custom-call(s32[4]{0:T(128)} %pad_add_fusion.place, bf16[8,64,256]{2,1,0:T(8,128)(2,1)} %all_to_all.15.held), custom_call_target="tpu_custom_call" | custom-call | tf_op jit(solution)/shard_map/mix/pallas_call | solution.py:225
  47.5 0.0 copy-start.3
  47.5 6.5 %all-to-all-start.2 = ((bf16[16,64,384]{2,1,0:T(8,128)(2,1)}), bf16[16,64,384]{2,1,0:T(8,128)(2,1)S(1)}, u32[]{:S(2)}, u32[]{:S(2)}) async-start(bf16[16,64,384]{2,1,0:T(8,128)(2,1)} %mix.1), calls=%async_computation.2 | async-start | bytes 1572864 | tf_op jit(solution)/shard_map/all_to_all | solution.py:398
  54.1 1.6 %collective-permute-start.2 = (bf16[112,512]{1,0:T(8,128)(2,1)S(1)}, bf16[112,512]{1,0:T(8,128)(2,1)S(1)}, u32[]{:S(2)}, u32[]{:S(2)}) collective-permute-start(bf16[112,512]{1,0:T(8,128)(2,1)S(1)} %get-tuple-element.33), channel_id=1, source_target_pairs={{0,2},{1,3},{2,0},{3,1},{4,6},{5,7},{6,4},{7,5},{8,10},{9,11},{10,... | collective-permute-start | bytes 344072 | tf_op jit(solution)/shard_map/ppermute | solution.py:39
  55.7 6.0 %collective-permute-done.2.refs_1_ = bf16[112,512]{1,0:T(8,128)(2,1)S(1)} collective-permute-done((bf16[112,512]{1,0:T(8,128)(2,1)S(1)}, bf16[112,512]{1,0:T(8,128)(2,1)S(1)}, u32[]{:S(2)}, u32[]{:S(2)}) %collective-permute-start.2) | collective-permute-done | bytes 114720 | tf_op jit(solution)/shard_map/ppermute | solution.py:39
  61.7 4.2 %all-to-all-done.2.near.refs_2_.refs_1_ = bf16[16,64,384]{2,1,0:T(8,128)(2,1)S(1)} async-done(((bf16[16,64,384]{2,1,0:T(8,128)(2,1)}), bf16[16,64,384]{2,1,0:T(8,128)(2,1)S(1)}, u32[]{:S(2)}, u32[]{:S(2)}) %all-to-all-start.2) | async-done | bytes 786464 | tf_op jit(solution)/shard_map/all_to_all | solution.py:398
  65.9 3.5 %collective-permute-start.4 = (bf16[16,64,384]{2,1,0:T(8,128)(2,1)S(1)}, bf16[16,64,384]{2,1,0:T(8,128)(2,1)S(1)}, u32[]{:S(2)}, u32[]{:S(2)}) collective-permute-start(bf16[16,64,384]{2,1,0:T(8,128)(2,1)S(1)} %all-to-all-done.2.near.refs_2_.refs_1_), channel_id=1, source_target_pairs={{0,1},{1,0},{2,3},{3,2},{4,5},{5,4},{6,7},{7,6},{8,9},{9,8},{10,11... | collective-permute-start | bytes 2359304 | tf_op jit(solution)/shard_map/ppermute | solution.py:39
  69.4 1.4 %collective-permute-start.3 = (bf16[112,2048]{1,0:T(8,128)(2,1)S(1)}, bf16[112,2048]{1,0:T(8,128)(2,1)S(1)}, u32[]{:S(2)}, u32[]{:S(2)}) collective-permute-start(bf16[112,2048]{1,0:T(8,128)(2,1)S(1)} %get-tuple-element.38), channel_id=1, source_target_pairs={{0,3},{1,2},{2,1},{3,0},{4,7},{5,6},{6,5},{7,4},{8,11},{9,10},{10,... | collective-permute-start | bytes 1376264 | tf_op jit(solution)/shard_map/ppermute | solution.py:39
  70.8 3.9 %collective-permute-start.5 = (bf16[112,1024]{1,0:T(8,128)(2,1)S(1)}, bf16[112,1024]{1,0:T(8,128)(2,1)S(1)}, u32[]{:S(2)}, u32[]{:S(2)}) collective-permute-start(bf16[112,1024]{1,0:T(8,128)(2,1)S(1)} %constant_dynamic-slice_fusion), channel_id=1, source_target_pairs={{0,2},{1,3},{2,0},{3,1},{4,6},{5,7},{6,4},{7,5},{8,10},{9,11},{10,... | collective-permute-start | bytes 688136 | tf_op jit(solution)/shard_map/ppermute | solution.py:39
  74.7 0.0 collective-permute-done.4.far.refs_3_.refs_2_
  74.7 0.0 copy-done.3
  74.7 22.9 %solve.1 = (bf16[256,1024]{1,0:T(8,128)(2,1)S(1)}, f32[1024,1]{1,0:T(8,128)S(1)}, f32[1024,1]{1,0:T(8,128)S(1)}) custom-call(bf16[16,64,384]{2,1,0:T(8,128)(2,1)S(1)} %all-to-all-done.2.near.refs_2_.refs_1_, bf16[16,64,384]{2,1,0:T(8,128)(2,1)S(1)} %collective-permute-done.4.far.refs_3_.refs_2_, s32[2,512]{1,0:T(2,128)S(1)} %copy-done.3), custom_call_target="tpu_custom_call" | custom-call | flops 1048576 | bytes 1048576 | tf_op jit(solution)/shard_map/solve/pallas_call | solution.py:289
  97.7 0.7 collective-permute-done.3.s3
  98.4 0.0 copy-start.2
  98.4 0.7 copy-done.2
  99.1 4.5 %update.2 = (f32[2,40,1024]{2,1,0:T(8,128)S(1)}, f32[2,40,1024]{2,1,0:T(8,128)S(1)}) custom-call(s32[4]{0:T(128)S(1)} %copy-done.2, bf16[112,2048]{1,0:T(8,128)(2,1)S(1)} %get-tuple-element.52.s0, bf16[112,2048]{1,0:T(8,128)(2,1)S(1)} %collective-permute-done.s2, bf16[112,2048]{1,0:T(8,128)(2,1)S(1)} %collective-permute-done.3.s3, ...), custom_call_target="tpu_custom_call" | custom-call | tf_op jit(solution)/shard_map/update/pallas_call | solution.py:344
  103.6 0.0 copy-start
  103.6 0.0 copy-start.1
  103.6 1.5 %collective-permute-done.5.refs_0_ = bf16[112,1024]{1,0:T(8,128)(2,1)S(1)} collective-permute-done((bf16[112,1024]{1,0:T(8,128)(2,1)S(1)}, bf16[112,1024]{1,0:T(8,128)(2,1)S(1)}, u32[]{:S(2)}, u32[]{:S(2)}) %collective-permute-start.5) | collective-permute-done | bytes 229408 | tf_op jit(solution)/shard_map/ppermute | solution.py:39
  105.0 4.7 %update.3 = (f32[2,40,1024]{2,1,0:T(8,128)S(1)}, f32[2,40,1024]{2,1,0:T(8,128)S(1)}) custom-call(s32[4]{0:T(128)S(1)} %copy-done.2, bf16[112,2048]{1,0:T(8,128)(2,1)S(1)} %get-tuple-element.52.s0, bf16[112,2048]{1,0:T(8,128)(2,1)S(1)} %collective-permute-done.s2, bf16[112,2048]{1,0:T(8,128)(2,1)S(1)} %collective-permute-done.3.s3, ...), custom_call_target="tpu_custom_call" | custom-call | tf_op jit(solution)/shard_map/update/pallas_call | solution.py:344
  109.8 1.2 %collective-permute-start.7 = (f32[2,40,1024]{2,1,0:T(8,128)S(1)}, f32[2,40,1024]{2,1,0:T(8,128)S(1)}, u32[]{:S(2)}, u32[]{:S(2)}) collective-permute-start(f32[2,40,1024]{2,1,0:T(8,128)S(1)} %get-tuple-element.51), channel_id=1, source_target_pairs={{0,1},{1,0},{2,3},{3,2},{4,5},{5,4},{6,7},{7,6},{8,9},{9,8},{10,11... | collective-permute-start | bytes 983048 | tf_op jit(solution)/shard_map/ppermute | solution.py:39
  111.0 0.1 collective-permute-start.6
  111.1 1.2 %collective-permute-done.7.got1 = f32[2,40,1024]{2,1,0:T(8,128)S(1)} collective-permute-done((f32[2,40,1024]{2,1,0:T(8,128)S(1)}, f32[2,40,1024]{2,1,0:T(8,128)S(1)}, u32[]{:S(2)}, u32[]{:S(2)}) %collective-permute-start.7) | collective-permute-done | bytes 327712 | tf_op jit(solution)/shard_map/ppermute | solution.py:39
  112.2 0.5 collective-permute-done.6.got0
  112.7 0.0 copy-done
  112.7 0.0 copy-done.1
  112.7 1.7 %finish.1 = (f32[37,4096]{1,0:T(8,128)}, f32[37,4096]{1,0:T(8,128)}) custom-call(s32[4]{0:T(128)S(1)} %copy-done.2, f32[37,4096]{1,0:T(8,128)S(1)} %copy-done, f32[37,4096]{1,0:T(8,128)S(1)} %copy-done.1, f32[2,40,1024]{2,1,0:T(8,128)S(1)} %get-tuple-element.46.mine0, f32[2,40,1024]{2,1,0:T(8,128)S(1)} %get-tuple-element.49.mine1, ...), custom_call_target="tpu_custom_call" | custom-call | tf_op jit(solution)/shard_map/finish/pallas_call | solution.py:369
  (2 shorter events, 0.0 us)
Async XLA Ops:
  6.9 7.7 %copy-start.4 = (bf16[112,4096]{1,0:T(8,128)(2,1)S(1)}, bf16[112,4096]{1,0:T(8,128)(2,1)}, u32[]{:S(2)}) copy-start(bf16[112,4096]{1,0:T(8,128)(2,1)} %frames.1) | copy-start | bytes 2752516
  6.9 18.2 %all-to-all-start = ((bf16[16,64,256]{2,1,0:T(8,128)(2,1)}), bf16[16,64,256]{2,1,0:T(8,128)(2,1)S(1)}, u32[]{:S(2)}, u32[]{:S(2)}) async-start(bf16[16,64,256]{2,1,0:T(8,128)(2,1)} %pick.1), calls=%async_computation | async-start | bytes 1048576 | tf_op jit(solution)/shard_map/all_to_all | solution.py:393
  14.7 13.0 %collective-permute-start = (bf16[112,2048]{1,0:T(8,128)(2,1)S(1)}, bf16[112,2048]{1,0:T(8,128)(2,1)S(1)}, u32[]{:S(2)}, u32[]{:S(2)}) collective-permute-start(bf16[112,2048]{1,0:T(8,128)(2,1)S(1)} %get-tuple-element.38), channel_id=1, source_target_pairs={{0,1},{1,0},{2,3},{3,2},{4,5},{5,4},{6,7},{7,6},{8,9},{9,8},{10,11... | collective-permute-start | bytes 1376264 | tf_op jit(solution)/shard_map/ppermute | solution.py:39
  15.8 11.9 %collective-permute-start.1 = (bf16[112,512]{1,0:T(8,128)(2,1)S(1)}, bf16[112,512]{1,0:T(8,128)(2,1)S(1)}, u32[]{:S(2)}, u32[]{:S(2)}) collective-permute-start(bf16[112,512]{1,0:T(8,128)(2,1)S(1)} %get-tuple-element.55), channel_id=1, source_target_pairs={{0,2},{1,3},{2,0},{3,1},{4,6},{5,7},{6,4},{7,5},{8,10},{9,11},{10,... | collective-permute-start | bytes 344072 | tf_op jit(solution)/shard_map/ppermute | solution.py:39
  25.1 0.8 copy-start.5
  47.5 27.2 %copy-start.3 = (s32[2,512]{1,0:T(2,128)S(1)}, s32[2,512]{1,0:T(2,128)}, u32[]{:S(2)}) copy-start(s32[2,512]{1,0:T(2,128)} %index.3) | copy-start | bytes 12292
  47.5 18.4 %all-to-all-start.2 = ((bf16[16,64,384]{2,1,0:T(8,128)(2,1)}), bf16[16,64,384]{2,1,0:T(8,128)(2,1)S(1)}, u32[]{:S(2)}, u32[]{:S(2)}) async-start(bf16[16,64,384]{2,1,0:T(8,128)(2,1)} %mix.1), calls=%async_computation.2 | async-start | bytes 1572864 | tf_op jit(solution)/shard_map/all_to_all | solution.py:398
  54.1 7.6 %collective-permute-start.2 = (bf16[112,512]{1,0:T(8,128)(2,1)S(1)}, bf16[112,512]{1,0:T(8,128)(2,1)S(1)}, u32[]{:S(2)}, u32[]{:S(2)}) collective-permute-start(bf16[112,512]{1,0:T(8,128)(2,1)S(1)} %get-tuple-element.33), channel_id=1, source_target_pairs={{0,2},{1,3},{2,0},{3,1},{4,6},{5,7},{6,4},{7,5},{8,10},{9,11},{10,... | collective-permute-start | bytes 344072 | tf_op jit(solution)/shard_map/ppermute | solution.py:39
  65.9 8.8 %collective-permute-start.4 = (bf16[16,64,384]{2,1,0:T(8,128)(2,1)S(1)}, bf16[16,64,384]{2,1,0:T(8,128)(2,1)S(1)}, u32[]{:S(2)}, u32[]{:S(2)}) collective-permute-start(bf16[16,64,384]{2,1,0:T(8,128)(2,1)S(1)} %all-to-all-done.2.near.refs_2_.refs_1_), channel_id=1, source_target_pairs={{0,1},{1,0},{2,3},{3,2},{4,5},{5,4},{6,7},{7,6},{8,9},{9,8},{10,11... | collective-permute-start | bytes 2359304 | tf_op jit(solution)/shard_map/ppermute | solution.py:39
  69.4 29.0 %collective-permute-start.3 = (bf16[112,2048]{1,0:T(8,128)(2,1)S(1)}, bf16[112,2048]{1,0:T(8,128)(2,1)S(1)}, u32[]{:S(2)}, u32[]{:S(2)}) collective-permute-start(bf16[112,2048]{1,0:T(8,128)(2,1)S(1)} %get-tuple-element.38), channel_id=1, source_target_pairs={{0,3},{1,2},{2,1},{3,0},{4,7},{5,6},{6,5},{7,4},{8,11},{9,10},{10,... | collective-permute-start | bytes 1376264 | tf_op jit(solution)/shard_map/ppermute | solution.py:39
  70.8 34.2 %collective-permute-start.5 = (bf16[112,1024]{1,0:T(8,128)(2,1)S(1)}, bf16[112,1024]{1,0:T(8,128)(2,1)S(1)}, u32[]{:S(2)}, u32[]{:S(2)}) collective-permute-start(bf16[112,1024]{1,0:T(8,128)(2,1)S(1)} %constant_dynamic-slice_fusion), channel_id=1, source_target_pairs={{0,2},{1,3},{2,0},{3,1},{4,6},{5,7},{6,4},{7,5},{8,10},{9,11},{10,... | collective-permute-start | bytes 688136 | tf_op jit(solution)/shard_map/ppermute | solution.py:39
  98.4 0.7 copy-start.2
  103.6 9.1 %copy-start = (f32[37,4096]{1,0:T(8,128)S(1)}, f32[37,4096]{1,0:T(8,128)}, u32[]{:S(2)}) copy-start(f32[37,4096]{1,0:T(8,128)} %residual.3) | copy-start | bytes 1818628
  103.6 9.1 %copy-start.1 = (f32[37,4096]{1,0:T(8,128)S(1)}, f32[37,4096]{1,0:T(8,128)}, u32[]{:S(2)}) copy-start(f32[37,4096]{1,0:T(8,128)} %coefficients.1) | copy-start | bytes 1818628
  109.8 2.4 %collective-permute-start.7 = (f32[2,40,1024]{2,1,0:T(8,128)S(1)}, f32[2,40,1024]{2,1,0:T(8,128)S(1)}, u32[]{:S(2)}, u32[]{:S(2)}) collective-permute-start(f32[2,40,1024]{2,1,0:T(8,128)S(1)} %get-tuple-element.51), channel_id=1, source_target_pairs={{0,1},{1,0},{2,3},{3,2},{4,5},{5,4},{6,7},{7,6},{8,9},{9,8},{10,11... | collective-permute-start | bytes 983048 | tf_op jit(solution)/shard_map/ppermute | solution.py:39
  111.0 1.7 %collective-permute-start.6 = (f32[2,40,1024]{2,1,0:T(8,128)S(1)}, f32[2,40,1024]{2,1,0:T(8,128)S(1)}, u32[]{:S(2)}, u32[]{:S(2)}) collective-permute-start(f32[2,40,1024]{2,1,0:T(8,128)S(1)} %get-tuple-element.50), channel_id=1, source_target_pairs={{0,1},{1,0},{2,3},{3,2},{4,5},{5,4},{6,7},{7,6},{8,9},{9,8},{10,11... | collective-permute-start | bytes 983048 | tf_op jit(solution)/shard_map/ppermute | solution.py:39
